TPU v7x, 32 devices: a whole 2x2x4 slice. The times are simulated.
32 devices in a mesh: walk: 8 (over z, x), pt: 4 (over y, core).
Axes of the slice: x: 2, y: 2, z: 4, core: 2. Of those that a mesh axis runs over, the one named last changes fastest.
Arguments:
- bra_orbitals: bfloat16 [8, 1536, 160], P('walk'), may hold values from -6 to 6
- ket_orbitals: bfloat16 [8, 1536, 160], P('walk'), may hold values from -6 to 6
- collocation: bfloat16 [12288, 1536], P('pt'), may hold values from -0.15625 to 0.15625
- kernel: bfloat16 [12288, 12288], P('pt', 'walk'), as said below
- walker_weight: float32 [8], P('walk'), may hold values from 0.3 to 3
- walker_group: int32 [8], P('walk'), may hold values from 0 to 19
- group_occupied: int32 [20], replicated, may hold values from 80 to 160, as said below
Outputs:
- gradient: float32 [12288, 1536], P('pt', 'walk')
Inputs may be any that keep to these rules, and one draw needn't show every extreme that they name: kernel is symmetric. `group_occupied`: some group has exactly 160 occupied orbitals.
All inputs are finite; a program needn't handle non-finite values.
Results may differ from a plain program's by a relative error of at most 0.0064.
Values may be sent and summed in bfloat16 or wider, within the bound.
No kernel may reach another device: no remote copies, remote signals or barrier semaphores. Data moves between devices by JAX's collectives and lax.ppermute only.
A program may use at most 192 MiB of HBM per device.

v0:
```python
import functools

import jax
import jax.numpy as jnp
from jax import lax
from jax.experimental import pallas as pl
from jax.experimental.pallas import tpu as pltpu
from jax.sharding import PartitionSpec as P

F32 = jnp.float32
BF16 = jnp.bfloat16
BOTH = ("walk", "pt")
NT = (((1,), (1,)), ((), ()))
TN = (((0,), (0,)), ((), ()))
VMEM_LIMIT = 56 * 1024 * 1024


def tile_of(size, limit):
    return next(t for t in range(min(size, limit), 0, -128) if size % t == 0)


def dot(a, b, dims=(((1,), (0,)), ((), ()))):
    return lax.dot_general(a, b, dims, preferred_element_type=F32)


def cost(flops, nbytes):
    return pl.CostEstimate(flops=flops, bytes_accessed=nbytes, transcendentals=0)


def turn_kernel(in_ref, out_ref):
    out_ref[...] = in_ref[...].T


def turned(block):
    rows, cols = block.shape
    tr, tc = tile_of(rows, 512), tile_of(cols, 512)
    return pl.pallas_call(
        turn_kernel,
        out_shape=jax.ShapeDtypeStruct((cols, rows), block.dtype),
        grid=(cols // tc, rows // tr),
        in_specs=[pl.BlockSpec((tr, tc), lambda c, r: (r, c))],
        out_specs=pl.BlockSpec((tc, tr), lambda c, r: (c, r)),
        compiler_params=pltpu.CompilerParams(vmem_limit_bytes=VMEM_LIMIT),
        cost_estimate=cost(0, 10 * rows * cols),
    )(block)


def pack_kernel(group_ref, occupied_ref, side_ref, weight_ref, bra_ref, ket_ref, own_ref, half_ref):
    occ = bra_ref.shape[0]
    used = occupied_ref[group_ref[0]]
    kept = lax.broadcasted_iota(jnp.int32, bra_ref.shape, 0) < used
    bra_t = jnp.where(kept, bra_ref[...].astype(F32), 0.0).astype(BF16)
    ket_t = jnp.where(kept, ket_ref[...].astype(F32), 0.0).astype(BF16)
    own_ref[:occ, :] = bra_t
    own_ref[occ:, :] = ket_t

    @pl.when(side_ref[0] == 0)
    def _():
        half_ref[:occ, :] = bra_t

    @pl.when(side_ref[0] != 0)
    def _():
        half_ref[:occ, :] = ket_t

    shape = (half_ref.shape[0] - occ, half_ref.shape[1])
    row = lax.broadcasted_iota(jnp.int32, shape, 0)
    rest, rows = jnp.full(shape, weight_ref[0], F32), jnp.zeros(shape, F32)
    for part in range(3):
        near = rest.astype(BF16).astype(F32)
        rows = jnp.where(row == part, near, rows)
        rest = rest - near
    half_ref[occ:, :] = rows.astype(BF16)


def packed(bra, ket, group, occupied, side, weight):
    occ, size_m = bra.shape
    smem = pl.BlockSpec(memory_space=pltpu.SMEM)
    return pl.pallas_call(
        pack_kernel,
        out_shape=[
            jax.ShapeDtypeStruct((2 * occ, size_m), BF16),
            jax.ShapeDtypeStruct((occ + 16, size_m), BF16),
        ],
        in_specs=[smem] * 4 + [pl.BlockSpec(memory_space=pltpu.VMEM)] * 2,
        compiler_params=pltpu.CompilerParams(vmem_limit_bytes=VMEM_LIMIT),
        cost_estimate=cost(0, 12 * size_m * occ),
    )(group, occupied, side, weight, bra, ket)


def columns_kernel(count, rows_each, waits, *refs):
    items, col_ref, refs = refs[:count], refs[count], refs[count + 1 + waits :]
    out_ref, stack = refs[0], refs[-1]

    @pl.when(pl.program_id(0) == 0)
    def _():
        at = 0
        for ref, rows in zip(items, rows_each):
            stack[at : at + rows, :] = ref[:rows, :]
            at += rows
        if len(refs) > 2:
            refs[1][...] = stack[...]

    out_ref[...] = dot(stack[...], col_ref[...], NT).astype(BF16)


def project(items, rows_each, col, keep_stack, after=()):
    count, size_m, size, total = len(items), col.shape[1], col.shape[0], sum(rows_each)
    tile = tile_of(size, 512)
    return pl.pallas_call(
        functools.partial(columns_kernel, count, tuple(rows_each), len(after)),
        out_shape=[
            jax.ShapeDtypeStruct((total, size), BF16),
            jax.ShapeDtypeStruct((total, size_m), BF16),
        ][: 1 + keep_stack],
        grid=(size // tile,),
        in_specs=[pl.BlockSpec(x.shape, lambda b: (0, 0), pipeline_mode=pl.Buffered(1)) for x in items]
        + [pl.BlockSpec((tile, size_m), lambda b: (b, 0))]
        + [pl.BlockSpec(memory_space=pl.ANY)] * len(after),
        out_specs=[
            pl.BlockSpec((total, tile), lambda b: (0, b)),
            pl.BlockSpec((total, size_m), lambda b: (0, 0), pipeline_mode=pl.Buffered(1)),
        ][: 1 + keep_stack],
        scratch_shapes=[pltpu.VMEM((total, size_m), BF16)],
        compiler_params=pltpu.CompilerParams(vmem_limit_bytes=VMEM_LIMIT),
        cost_estimate=cost(2 * total * size_m * size + 2 * 2 * 640 * size_m * size, 2 * size_m * size),
    )(*items, col, *after)


def pair_kernel(parts, groups, sub, waits, share_ref, *refs):
    kts, refs = refs[:parts], refs[parts:]
    lrps, refs = refs[: parts * groups], refs[parts * groups :]
    lrqs, refs = refs[:groups], refs[groups + waits :]
    out_ref, sides_a, totals = refs
    item, step = pl.program_id(0), pl.program_id(1)
    occ = lrps[0].shape[0] // 2
    tile = kts[0].shape[1]

    @pl.when(step == 0)
    def _():
        totals[...] = jnp.zeros_like(totals)
        for g in range(groups):
            for side in (0, 1):
                sides_a[2 * g + side] = lrqs[g][side * occ : (side + 1) * occ, :].T

    for g in range(groups):
        sum_l, sum_r = totals[2 * g], totals[2 * g + 1]
        left_a, right_a = sides_a[2 * g], sides_a[2 * g + 1]
        for h in range(parts):
            for at in range(0, tile, sub):
                left_t = lrps[g * parts + h][:occ, at : at + sub]
                right_t = lrps[g * parts + h][occ:, at : at + sub]
                kern = kts[h][:, at : at + sub]
                had_t = kern * dot(right_a, left_t).astype(BF16)
                had = kern * dot(left_a, right_t).astype(BF16)
                sum_l += dot(had_t, right_t, NT)
                sum_r += dot(had, left_t, NT)
        totals[2 * g], totals[2 * g + 1] = sum_l, sum_r

    @pl.when(step == pl.num_programs(1) - 1)
    def _():
        for g in range(groups):
            scale = 2.0 * share_ref[g * pl.num_programs(0) + item]
            for side in (0, 1):
                out_ref[g, 0, side * occ : (side + 1) * occ, :] = (totals[2 * g + side] * scale).astype(BF16).T


def pair_gradients(share, kts, row_at, lrps, lrqs, after=()):
    parts, groups, count = len(kts), len(lrqs), share.shape[0] // len(lrqs)
    size_b = kts[0].shape[1]
    width, chunk = lrqs[0].shape[0] // count, lrqs[0].shape[1]
    occ = width // 2
    tile = tile_of(size_b, 1024 // groups)
    sub = tile_of(tile, 512)
    at = row_at // chunk
    return pl.pallas_call(
        functools.partial(pair_kernel, parts, groups, sub, len(after)),
        out_shape=jax.ShapeDtypeStruct((groups, count, width, chunk), BF16),
        grid_spec=pltpu.PrefetchScalarGridSpec(
            num_scalar_prefetch=1,
            grid=(count, size_b // tile),
            in_specs=[pl.BlockSpec((chunk, tile), lambda w, b, s: (at, b))] * parts
            + [pl.BlockSpec((width, tile), lambda w, b, s: (w, b))] * (parts * groups)
            + [pl.BlockSpec((width, chunk), lambda w, b, s: (w, 0))] * groups
            + [pl.BlockSpec(memory_space=pl.ANY)] * len(after),
            out_specs=pl.BlockSpec((groups, 1, width, chunk), lambda w, b, s: (0, w, 0, 0)),
            scratch_shapes=[
                pltpu.VMEM((2 * groups, chunk, occ), BF16),
                pltpu.VMEM((2 * groups, chunk, occ), F32),
            ],
        ),
        compiler_params=pltpu.CompilerParams(vmem_limit_bytes=VMEM_LIMIT),
        cost_estimate=cost(
            2 * 4 * groups * count * 256 * chunk * size_b * parts, 2 * groups * count * chunk * size_b * parts
        ),
    )(share, *kts, *[x for group in lrps for x in group], *lrqs, *after)


def send(x, axes, pairs):
    return lax.ppermute(x, axes, pairs)


def masked_orbitals(bra_orbitals, ket_orbitals, walker_group, group_occupied):
    group_count, occ = group_occupied.shape[0], bra_orbitals.shape[2]
    matches = walker_group[:, None] == jnp.arange(group_count, dtype=jnp.int32)[None, :]
    occupied = jnp.sum(jnp.where(matches, group_occupied[None, :], 0), axis=1)
    masks = (jnp.arange(occ, dtype=jnp.int32)[None, :] < occupied[:, None]).astype(BF16)
    bra_t = jnp.swapaxes(bra_orbitals * masks[:, None, :], 1, 2)
    ket_t = jnp.swapaxes(ket_orbitals * masks[:, None, :], 1, 2)
    return jnp.concatenate([bra_t, ket_t], axis=1)


def on_device_8x4(bra, ket, collocation, kernel, walker_weight, walker_group, group_occupied):
    nw, npt = 8, 4
    size_b, size_a = kernel.shape
    occ, size_m = bra.shape
    width = 2 * occ
    me_w, me_p = lax.axis_index("walk"), lax.axis_index("pt")
    z, x, y, core = me_w // 2, me_w % 2, me_p // 2, me_p % 2

    def put(j, i):
        return j * npt + i

    def across(part):
        return send(part, "walk", [(j, j ^ 1) for j in range(nw)])

    def along(part, r):
        return send(part, "walk", [(j, (j - 2 * r) % nw) for j in range(nw)])

    def other(part):
        return send(part, "pt", [(i, i ^ 1) for i in range(npt)])

    def columns_q(begin, chunk):
        rows = lax.dynamic_slice_in_dim(collocation, x * size_a + begin, chunk, 0)
        far = send(rows, BOTH, [(put(j, j // 2), put(j, j // 2 ^ 2)) for j in range(nw)])
        near = jnp.where(me_p == z, rows, far)
        pairs = [(put(j, j // 2 ^ s), put(j, j // 2 ^ s ^ 1)) for j in range(nw) for s in (0, 2)]
        return jnp.where(core == z % 2, near, send(near, BOTH, pairs))

    def weight_of(part):
        return jnp.sum(part[occ : occ + 3, 0].astype(F32))

    chunks = [(0, 2 * size_a // 3), (2 * size_a // 3, size_a // 3)]
    own, half = packed(bra, ket, walker_group, group_occupied, core.reshape(1), walker_weight)
    cols_q = [columns_q(*chunk) for chunk in chunks]
    z1, z3, x0 = along(half, 1), along(half, 3), across(half)
    z2 = along(half, 2)
    x1, x3, x2 = across(z1), across(z3), across(z2)
    groups = [[own, x0, other(x0)], [h for part in (z1, z3, x1, x3, z2, x2) for h in (part, other(part))]]
    rows_each = [[width, occ, occ], [occ] * 12]
    weights = [
        jnp.stack([walker_weight[0], weight_of(x0)]),
        jnp.stack([weight_of(part) for part in (z1, z3, x1, x3, z2, x2)]),
    ]
    total = jnp.sum(weights[0]) + jnp.sum(weights[1])

    kts = [turned(kernel)]

    def gradients(g, c, lrp, after=()):
        (lrq,) = project(groups[g], rows_each[g], cols_q[c], False)
        return pair_gradients(weights[g], kts, chunks[c][0], [[lrp]], [lrq], after).reshape(sum(rows_each[g]), -1)

    lrp_0, stack_0 = project(groups[0], rows_each[0], collocation, True)
    first_grads = gradients(0, 0, lrp_0)
    lrp_1, stack_1 = project(groups[1], rows_each[1], collocation, True, (first_grads,))

    half_m, quarter, eighth = size_m // 2, size_m // 4, size_m // 8
    landed, after = [], ()
    for c in range(len(chunks)):
        grads_0 = first_grads if c == 0 else gradients(0, c, lrp_0, after)
        grads_1 = gradients(1, c, lrp_1, after)
        part = dot(stack_0, grads_0, TN) + dot(stack_1, grads_1, TN)
        give = lax.dynamic_slice_in_dim(part, (1 - core) * half_m, half_m, 0).astype(BF16)
        keep = lax.dynamic_slice_in_dim(part, core * half_m, half_m, 0)
        part = keep + other(give).astype(F32)
        give = lax.dynamic_slice_in_dim(part, (1 - y) * quarter, quarter, 0).astype(BF16)
        keep = lax.dynamic_slice_in_dim(part, y * quarter, quarter, 0)
        after = (give,)
        got = send(give, "pt", [(i, i ^ 2) for i in range(npt)])
        part = (keep + got.astype(F32)).astype(BF16)
        came = []
        for t in (0, 1):
            piece = lax.dynamic_slice_in_dim(part, (x ^ t) * eighth, eighth, 0)
            pairs = []
            for j in range(nw):
                for i in range(npt):
                    quarter_of = 2 * (i % 2) + i // 2
                    pairs.append((put(j, i), put(2 * quarter_of + (j % 2 ^ t), j // 2)))
            came.append(send(piece, BOTH, pairs))
        landed.append(came)
    first = jnp.concatenate([jnp.where(x == 0, came[0], came[1]) for came in landed], axis=1)
    second = jnp.concatenate([jnp.where(x == 0, came[1], came[0]) for came in landed], axis=1)
    return (jnp.concatenate([first, second], axis=1).astype(F32) / total).T


def on_device_any(nw, own, collocation, kernel, walker_weight):
    size_b, size_a = kernel.shape
    local, size_m = walker_weight.shape[0], collocation.shape[1]
    me_w, me_p = lax.axis_index("walk"), lax.axis_index("pt")
    weights = lax.all_gather(walker_weight, "walk", axis=0, tiled=True)
    orbitals = lax.all_gather(own, "walk", axis=0, tiled=True)
    all_rows = lax.all_gather(collocation, "pt", axis=0, tiled=True)
    col_q = lax.dynamic_slice_in_dim(all_rows, me_w * size_a, size_a, 0)
    lrp = dot(orbitals, collocation, NT).astype(BF16)
    lrq = dot(orbitals, col_q, NT).astype(BF16)
    grads = pair_gradients(weights / jnp.sum(weights), [turned(kernel)], 0, [[lrp]], [lrq])
    part = lax.psum(dot(orbitals, grads.reshape(orbitals.shape[0], size_a), TN), "pt")
    part = jnp.where((me_w * size_a) // size_b == me_p, part, 0.0)
    wide = lax.dynamic_update_slice_in_dim(jnp.zeros((size_m, size_b), F32), part, (me_w * size_a) % size_b, 1)
    return lax.psum_scatter(wide, "walk", scatter_dimension=0, tiled=True).T


def on_device(
    nw, npt, bra_orbitals, ket_orbitals, collocation, kernel, walker_weight, walker_group, group_occupied
):
    if (nw, npt, walker_weight.shape[0]) == (8, 4, 1) and kernel.shape[0] == 2 * kernel.shape[1]:
        bra, ket = bra_orbitals[0].T, ket_orbitals[0].T
        return on_device_8x4(bra, ket, collocation, kernel, walker_weight, walker_group, group_occupied)
    own = masked_orbitals(bra_orbitals, ket_orbitals, walker_group, group_occupied)
    return on_device_any(nw, own.reshape(-1, own.shape[2]), collocation, kernel, walker_weight)


def solution(mesh):
    in_specs = (
        P("walk", None, None),
        P("walk", None, None),
        P("pt", None),
        P("pt", "walk"),
        P("walk"),
        P("walk"),
        P(),
    )
    out_specs = P("pt", "walk")
    body = functools.partial(on_device, mesh.shape["walk"], mesh.shape["pt"])
    return jax.shard_map(body, mesh=mesh, in_specs=in_specs, out_specs=out_specs, check_vma=False)
```

profile of v0, /device:TPU:1, one launch (start us, length us, event | category | flops | bytes accessed | tf_op | source)
XLA Modules:
  0.0 381.1 jit_solution(15882431267053674758)
XLA Ops:
  0.0 2.1 constant_dynamic-slice_fusion.5
  2.1 2.3 collective-permute-start.2
  5.7 2.5 shard_map.73
  8.2 2.0 collective-permute-start
  10.3 3.8 collective-permute-start.6
  14.0 2.1 collective-permute-start.4
  16.1 14.6 %shard_map.75.refs_0_ = bf16[1536,3072]{1,0:T(8,128)(2,1)} custom-call(bf16[3072,1536]{1,0:T(8,128)(2,1)} %in_ref.1), custom_call_target="tpu_custom_call" | custom-call | bytes 47185920 | tf_op jit(solution)/shard_map/pallas_call | solution.py:37
  30.8 2.7 constant_dynamic-slice_fusion.2
  33.5 1.7 collective-permute-start.1
  35.4 14.5 %collective-permute-done.12.refs_8_ = bf16[176,1536]{1,0:T(8,128)(2,1)} collective-permute-done((bf16[176,1536]{1,0:T(8,128)(2,1)}, bf16[176,1536]{1,0:T(8,128)(2,1)}, u32[]{:S(2)}, u32[]{:S(2)}) %collective-permute-start.12) | collective-permute-done | bytes 540704 | tf_op jit(solution)/shard_map/ppermute | solution.py:199
  49.9 1.5 collective-permute-start.8
  51.3 3.7 broadcast_select_fusion
  55.0 1.3 collective-permute-start.3
  56.3 1.3 convert_reduce_fusion.6
  57.7 1.4 convert_reduce_fusion.1
  59.0 1.2 convert_reduce_fusion.5
  60.2 1.2 pad_maximum_fusion.share_ref
  61.4 1.3 convert_reduce_fusion.4
  62.8 1.9 collective-permute-start.20
  65.2 6.8 %collective-permute-start.13 = (bf16[176,1536]{1,0:T(8,128)(2,1)}, bf16[176,1536]{1,0:T(8,128)(2,1)}, u32[]{:S(2)}, u32[]{:S(2)}) collective-permute-start(bf16[176,1536]{1,0:T(8,128)(2,1)} %collective-permute-done.12.refs_8_), channel_id=1, source_target_pairs={{0,1},{1,0},{2,3},{3,2},{4,5},{5,4},{6,7},{7,6},{8,9},{9,8},{10,11... | collective-permute-start | bytes 1622024 | tf_op jit(solution)/shard_map/ppermute | solution.py:199
  72.7 2.3 collective-permute-done.8.refs_4_
  75.0 1.3 collective-permute-start.5
  77.0 4.4 %stack.35.share_ref = f32[6]{0:T(128)} concatenate(f32[1]{0:T(128)} %bitcast.7, f32[1]{0:T(128)} %bitcast.8, f32[1]{0:T(128)} %bitcast.9, f32[1]{0:T(128)} %bitcast.10, f32[1]{0:T(128)} %bitcast.11, f32[1]{0:T(128)} %bitcast.12), dimensions={0} | concatenate | bytes 48 | tf_op jit(solution)/shard_map/stack | solution.py:252
  82.2 11.6 %shard_map.74 = (bf16[640,3072]{1,0:T(8,128)(2,1)}, bf16[640,1536]{1,0:T(8,128)(2,1)}) custom-call(bf16[320,1536]{1,0:T(8,128)(2,1)} %get-tuple-element.11.refs_0_, bf16[176,1536]{1,0:T(8,128)(2,1)} %collective-permute-done.refs_1_, bf16[176,1536]{1,0:T(8,128)(2,1)} %collective-permute-done.1.refs_2_, bf16[3072,1536]{1,0:T(8,128)(2,1)} %refs_12_.1), custom_call_target="tpu_custom_call" | custom-call | flops 18119393280 | bytes 9437184 | tf_op jit(solution)/shard_map/pallas_call | solution.py:109
  93.9 3.5 broadcast_select_fusion.2
  97.4 3.9 %broadcast_select_fusion.1.refs_3_.refs_12_ = bf16[1024,1536]{1,0:T(8,128)(2,1)} fusion(bf16[1024,1536]{1,0:T(8,128)(2,1)S(1)} %broadcast_select_fusion, bf16[1024,1536]{1,0:T(8,128)(2,1)} %collective-permute-done.3, pred[]{:T(512)S(6)} %eq.20), kind=kLoop, calls=%fused_computation.5 | loop fusion | flops 1572864 | bytes 9437185 | tf_op jit(solution)/shard_map/jit(_where)/select_n | solution.py:237
  101.3 5.5 %shard_map.76.refs_2_ = bf16[640,1024]{1,0:T(8,128)(2,1)} custom-call(bf16[320,1536]{1,0:T(8,128)(2,1)} %get-tuple-element.11.refs_0_, bf16[176,1536]{1,0:T(8,128)(2,1)} %collective-permute-done.refs_1_, bf16[176,1536]{1,0:T(8,128)(2,1)} %collective-permute-done.1.refs_2_, bf16[1024,1536]{1,0:T(8,128)(2,1)} %broadcast_select_fusion.1.refs_3_.refs_12_), custom_call_target="tpu_custom_call" | custom-call | flops 6039797760 | bytes 3145728 | tf_op jit(solution)/shard_map/pallas_call | solution.py:109
  106.9 19.4 %shard_map.77 = bf16[1,2,320,1024]{3,2,1,0:T(8,128)(2,1)} custom-call(f32[2]{0:T(128)} %pad_maximum_fusion.share_ref, bf16[1536,3072]{1,0:T(8,128)(2,1)} %shard_map.75.refs_0_, bf16[640,3072]{1,0:T(8,128)(2,1)} %get-tuple-element.14.refs_1_, bf16[640,1024]{1,0:T(8,128)(2,1)} %shard_map.76.refs_2_), custom_call_target="tpu_custom_call" | custom-call | flops 12884901888 | bytes 12582912 | tf_op jit(solution)/shard_map/pallas_call | solution.py:175
  126.3 6.0 %fusion = f32[1536,1024]{1,0:T(8,128)} fusion(bf16[640,1536]{1,0:T(8,128)(2,1)S(1)} %copy-done.14, bf16[640,1024]{1,0:T(8,128)(2,1)} %bitcast.34), kind=kOutput, calls=%fused_computation.33 | convolution fusion | flops 2013265920 | bytes 9568256 | tf_op jit(solution)/shard_map/dot_general | solution.py:23
  132.3 1.3 collective-permute-start.21
  134.8 0.8 copy-done.12
  135.6 25.3 %shard_map.78 = (bf16[1920,3072]{1,0:T(8,128)(2,1)}, bf16[1920,1536]{1,0:T(8,128)(2,1)}) custom-call(bf16[176,1536]{1,0:T(8,128)(2,1)} %collective-permute-done.4.refs_0_, bf16[176,1536]{1,0:T(8,128)(2,1)} %collective-permute-done.5.refs_1_, bf16[176,1536]{1,0:T(8,128)(2,1)} %collective-permute-done.6.refs_2_, bf16[176,1536]{1,0:T(8,128)(2,1)} %copy-done.9, ...), custom_call_target="tpu_custom_call" | custom-call | flops 30198988800 | bytes 9437184 | tf_op jit(solution)/shard_map/pallas_call | solution.py:109
  160.9 11.7 %shard_map.79.refs_2_ = bf16[1920,1024]{1,0:T(8,128)(2,1)} custom-call(bf16[176,1536]{1,0:T(8,128)(2,1)} %collective-permute-done.4.refs_0_, bf16[176,1536]{1,0:T(8,128)(2,1)} %collective-permute-done.5.refs_1_, bf16[176,1536]{1,0:T(8,128)(2,1)} %collective-permute-done.6.refs_2_, bf16[176,1536]{1,0:T(8,128)(2,1)} %copy-done.9, bf16[176,1536]{1,0:T(8,128)(2,1)} %copy-done.7, ...), custom_call_target="tpu_custom_call" | custom-call | flops 10066329600 | bytes 3145728 | tf_op jit(solution)/shard_map/pallas_call | solution.py:109
  172.6 50.8 %shard_map.80 = bf16[1,6,320,1024]{3,2,1,0:T(8,128)(2,1)} custom-call(f32[6]{0:T(128)} %stack.35.share_ref, bf16[1536,3072]{1,0:T(8,128)(2,1)} %shard_map.75.refs_0_, bf16[1920,3072]{1,0:T(8,128)(2,1)} %get-tuple-element.16.refs_1_, bf16[1920,1024]{1,0:T(8,128)(2,1)} %shard_map.79.refs_2_), custom_call_target="tpu_custom_call" | custom-call | flops 38654705664 | bytes 37748736 | tf_op jit(solution)/shard_map/pallas_call | solution.py:175
  223.3 11.5 %convolution_add_fusion = f32[1536,1024]{1,0:T(8,128)S(1)} fusion(f32[1536,1024]{1,0:T(8,128)} %fusion, bf16[1920,1536]{1,0:T(8,128)(2,1)} %get-tuple-element.15, bf16[1920,1024]{1,0:T(8,128)(2,1)} %bitcast.32), kind=kOutput, calls=%fused_computation | convolution fusion | flops 6041370624 | bytes 22413312 | tf_op jit(solution)/shard_map/dot_general | solution.py:23
  234.8 2.7 copy-done.1
  237.7 1.3 collective-permute-start.16
  239.0 1.3 broadcast_select_fusion.3.refs_3_.refs_12_
  240.4 4.1 %shard_map.81.refs_2_ = bf16[640,512]{1,0:T(8,128)(2,1)} custom-call(bf16[320,1536]{1,0:T(8,128)(2,1)} %get-tuple-element.11.refs_0_, bf16[176,1536]{1,0:T(8,128)(2,1)} %collective-permute-done.refs_1_, bf16[176,1536]{1,0:T(8,128)(2,1)} %collective-permute-done.1.refs_2_, bf16[512,1536]{1,0:T(8,128)(2,1)} %broadcast_select_fusion.3.refs_3_.refs_12_), custom_call_target="tpu_custom_call" | custom-call | flops 3019898880 | bytes 1572864 | tf_op jit(solution)/shard_map/pallas_call | solution.py:109
  244.5 7.9 %shard_map.83.refs_2_ = bf16[1920,512]{1,0:T(8,128)(2,1)} custom-call(bf16[176,1536]{1,0:T(8,128)(2,1)} %collective-permute-done.4.refs_0_, bf16[176,1536]{1,0:T(8,128)(2,1)} %collective-permute-done.5.refs_1_, bf16[176,1536]{1,0:T(8,128)(2,1)} %collective-permute-done.6.refs_2_, bf16[176,1536]{1,0:T(8,128)(2,1)} %copy-done.9, bf16[176,1536]{1,0:T(8,128)(2,1)} %copy-done.7, ...), custom_call_target="tpu_custom_call" | custom-call | flops 5033164800 | bytes 1572864 | tf_op jit(solution)/shard_map/pallas_call | solution.py:109
  252.4 2.8 convert_add_fusion
  255.2 1.0 dynamic-slice_convert_fusion.2.refs_3_
  256.3 29.1 %shard_map.84 = bf16[1,6,320,512]{3,2,1,0:T(8,128)(2,1)} custom-call(f32[6]{0:T(128)} %stack.35.share_ref, bf16[1536,3072]{1,0:T(8,128)(2,1)} %shard_map.75.refs_0_, bf16[1920,3072]{1,0:T(8,128)(2,1)} %get-tuple-element.16.refs_1_, bf16[1920,512]{1,0:T(8,128)(2,1)} %shard_map.83.refs_2_, bf16[384,1024]{1,0:T(8,128)(2,1)} %dynamic-slice_convert_fusion.2.refs_3_), custom_call_target="tpu_custom_call" | custom-call | flops 19327352832 | bytes 18874368 | tf_op jit(solution)/shard_map/pallas_call | solution.py:175
  285.4 11.7 %shard_map.82 = bf16[1,2,320,512]{3,2,1,0:T(8,128)(2,1)} custom-call(f32[2]{0:T(128)} %pad_maximum_fusion.share_ref, bf16[1536,3072]{1,0:T(8,128)(2,1)} %shard_map.75.refs_0_, bf16[640,3072]{1,0:T(8,128)(2,1)} %get-tuple-element.14.refs_1_, bf16[640,512]{1,0:T(8,128)(2,1)} %shard_map.81.refs_2_, bf16[384,1024]{1,0:T(8,128)(2,1)} %dynamic-slice_convert_fusion.2.refs_3_), custom_call_target="tpu_custom_call" | custom-call | flops 6442450944 | bytes 6291456 | tf_op jit(solution)/shard_map/pallas_call | solution.py:175
  297.1 2.7 fusion.1
  299.8 5.5 %convolution_add_fusion.1 = f32[1536,512]{1,0:T(8,128)S(1)} fusion(f32[1536,512]{1,0:T(8,128)S(1)} %fusion.1, bf16[1920,1536]{1,0:T(8,128)(2,1)} %get-tuple-element.15, bf16[1920,512]{1,0:T(8,128)(2,1)S(1)} %bitcast.33), kind=kOutput, calls=%fused_computation.1 | convolution fusion | flops 3020685312 | bytes 14155776 | tf_op jit(solution)/shard_map/dot_general | solution.py:23
  305.3 1.6 copy-done.2
  306.9 1.0 dynamic-slice_convert_fusion.1
  307.9 1.5 collective-permute-start.22
  309.4 2.9 collective-permute-start.17
  312.3 1.9 convert_add_fusion.1
  314.2 0.9 dynamic-slice_convert_fusion.3
  315.1 2.2 collective-permute-start.23
  317.3 13.2 %collective-permute-done.17 = bf16[384,1024]{1,0:T(8,128)(2,1)} collective-permute-done((bf16[384,1024]{1,0:T(8,128)(2,1)}, bf16[384,1024]{1,0:T(8,128)(2,1)}, u32[]{:S(2)}, u32[]{:S(2)}) %collective-permute-start.17) | collective-permute-done | bytes 786464 | tf_op jit(solution)/shard_map/ppermute | solution.py:199
  330.5 1.4 add_convert_fusion
  332.0 7.2 %collective-permute-start.18 = (bf16[192,1024]{1,0:T(8,128)(2,1)S(1)}, bf16[192,1024]{1,0:T(8,128)(2,1)S(1)}, u32[]{:S(2)}, u32[]{:S(2)}) collective-permute-start(bf16[192,1024]{1,0:T(8,128)(2,1)S(1)} %get-tuple-element.19), channel_id=1, source_target_pairs={{0,0},{1,16},{2,8},{3,24},{4,4},{5,20},{6,12},{7,28},{8,1},{9,17},... | collective-permute-start | bytes 1179656 | tf_op jit(solution)/shard_map/ppermute | solution.py:199
  343.7 1.3 add_convert_fusion.1
  345.0 11.0 %collective-permute-start.24 = (bf16[192,512]{1,0:T(8,128)(2,1)S(1)}, bf16[192,512]{1,0:T(8,128)(2,1)S(1)}, u32[]{:S(2)}, u32[]{:S(2)}) collective-permute-start(bf16[192,512]{1,0:T(8,128)(2,1)S(1)} %get-tuple-element.23), channel_id=1, source_target_pairs={{0,0},{1,16},{2,8},{3,24},{4,4},{5,20},{6,12},{7,28},{8,1},{9,17},... | collective-permute-start | bytes 589832 | tf_op jit(solution)/shard_map/ppermute | solution.py:199
  356.0 1.0 collective-permute-start.25
  357.0 7.7 %collective-permute-done.18 = bf16[192,1024]{1,0:T(8,128)(2,1)S(1)} collective-permute-done((bf16[192,1024]{1,0:T(8,128)(2,1)S(1)}, bf16[192,1024]{1,0:T(8,128)(2,1)S(1)}, u32[]{:S(2)}, u32[]{:S(2)}) %collective-permute-start.18) | collective-permute-done | bytes 393248 | tf_op jit(solution)/shard_map/ppermute | solution.py:199
  364.7 6.3 %collective-permute-done.19 = bf16[192,1024]{1,0:T(8,128)(2,1)S(1)} collective-permute-done((bf16[192,1024]{1,0:T(8,128)(2,1)S(1)}, bf16[192,1024]{1,0:T(8,128)(2,1)S(1)}, u32[]{:S(2)}, u32[]{:S(2)}) %collective-permute-start.19) | collective-permute-done | bytes 393248 | tf_op jit(solution)/shard_map/ppermute | solution.py:199
  371.0 4.2 %collective-permute-done.24 = bf16[192,512]{1,0:T(8,128)(2,1)S(1)} collective-permute-done((bf16[192,512]{1,0:T(8,128)(2,1)S(1)}, bf16[192,512]{1,0:T(8,128)(2,1)S(1)}, u32[]{:S(2)}, u32[]{:S(2)}) %collective-permute-start.24) | collective-permute-done | bytes 196640 | tf_op jit(solution)/shard_map/ppermute | solution.py:199
  375.2 4.2 %collective-permute-done.25 = bf16[192,512]{1,0:T(8,128)(2,1)S(1)} collective-permute-done((bf16[192,512]{1,0:T(8,128)(2,1)S(1)}, bf16[192,512]{1,0:T(8,128)(2,1)S(1)}, u32[]{:S(2)}, u32[]{:S(2)}) %collective-permute-start.25) | collective-permute-done | bytes 196640 | tf_op jit(solution)/shard_map/ppermute | solution.py:199
  379.4 1.7 divide_bitcast_fusion
  (64 shorter events, 4.8 us)
Async XLA Ops:
  2.1 49.2 %collective-permute-start.2 = (bf16[1024,1536]{1,0:T(8,128)(2,1)S(1)}, bf16[1024,1536]{1,0:T(8,128)(2,1)}, u32[]{:S(2)}, u32[]{:S(2)}) collective-permute-start(bf16[1024,1536]{1,0:T(8,128)(2,1)S(1)} %constant_dynamic-slice_fusion.5), channel_id=1, source_target_pairs={{0,2},{4,6},{9,11},{13,15},{18,16},{22,20},{27,25},{31,29}} | collective-permute-start | bytes 9437192 | tf_op jit(solution)/shard_map/ppermute | solution.py:199
  8.2 25.2 %collective-permute-start = (bf16[176,1536]{1,0:T(8,128)(2,1)}, bf16[176,1536]{1,0:T(8,128)(2,1)}, u32[]{:S(2)}, u32[]{:S(2)}) collective-permute-start(bf16[176,1536]{1,0:T(8,128)(2,1)} %get-tuple-element.12), channel_id=1, source_target_pairs={{0,4},{4,0},{8,12},{12,8},{16,20},{20,16},{24,28},{28,24},{1,5},{5... | collective-permute-start | bytes 1622024 | tf_op jit(solution)/shard_map/ppermute | solution.py:199
  10.3 24.9 %collective-permute-start.6 = (bf16[176,1536]{1,0:T(8,128)(2,1)}, bf16[176,1536]{1,0:T(8,128)(2,1)}, u32[]{:S(2)}, u32[]{:S(2)}) collective-permute-start(bf16[176,1536]{1,0:T(8,128)(2,1)} %get-tuple-element.12), channel_id=1, source_target_pairs={{0,8},{4,12},{8,16},{12,20},{16,24},{20,28},{24,0},{28,4},{1,9},{5... | collective-permute-start | bytes 1622024 | tf_op jit(solution)/shard_map/ppermute | solution.py:199
  14.0 35.8 %collective-permute-start.12 = (bf16[176,1536]{1,0:T(8,128)(2,1)}, bf16[176,1536]{1,0:T(8,128)(2,1)}, u32[]{:S(2)}, u32[]{:S(2)}) collective-permute-start(bf16[176,1536]{1,0:T(8,128)(2,1)} %get-tuple-element.12), channel_id=1, source_target_pairs={{0,16},{4,20},{8,24},{12,28},{16,0},{20,4},{24,8},{28,12},{1,17},{... | collective-permute-start | bytes 1622024 | tf_op jit(solution)/shard_map/ppermute | solution.py:199
  14.0 35.8 %collective-permute-start.4 = (bf16[176,1536]{1,0:T(8,128)(2,1)}, bf16[176,1536]{1,0:T(8,128)(2,1)}, u32[]{:S(2)}, u32[]{:S(2)}) collective-permute-start(bf16[176,1536]{1,0:T(8,128)(2,1)} %get-tuple-element.12), channel_id=1, source_target_pairs={{0,24},{4,28},{8,0},{12,4},{16,8},{20,12},{24,16},{28,20},{1,25},{... | collective-permute-start | bytes 1622024 | tf_op jit(solution)/shard_map/ppermute | solution.py:199
  33.5 47.9 %collective-permute-start.1 = (bf16[176,1536]{1,0:T(8,128)(2,1)}, bf16[176,1536]{1,0:T(8,128)(2,1)}, u32[]{:S(2)}, u32[]{:S(2)}) collective-permute-start(bf16[176,1536]{1,0:T(8,128)(2,1)} %collective-permute-done.refs_1_), channel_id=1, source_target_pairs={{0,1},{1,0},{2,3},{3,2},{4,5},{5,4},{6,7},{7,6},{8,9},{9,8},{10,11... | collective-permute-start | bytes 1622024 | tf_op jit(solution)/shard_map/ppermute | solution.py:199
  35.1 27.6 %collective-permute-start.10 = (bf16[176,1536]{1,0:T(8,128)(2,1)}, bf16[176,1536]{1,0:T(8,128)(2,1)S(1)}, u32[]{:S(2)}, u32[]{:S(2)}) collective-permute-start(bf16[176,1536]{1,0:T(8,128)(2,1)} %collective-permute-done.6.refs_2_), channel_id=1, source_target_pairs={{0,4},{4,0},{8,12},{12,8},{16,20},{20,16},{24,28},{28,24},{1,5},{5... | collective-permute-start | bytes 1622024 | tf_op jit(solution)/shard_map/ppermute | solution.py:199
  49.9 15.4 %collective-permute-start.14 = (bf16[176,1536]{1,0:T(8,128)(2,1)}, bf16[176,1536]{1,0:T(8,128)(2,1)S(1)}, u32[]{:S(2)}, u32[]{:S(2)}) collective-permute-start(bf16[176,1536]{1,0:T(8,128)(2,1)} %collective-permute-done.12.refs_8_), channel_id=1, source_target_pairs={{0,4},{4,0},{8,12},{12,8},{16,20},{20,16},{24,28},{28,24},{1,5},{5... | collective-permute-start | bytes 1622024 | tf_op jit(solution)/shard_map/ppermute | solution.py:199
  49.9 25.2 %collective-permute-start.8 = (bf16[176,1536]{1,0:T(8,128)(2,1)}, bf16[176,1536]{1,0:T(8,128)(2,1)S(1)}, u32[]{:S(2)}, u32[]{:S(2)}) collective-permute-start(bf16[176,1536]{1,0:T(8,128)(2,1)} %collective-permute-done.4.refs_0_), channel_id=1, source_target_pairs={{0,4},{4,0},{8,12},{12,8},{16,20},{20,16},{24,28},{28,24},{1,5},{5... | collective-permute-start | bytes 1622024 | tf_op jit(solution)/shard_map/ppermute | solution.py:199
  55.0 42.4 %collective-permute-start.3 = (bf16[1024,1536]{1,0:T(8,128)(2,1)S(1)}, bf16[1024,1536]{1,0:T(8,128)(2,1)}, u32[]{:S(2)}, u32[]{:S(2)}) collective-permute-start(bf16[1024,1536]{1,0:T(8,128)(2,1)S(1)} %broadcast_select_fusion), channel_id=1, source_target_pairs={{0,1},{2,3},{4,5},{6,7},{9,8},{11,10},{13,12},{15,14},{18,19},{16,... | collective-permute-start | bytes 9437192 | tf_op jit(solution)/shard_map/ppermute | solution.py:199
  62.8 1.9 copy-start.3
  62.8 31.0 %collective-permute-start.20 = (bf16[512,1536]{1,0:T(8,128)(2,1)}, bf16[512,1536]{1,0:T(8,128)(2,1)}, u32[]{:S(2)}, u32[]{:S(2)}) collective-permute-start(bf16[512,1536]{1,0:T(8,128)(2,1)} %constant_dynamic-slice_fusion.2), channel_id=1, source_target_pairs={{0,2},{4,6},{9,11},{13,15},{18,16},{22,20},{27,25},{31,29}} | collective-permute-start | bytes 4718600 | tf_op jit(solution)/shard_map/ppermute | solution.py:199
  65.2 6.8 %copy-start.5 = (bf16[176,1536]{1,0:T(8,128)(2,1)}, bf16[176,1536]{1,0:T(8,128)(2,1)S(1)}, u32[]{:S(2)}) copy-start(bf16[176,1536]{1,0:T(8,128)(2,1)S(1)} %collective-permute-done.14.refs_10_) | copy-start | bytes 1622020
  65.2 41.6 %collective-permute-start.13 = (bf16[176,1536]{1,0:T(8,128)(2,1)}, bf16[176,1536]{1,0:T(8,128)(2,1)}, u32[]{:S(2)}, u32[]{:S(2)}) collective-permute-start(bf16[176,1536]{1,0:T(8,128)(2,1)} %collective-permute-done.12.refs_8_), channel_id=1, source_target_pairs={{0,1},{1,0},{2,3},{3,2},{4,5},{5,4},{6,7},{7,6},{8,9},{9,8},{10,11... | collective-permute-start | bytes 1622024 | tf_op jit(solution)/shard_map/ppermute | solution.py:199
  75.0 1.3 copy-start.7
  75.0 57.3 %collective-permute-start.5 = (bf16[176,1536]{1,0:T(8,128)(2,1)}, bf16[176,1536]{1,0:T(8,128)(2,1)}, u32[]{:S(2)}, u32[]{:S(2)}) collective-permute-start(bf16[176,1536]{1,0:T(8,128)(2,1)} %collective-permute-done.4.refs_0_), channel_id=1, source_target_pairs={{0,1},{1,0},{2,3},{3,2},{4,5},{5,4},{6,7},{7,6},{8,9},{9,8},{10,11... | collective-permute-start | bytes 1622024 | tf_op jit(solution)/shard_map/ppermute | solution.py:199
  81.4 52.2 %collective-permute-start.7 = (bf16[176,1536]{1,0:T(8,128)(2,1)}, bf16[176,1536]{1,0:T(8,128)(2,1)S(1)}, u32[]{:S(2)}, u32[]{:S(2)}) collective-permute-start(bf16[176,1536]{1,0:T(8,128)(2,1)} %collective-permute-done.6.refs_2_), channel_id=1, source_target_pairs={{0,1},{1,0},{2,3},{3,2},{4,5},{5,4},{6,7},{7,6},{8,9},{9,8},{10,11... | collective-permute-start | bytes 1622024 | tf_op jit(solution)/shard_map/ppermute | solution.py:199
  82.1 11.7 %copy-start.4 = (bf16[176,1536]{1,0:T(8,128)(2,1)S(1)}, bf16[176,1536]{1,0:T(8,128)(2,1)}, u32[]{:S(2)}) copy-start(bf16[176,1536]{1,0:T(8,128)(2,1)} %copy-done.3) | copy-start | bytes 1622020
  93.8 3.6 copy-start.6
  93.8 39.8 %collective-permute-start.11 = (bf16[176,1536]{1,0:T(8,128)(2,1)S(1)}, bf16[176,1536]{1,0:T(8,128)(2,1)S(1)}, u32[]{:S(2)}, u32[]{:S(2)}) collective-permute-start(bf16[176,1536]{1,0:T(8,128)(2,1)S(1)} %copy-done.4), channel_id=1, source_target_pairs={{0,1},{1,0},{2,3},{3,2},{4,5},{5,4},{6,7},{7,6},{8,9},{9,8},{10,11... | collective-permute-start | bytes 1622024 | tf_op jit(solution)/shard_map/ppermute | solution.py:199
  97.4 36.2 %collective-permute-start.15 = (bf16[176,1536]{1,0:T(8,128)(2,1)S(1)}, bf16[176,1536]{1,0:T(8,128)(2,1)S(1)}, u32[]{:S(2)}, u32[]{:S(2)}) collective-permute-start(bf16[176,1536]{1,0:T(8,128)(2,1)S(1)} %copy-done.6), channel_id=1, source_target_pairs={{0,1},{1,0},{2,3},{3,2},{4,5},{5,4},{6,7},{7,6},{8,9},{9,8},{10,11... | collective-permute-start | bytes 1622024 | tf_op jit(solution)/shard_map/ppermute | solution.py:199
  101.3 5.5 %copy-start.8 = (bf16[176,1536]{1,0:T(8,128)(2,1)S(1)}, bf16[176,1536]{1,0:T(8,128)(2,1)}, u32[]{:S(2)}) copy-start(bf16[176,1536]{1,0:T(8,128)(2,1)} %copy-done.7) | copy-start | bytes 1622020
  106.8 26.8 %collective-permute-start.9 = (bf16[176,1536]{1,0:T(8,128)(2,1)S(1)}, bf16[176,1536]{1,0:T(8,128)(2,1)S(1)}, u32[]{:S(2)}, u32[]{:S(2)}) collective-permute-start(bf16[176,1536]{1,0:T(8,128)(2,1)S(1)} %copy-done.8), channel_id=1, source_target_pairs={{0,1},{1,0},{2,3},{3,2},{4,5},{5,4},{6,7},{7,6},{8,9},{9,8},{10,11... | collective-permute-start | bytes 1622024 | tf_op jit(solution)/shard_map/ppermute | solution.py:199
  106.9 19.4 %copy-start.14 = (bf16[640,1536]{1,0:T(8,128)(2,1)S(1)}, bf16[640,1536]{1,0:T(8,128)(2,1)}, u32[]{:S(2)}) copy-start(bf16[640,1536]{1,0:T(8,128)(2,1)} %get-tuple-element.13) | copy-start | bytes 5898244
  132.3 106.7 %collective-permute-start.21 = (bf16[512,1536]{1,0:T(8,128)(2,1)}, bf16[512,1536]{1,0:T(8,128)(2,1)S(1)}, u32[]{:S(2)}, u32[]{:S(2)}) collective-permute-start(bf16[512,1536]{1,0:T(8,128)(2,1)} %broadcast_select_fusion.2), channel_id=1, source_target_pairs={{0,1},{2,3},{4,5},{6,7},{9,8},{11,10},{13,12},{15,14},{18,19},{16,... | collective-permute-start | bytes 4718600 | tf_op jit(solution)/shard_map/ppermute | solution.py:199
  133.6 0.8 copy-start.9
  133.6 1.0 copy-start.10
  133.6 1.1 copy-start.11
  134.8 0.8 copy-start.12
  234.8 2.7 copy-start.1
  237.7 14.6 %collective-permute-start.16 = (bf16[768,1024]{1,0:T(8,128)(2,1)S(1)}, bf16[768,1024]{1,0:T(8,128)(2,1)}, u32[]{:S(2)}, u32[]{:S(2)}) collective-permute-start(bf16[768,1024]{1,0:T(8,128)(2,1)S(1)} %dynamic-slice_convert_fusion), channel_id=1, source_target_pairs={{0,1},{1,0},{2,3},{3,2},{4,5},{5,4},{6,7},{7,6},{8,9},{9,8},{10,11... | collective-permute-start | bytes 4718600 | tf_op jit(solution)/shard_map/ppermute | solution.py:199
  285.4 11.8 %copy-start.15 = (bf16[640,1536]{1,0:T(8,128)(2,1)S(1)}, bf16[640,1536]{1,0:T(8,128)(2,1)}, u32[]{:S(2)}) copy-start(bf16[640,1536]{1,0:T(8,128)(2,1)} %get-tuple-element.13) | copy-start | bytes 5898244
  297.1 2.7 copy-start.13
  305.3 1.6 copy-start.2
  307.9 4.4 %collective-permute-start.22 = (bf16[768,512]{1,0:T(8,128)(2,1)}, bf16[768,512]{1,0:T(8,128)(2,1)}, u32[]{:S(2)}, u32[]{:S(2)}) collective-permute-start(bf16[768,512]{1,0:T(8,128)(2,1)} %dynamic-slice_convert_fusion.1), channel_id=1, source_target_pairs={{0,1},{1,0},{2,3},{3,2},{4,5},{5,4},{6,7},{7,6},{8,9},{9,8},{10,11... | collective-permute-start | bytes 2359304 | tf_op jit(solution)/shard_map/ppermute | solution.py:199
  309.4 21.1 %collective-permute-start.17 = (bf16[384,1024]{1,0:T(8,128)(2,1)}, bf16[384,1024]{1,0:T(8,128)(2,1)}, u32[]{:S(2)}, u32[]{:S(2)}) collective-permute-start(bf16[384,1024]{1,0:T(8,128)(2,1)} %dynamic-slice_convert_fusion.2.refs_3_), channel_id=1, source_target_pairs={{0,2},{1,3},{2,0},{3,1},{4,6},{5,7},{6,4},{7,5},{8,10},{9,11},{10,... | collective-permute-start | bytes 2359304 | tf_op jit(solution)/shard_map/ppermute | solution.py:199
  314.2 17.8 %copy-start = (f32[768,512]{1,0:T(8,128)}, f32[768,512]{1,0:T(8,128)S(1)}, u32[]{:S(2)}) copy-start(f32[768,512]{1,0:T(8,128)S(1)} %convert_add_fusion.1) | copy-start | bytes 4718596
  315.1 28.6 %collective-permute-start.23 = (bf16[384,512]{1,0:T(8,128)(2,1)}, bf16[384,512]{1,0:T(8,128)(2,1)S(1)}, u32[]{:S(2)}, u32[]{:S(2)}) collective-permute-start(bf16[384,512]{1,0:T(8,128)(2,1)} %dynamic-slice_convert_fusion.3), channel_id=1, source_target_pairs={{0,2},{1,3},{2,0},{3,1},{4,6},{5,7},{6,4},{7,5},{8,10},{9,11},{10,... | collective-permute-start | bytes 1179656 | tf_op jit(solution)/shard_map/ppermute | solution.py:199
  332.0 32.7 %collective-permute-start.18 = (bf16[192,1024]{1,0:T(8,128)(2,1)S(1)}, bf16[192,1024]{1,0:T(8,128)(2,1)S(1)}, u32[]{:S(2)}, u32[]{:S(2)}) collective-permute-start(bf16[192,1024]{1,0:T(8,128)(2,1)S(1)} %get-tuple-element.19), channel_id=1, source_target_pairs={{0,0},{1,16},{2,8},{3,24},{4,4},{5,20},{6,12},{7,28},{8,1},{9,17},... | collective-permute-start | bytes 1179656 | tf_op jit(solution)/shard_map/ppermute | solution.py:199
  339.2 31.8 %collective-permute-start.19 = (bf16[192,1024]{1,0:T(8,128)(2,1)S(1)}, bf16[192,1024]{1,0:T(8,128)(2,1)S(1)}, u32[]{:S(2)}, u32[]{:S(2)}) collective-permute-start(bf16[192,1024]{1,0:T(8,128)(2,1)S(1)} %get-tuple-element.20), channel_id=1, source_target_pairs={{0,4},{1,20},{2,12},{3,28},{4,0},{5,16},{6,8},{7,24},{8,5},{9,21},... | collective-permute-start | bytes 1179656 | tf_op jit(solution)/shard_map/ppermute | solution.py:199
  345.0 30.2 %collective-permute-start.24 = (bf16[192,512]{1,0:T(8,128)(2,1)S(1)}, bf16[192,512]{1,0:T(8,128)(2,1)S(1)}, u32[]{:S(2)}, u32[]{:S(2)}) collective-permute-start(bf16[192,512]{1,0:T(8,128)(2,1)S(1)} %get-tuple-element.23), channel_id=1, source_target_pairs={{0,0},{1,16},{2,8},{3,24},{4,4},{5,20},{6,12},{7,28},{8,1},{9,17},... | collective-permute-start | bytes 589832 | tf_op jit(solution)/shard_map/ppermute | solution.py:199
  356.0 23.4 %collective-permute-start.25 = (bf16[192,512]{1,0:T(8,128)(2,1)S(1)}, bf16[192,512]{1,0:T(8,128)(2,1)S(1)}, u32[]{:S(2)}, u32[]{:S(2)}) collective-permute-start(bf16[192,512]{1,0:T(8,128)(2,1)S(1)} %get-tuple-element.24), channel_id=1, source_target_pairs={{0,4},{1,20},{2,12},{3,28},{4,0},{5,16},{6,8},{7,24},{8,5},{9,21},... | collective-permute-start | bytes 589832 | tf_op jit(solution)/shard_map/ppermute | solution.py:199
where the time goes:
time: 387 us; the launch traced here: 381 us
  Pallas kernels  194 us (50%)
  starting transfers between devices  54.2 us (14%)
  waiting for transfers between devices  52.4 us (14%)
  other arithmetic  29.9 us (8%)
  matrix products  25.6 us (7%)
  local copies, waits for them, and re-layouts  18.7 us (5%)
  between operations  6.03 us (2%)
    pallas_call x4, Pallas kernels, pair_gradients(): pl.pallas_call(functools.partial(pair_kernel, parts, groups, sub, len(aft...  111 us
    pallas_call x6, Pallas kernels, project(): pl.pallas_call(functools.partial(columns_kernel, count, tuple(rows_each),...  66.2 us
    ppermute x26, starting transfers between devices, send(): return lax.ppermute(x, axes, pairs)  54.2 us
    ppermute x26, waiting for transfers between devices, send(): return lax.ppermute(x, axes, pairs)  52.4 us
    dot_general x4, matrix products, dot(): return lax.dot_general(a, b, dims, preferred_element_type=F32)  25.6 us
    pallas_call x1, Pallas kernels, turned(): pl.pallas_call(turn_kernel, out_shape=jax.ShapeDtypeStruct((cols, rows),...  14.6 us
  transfers between devices with their start and end apart: 26, of which 7 were waited for; matrix products, arithmetic and copies ran while one was open for 13% of the time, Pallas kernels for 40%

commit v1 on v0

v1 whole, which is shorter than its diff:
```python
import functools

import jax
import jax.numpy as jnp
from jax import lax
from jax.experimental import pallas as pl
from jax.experimental.pallas import tpu as pltpu
from jax.sharding import PartitionSpec as P

F32 = jnp.float32
BF16 = jnp.bfloat16
BOTH = ("walk", "pt")
NT = (((1,), (1,)), ((), ()))
VMEM_LIMIT = 56 * 1024 * 1024


def tile_of(size, limit):
    return next(t for t in range(min(size, limit), 0, -128) if size % t == 0)


def dot(a, b, dims=(((1,), (0,)), ((), ()))):
    return lax.dot_general(a, b, dims, preferred_element_type=F32)


def cost(flops, nbytes):
    return pl.CostEstimate(flops=flops, bytes_accessed=nbytes, transcendentals=0)


def turn_kernel(in_ref, out_ref):
    out_ref[...] = in_ref[...].T


def turned(block):
    rows, cols = block.shape
    tr, tc = tile_of(rows, 512), tile_of(cols, 512)
    return pl.pallas_call(
        turn_kernel,
        out_shape=jax.ShapeDtypeStruct((cols, rows), block.dtype),
        grid=(cols // tc, rows // tr),
        in_specs=[pl.BlockSpec((tr, tc), lambda c, r: (r, c))],
        out_specs=pl.BlockSpec((tc, tr), lambda c, r: (c, r)),
        compiler_params=pltpu.CompilerParams(vmem_limit_bytes=VMEM_LIMIT),
        cost_estimate=cost(0, 10 * rows * cols),
    )(block)


def pack_kernel(group_ref, occupied_ref, side_ref, weight_ref, bra_ref, ket_ref, own_ref, half_ref):
    occ = bra_ref.shape[0]
    used = occupied_ref[group_ref[0]]
    kept = lax.broadcasted_iota(jnp.int32, bra_ref.shape, 0) < used
    bra_t = jnp.where(kept, bra_ref[...].astype(F32), 0.0).astype(BF16)
    ket_t = jnp.where(kept, ket_ref[...].astype(F32), 0.0).astype(BF16)
    own_ref[:occ, :] = bra_t
    own_ref[occ : 2 * occ, :] = ket_t

    @pl.when(side_ref[0] == 0)
    def _():
        half_ref[:occ, :] = bra_t

    @pl.when(side_ref[0] != 0)
    def _():
        half_ref[:occ, :] = ket_t

    shape = (half_ref.shape[0] - occ, half_ref.shape[1])
    row = lax.broadcasted_iota(jnp.int32, shape, 0)
    rest, rows = jnp.full(shape, weight_ref[0], F32), jnp.zeros(shape, F32)
    for part in range(3):
        near = rest.astype(BF16).astype(F32)
        rows = jnp.where(row == part, near, rows)
        rest = rest - near
    half_ref[occ:, :] = rows.astype(BF16)
    own_ref[2 * occ :, :] = rows.astype(BF16)


def packed(bra, ket, group, occupied, side, weight):
    occ, size_m = bra.shape
    smem = pl.BlockSpec(memory_space=pltpu.SMEM)
    return pl.pallas_call(
        pack_kernel,
        out_shape=[
            jax.ShapeDtypeStruct((2 * occ + 16, size_m), BF16),
            jax.ShapeDtypeStruct((occ + 16, size_m), BF16),
        ],
        in_specs=[smem] * 4 + [pl.BlockSpec(memory_space=pltpu.VMEM)] * 2,
        compiler_params=pltpu.CompilerParams(vmem_limit_bytes=VMEM_LIMIT),
        cost_estimate=cost(0, 12 * size_m * occ),
    )(group, occupied, side, weight, bra, ket)


def project_kernel(rows_each, waits, *refs):
    count = len(rows_each)
    items, col_ref = refs[:count], refs[count]
    out_ref, stack_out, weight_out, stack = refs[count + 1 + waits :]
    occ = min(rows_each)

    @pl.when(pl.program_id(0) == 0)
    def _():
        at = 0
        weight_out[...] = jnp.zeros_like(weight_out)
        for ref, rows in zip(items, rows_each):
            stack[at : at + rows, :] = ref[:rows, :]
            if at % (2 * occ) == 0:
                s = at // (2 * occ)
                weight_out[s : s + 1, :] = jnp.sum(ref[rows : rows + 16, :128].astype(F32), axis=0, keepdims=True)
            at += rows
        stack_out[...] = stack[...]

    out_ref[...] = dot(stack[...], col_ref[...], NT).astype(BF16)


def project(items, rows_each, col, groups, index, before=(), after=()):
    size_m, size, total = col.shape[1], col.shape[0], sum(rows_each)
    tile = tile_of(size, 512)
    hbm, waits = pl.BlockSpec(memory_space=pl.ANY), (*before, *after)
    return pl.pallas_call(
        functools.partial(project_kernel, tuple(rows_each), len(waits)),
        out_shape=[
            jax.ShapeDtypeStruct((groups * total, size), BF16),
            jax.ShapeDtypeStruct((groups * total, size_m), BF16),
            jax.ShapeDtypeStruct((groups * 8, 128), F32),
        ],
        grid=(size // tile,),
        in_specs=[pl.BlockSpec(x.shape, lambda b: (0, 0), pipeline_mode=pl.Buffered(1)) for x in items]
        + [pl.BlockSpec((tile, size_m), lambda b: (b, 0))]
        + [hbm] * len(waits),
        out_specs=[
            pl.BlockSpec((total, tile), lambda b: (index, b)),
            pl.BlockSpec((total, size_m), lambda b: (index, 0), pipeline_mode=pl.Buffered(1)),
            pl.BlockSpec((8, 128), lambda b: (index, 0)),
        ],
        scratch_shapes=[pltpu.VMEM((total, size_m), BF16)],
        input_output_aliases={len(items) + 1 + n: n for n in range(len(before))},
        compiler_params=pltpu.CompilerParams(vmem_limit_bytes=VMEM_LIMIT),
        cost_estimate=cost(2 * (total + 640) * size_m * size, 2 * size_m * size),
    )(*items, col, *waits)


def pair_kernel(sub, first, waits, weight_ref, kt_ref, lrp_ref, lrq_ref, *refs):
    out_ref, sides, totals = refs[waits:]
    occ = sides.shape[2]
    count = sides.shape[0] // 2
    for n in range(2 * count):
        sides[n] = lrq_ref[:, n * occ : (n + 1) * occ]
    totals[...] = jnp.zeros_like(totals)

    def columns(t, carry):
        at = pl.ds(pl.multiple_of(t * sub, sub), sub)
        kern = kt_ref[:, at]
        for n in range(count):
            left_t = lrp_ref[2 * n * occ : (2 * n + 1) * occ, at]
            right_t = lrp_ref[(2 * n + 1) * occ : (2 * n + 2) * occ, at]
            had_t = kern * dot(sides[2 * n + 1], left_t).astype(BF16)
            had = kern * dot(sides[2 * n], right_t).astype(BF16)
            totals[2 * n] += dot(had_t, right_t, NT)
            totals[2 * n + 1] += dot(had, left_t, NT)
        return carry

    lax.fori_loop(0, kt_ref.shape[1] // sub, columns, 0)
    for n in range(2 * count):
        scale = 2.0 * weight_ref[(first + pl.program_id(0)) * count + n // 2]
        out_ref[:, n * occ : (n + 1) * occ] = (totals[n] * scale).astype(BF16)


def pair_gradients(weights, kernel_t, lrp, lrq, row_at, pairs=None, after=()):
    size_b, rows, count = kernel_t.shape[1], lrq.shape[0], weights.shape[0] // 2
    first, last = pairs or (0, count)
    width = lrp.shape[0] // count
    occ = width // 4
    at, sub = row_at // rows, tile_of(size_b, 512)
    return pl.pallas_call(
        functools.partial(pair_kernel, sub, first, len(after)),
        out_shape=jax.ShapeDtypeStruct((rows, (last - first) * width), BF16),
        grid_spec=pltpu.PrefetchScalarGridSpec(
            num_scalar_prefetch=1,
            grid=(last - first,),
            in_specs=[
                pl.BlockSpec((rows, size_b), lambda p, s: (at, 0), pipeline_mode=pl.Buffered(1)),
                pl.BlockSpec((width, size_b), lambda p, s: (first + p, 0)),
                pl.BlockSpec((rows, width), lambda p, s: (0, first + p)),
            ]
            + [pl.BlockSpec(memory_space=pl.ANY)] * len(after),
            out_specs=pl.BlockSpec((rows, width), lambda p, s: (0, p)),
            scratch_shapes=[pltpu.VMEM((4, rows, occ), BF16), pltpu.VMEM((4, rows, occ), F32)],
        ),
        compiler_params=pltpu.CompilerParams(vmem_limit_bytes=VMEM_LIMIT),
        cost_estimate=cost(
            2 * 4 * (last - first) * 2 * 256 * rows * size_b, 2 * (last - first) * (rows + width) * size_b
        ),
    )(weights, kernel_t, lrp, lrq, *after)


def send(x, axes, pairs):
    return lax.ppermute(x, axes, pairs)


def masked_orbitals(bra_orbitals, ket_orbitals, walker_group, group_occupied):
    group_count, occ = group_occupied.shape[0], bra_orbitals.shape[2]
    matches = walker_group[:, None] == jnp.arange(group_count, dtype=jnp.int32)[None, :]
    occupied = jnp.sum(jnp.where(matches, group_occupied[None, :], 0), axis=1)
    masks = (jnp.arange(occ, dtype=jnp.int32)[None, :] < occupied[:, None]).astype(BF16)
    bra_t = jnp.swapaxes(bra_orbitals * masks[:, None, :], 1, 2)
    ket_t = jnp.swapaxes(ket_orbitals * masks[:, None, :], 1, 2)
    return jnp.concatenate([bra_t, ket_t], axis=1)


def on_device_8x4(bra, ket, collocation, kernel, walker_weight, walker_group, group_occupied):
    nw, npt = 8, 4
    size_b, size_a = kernel.shape
    occ, size_m = bra.shape
    width = 2 * occ
    me_w, me_p = lax.axis_index("walk"), lax.axis_index("pt")
    z, x, y, core = me_w // 2, me_w % 2, me_p // 2, me_p % 2

    def put(j, i):
        return j * npt + i

    def across(part):
        return send(part, "walk", [(j, j ^ 1) for j in range(nw)])

    def along(part, r):
        return send(part, "walk", [(j, (j - 2 * r) % nw) for j in range(nw)])

    def other(part):
        return send(part, "pt", [(i, i ^ 1) for i in range(npt)])

    def columns_q(begin, chunk):
        rows = lax.dynamic_slice_in_dim(collocation, x * size_a + begin, chunk, 0)
        far = send(rows, BOTH, [(put(j, j // 2), put(j, j // 2 ^ 2)) for j in range(nw)])
        near = jnp.where(me_p == z, rows, far)
        pairs = [(put(j, j // 2 ^ s), put(j, j // 2 ^ s ^ 1)) for j in range(nw) for s in (0, 2)]
        return jnp.where(core == z % 2, near, send(near, BOTH, pairs))

    def split(part, at, size, axis=1):
        give = lax.dynamic_slice_in_dim(part, (1 - at) * size, size, axis).astype(BF16)
        return give, lax.dynamic_slice_in_dim(part, at * size, size, axis)

    chunks = [(0, 2 * size_a // 3), (2 * size_a // 3, size_a // 3)]
    own, half = packed(bra, ket, walker_group, group_occupied, core.reshape(1), walker_weight)
    cols_q = [columns_q(*chunk) for chunk in chunks]
    z1, z3, x0 = along(half, 1), along(half, 3), across(half)
    z2 = along(half, 2)
    kernel_t = turned(kernel)
    x0, z1, z3, kernel_t = lax.optimization_barrier((x0, z1, z3, kernel_t))
    x1, x3, x2 = across(z1), across(z3), across(z2)
    near_four = [own] + [h for part in (x0, z1, z3) for h in (part, other(part))]
    far_four = [h for part in (x1, x3, z2, x2) for h in (part, other(part))]
    first = project(near_four, [width] + [occ] * 6, collocation, 2, 0)
    lrp, stack, weight_rows = project(far_four, [occ] * 8, collocation, 2, 1, first)
    weights = jnp.concatenate([weight_rows[:4, 0], weight_rows[8:12, 0]])

    def rows_q(c):
        return dot(cols_q[c], stack, NT).astype(BF16)

    half_m, quarter, eighth = size_m // 2, size_m // 4, size_m // 8
    swap_y = [(i, i ^ 2) for i in range(npt)]

    def to_place(part):
        pieces = [lax.dynamic_slice_in_dim(part, (x ^ t) * eighth, eighth, 1) for t in (0, 1)]
        came = []
        for t in (0, 1):
            pairs = []
            for j in range(nw):
                for i in range(npt):
                    quarter_of = 2 * (i % 2) + i // 2
                    pairs.append((put(j, i), put(2 * quarter_of + (j % 2 ^ t), j // 2)))
            came.append(send(pieces[t], BOTH, pairs))
        return pieces, came

    def over_cores(grads):
        give, keep = split(dot(grads, stack), core, half_m)
        return split(keep + other(give).astype(F32), y, quarter)

    grads = pair_gradients(weights, kernel_t, lrp, rows_q(0), chunks[0][0])
    lrq = rows_q(1)
    give, keep = over_cores(grads)
    got = send(give, "pt", swap_y)
    early = pair_gradients(weights, kernel_t, lrp, lrq, chunks[1][0], (0, 2), (give[:16, :128],))
    pieces, came_0 = to_place((keep + got.astype(F32)).astype(BF16))
    late = pair_gradients(weights, kernel_t, lrp, lrq, chunks[1][0], (2, 4), (early, *pieces))
    give, keep = over_cores(jnp.concatenate([early, late], axis=1))
    _, came_1 = to_place((keep + send(give, "pt", swap_y).astype(F32)).astype(BF16))

    ordered = [jnp.where(x == side, came[0], came[1]) for side in (0, 1) for came in (came_0, came_1)]
    return jnp.concatenate(ordered, axis=0).astype(F32) / jnp.sum(weights)


def on_device_any(nw, own, collocation, kernel, walker_weight):
    size_b, size_a = kernel.shape
    size_m = collocation.shape[1]
    me_w, me_p = lax.axis_index("walk"), lax.axis_index("pt")
    weights = lax.all_gather(walker_weight, "walk", axis=0, tiled=True)
    orbitals = lax.all_gather(own, "walk", axis=0, tiled=True)
    all_rows = lax.all_gather(collocation, "pt", axis=0, tiled=True)
    col_q = lax.dynamic_slice_in_dim(all_rows, me_w * size_a, size_a, 0)
    lrp = dot(orbitals, collocation, NT).astype(BF16)
    lrq = dot(col_q, orbitals, NT).astype(BF16)
    grads = pair_gradients(weights / jnp.sum(weights), turned(kernel), lrp, lrq, 0)
    part = lax.psum(dot(grads, orbitals), "pt")
    part = jnp.where((me_w * size_a) // size_b == me_p, part, 0.0)
    wide = lax.dynamic_update_slice_in_dim(jnp.zeros((size_b, size_m), F32), part, (me_w * size_a) % size_b, 0)
    return lax.psum_scatter(wide, "walk", scatter_dimension=1, tiled=True)


def on_device(
    nw, npt, bra_orbitals, ket_orbitals, collocation, kernel, walker_weight, walker_group, group_occupied
):
    if (nw, npt, walker_weight.shape[0]) == (8, 4, 1) and kernel.shape[0] == 2 * kernel.shape[1]:
        bra, ket = bra_orbitals[0].T, ket_orbitals[0].T
        return on_device_8x4(bra, ket, collocation, kernel, walker_weight, walker_group, group_occupied)
    own = masked_orbitals(bra_orbitals, ket_orbitals, walker_group, group_occupied)
    return on_device_any(nw, own.reshape(-1, own.shape[2]), collocation, kernel, walker_weight)


def solution(mesh):
    in_specs = (
        P("walk", None, None),
        P("walk", None, None),
        P("pt", None),
        P("pt", "walk"),
        P("walk"),
        P("walk"),
        P(),
    )
    out_specs = P("pt", "walk")
    body = functools.partial(on_device, mesh.shape["walk"], mesh.shape["pt"])
    return jax.shard_map(body, mesh=mesh, in_specs=in_specs, out_specs=out_specs, check_vma=False)
```

time: 387 us -> 350 us (0.904); the launches traced: 381 us -> 349 us
  Pallas kernels: 194 us -> 165 us
  waiting for transfers between devices: 52.4 us -> 75.5 us
  other arithmetic: 29.9 us -> 10.2 us
  matrix products: 25.6 us -> 42.2 us
  starting transfers between devices: 54.2 us -> 37.7 us
    pallas_call x11 -> x6, Pallas kernels: 180 us -> 150 us  [the longest x3 111 us: pair_gradients(): pl.pallas_call(functools.partial(pair_kernel, sub, first, len(after)), ou...]
    ppermute x26, waiting for transfers between devices: 52.4 us -> 75.5 us  [send(): return lax.ppermute(x, axes, pairs)]
    dot_general x4, matrix products: 25.6 us -> 42.2 us  [dot(): return lax.dot_general(a, b, dims, preferred_element_type=F32)]
    ppermute x26, starting transfers between devices: 54.2 us -> 37.7 us  [send(): return lax.ppermute(x, axes, pairs)]
    reduce_sum x7 -> x1, other arithmetic: 7.18 us -> 1.31 us  [on_device_8x4(): return jnp.concatenate(ordered, axis=0).astype(F32) / jnp.sum(weights)]
    another operation x1 -> x0, local copies, waits for them, and re-layouts: 4.41 us -> none  [on_device_8x4(): jnp.stack([weight_of(part) for part in (z1, z3, x1, x3, z2, x2)])]
    select_n x4 -> x2, other arithmetic: 5.33 us -> 1.15 us  [on_device_8x4(): jnp.where(x == side, came[0], came[1])]
  transfers between devices with their start and end apart: 26 -> 26, of which waited for: 7 -> 8; matrix products, arithmetic and copies ran while one was open for 13% -> 13% of each run, Pallas kernels for 40% -> 41%
where the time goes in v1:
time: 350 us; the launch traced here: 349 us
  Pallas kernels  165 us (47%)
  waiting for transfers between devices  75.5 us (22%)
  matrix products  42.2 us (12%)
  starting transfers between devices  37.7 us (11%)
  local copies, waits for them, and re-layouts  16.2 us (5%)
  other arithmetic  10.2 us (3%)
    pallas_call x3, Pallas kernels, pair_gradients(): pl.pallas_call(functools.partial(pair_kernel, sub, first, len(after)), ou...  111 us
    ppermute x26, waiting for transfers between devices, send(): return lax.ppermute(x, axes, pairs)  75.5 us
    dot_general x4, matrix products, dot(): return lax.dot_general(a, b, dims, preferred_element_type=F32)  42.2 us
    ppermute x26, starting transfers between devices, send(): return lax.ppermute(x, axes, pairs)  37.7 us
    pallas_call x2, Pallas kernels, project(): pl.pallas_call(functools.partial(project_kernel, tuple(rows_each), len(wa...  35.9 us
    pallas_call x1, Pallas kernels, turned(): pl.pallas_call(turn_kernel, out_shape=jax.ShapeDtypeStruct((cols, rows),...  14.8 us
  transfers between devices with their start and end apart: 26, of which 8 were waited for; matrix products, arithmetic and copies ran while one was open for 13% of the time, Pallas kernels for 41%

profile of v1, /device:TPU:1, one launch (start us, length us, event | category | flops | bytes accessed | tf_op | source)
XLA Modules:
  0.0 349.3 jit_solution(7252383162165481198)
XLA Ops:
  0.0 3.7 %constant_dynamic-slice_fusion.5 = bf16[1024,1536]{1,0:T(8,128)(2,1)} fusion(bf16[3072,1536]{1,0:T(8,128)(2,1)} %refs_8_.1, s32[]{:T(128)S(6)} %select_n.117), kind=kLoop, calls=%fused_computation.30 | loop fusion | bytes 6291460 | tf_op jit(solution)/shard_map/dynamic_slice | solution.py:227
  3.7 0.9 collective-permute-start.14
  5.9 2.5 shard_map.73
  8.4 2.0 collective-permute-start
  10.5 3.8 %collective-permute-start.1 = (bf16[176,1536]{1,0:T(8,128)(2,1)}, bf16[176,1536]{1,0:T(8,128)(2,1)}, u32[]{:S(2)}, u32[]{:S(2)}) collective-permute-start(bf16[176,1536]{1,0:T(8,128)(2,1)} %get-tuple-element.17), channel_id=1, source_target_pairs={{0,24},{4,28},{8,0},{12,4},{16,8},{20,12},{24,16},{28,20},{1,25},{... | collective-permute-start | bytes 1622024 | tf_op jit(solution)/shard_map/ppermute | solution.py:193
  14.3 1.2 collective-permute-start.7
  15.4 14.8 %shard_map.74.kt_ref = bf16[1536,3072]{1,0:T(8,128)(2,1)} custom-call(bf16[3072,1536]{1,0:T(8,128)(2,1)} %in_ref.1), custom_call_target="tpu_custom_call" | custom-call | bytes 47185920 | tf_op jit(solution)/shard_map/pallas_call | solution.py:36
  30.2 2.7 constant_dynamic-slice_fusion.2
  32.9 0.8 collective-permute-start.20
  33.6 3.8 %collective-permute-done.2.refs_5_ = bf16[176,1536]{1,0:T(8,128)(2,1)} collective-permute-done((bf16[176,1536]{1,0:T(8,128)(2,1)}, bf16[176,1536]{1,0:T(8,128)(2,1)}, u32[]{:S(2)}, u32[]{:S(2)}) %collective-permute-start.2) | collective-permute-done | bytes 540704 | tf_op jit(solution)/shard_map/ppermute | solution.py:193
  37.4 3.7 %collective-permute-start.11 = (bf16[176,1536]{1,0:T(8,128)(2,1)}, bf16[176,1536]{1,0:T(8,128)(2,1)S(1)}, u32[]{:S(2)}, u32[]{:S(2)}) collective-permute-start(bf16[176,1536]{1,0:T(8,128)(2,1)} %collective-permute-done.refs_1_), channel_id=1, source_target_pairs={{0,1},{1,0},{2,3},{3,2},{4,5},{5,4},{6,7},{7,6},{8,9},{9,8},{10,11... | collective-permute-start | bytes 1622024 | tf_op jit(solution)/shard_map/ppermute | solution.py:193
  41.1 2.6 collective-permute-start.13
  43.7 2.7 broadcast_select_fusion
  46.5 15.5 %collective-permute-done.7.refs_4_ = bf16[176,1536]{1,0:T(8,128)(2,1)} collective-permute-done((bf16[176,1536]{1,0:T(8,128)(2,1)}, bf16[176,1536]{1,0:T(8,128)(2,1)}, u32[]{:S(2)}, u32[]{:S(2)}) %collective-permute-start.7) | collective-permute-done | bytes 540704 | tf_op jit(solution)/shard_map/ppermute | solution.py:193
  62.0 0.3 collective-permute-start.3
  62.3 1.2 collective-permute-start.5
  63.5 0.3 collective-permute-start.9
  63.7 0.5 copy-done.9
  64.3 1.3 collective-permute-start.15
  65.6 17.9 %shard_map.75 = (bf16[2560,3072]{1,0:T(8,128)(2,1)}, bf16[2560,1536]{1,0:T(8,128)(2,1)}, f32[16,128]{1,0:T(8,128)}) custom-call(bf16[336,1536]{1,0:T(8,128)(2,1)} %get-tuple-element.20.refs_0_, bf16[176,1536]{1,0:T(8,128)(2,1)} %collective-permute-done.refs_1_, bf16[176,1536]{1,0:T(8,128)(2,1)} %copy-done.8, ...), custom_call_target="tpu_custom_call" | custom-call | flops 18119393280 | bytes 9437184 | tf_op jit(solution)/shard_map/pallas_call | solution.py:115
  83.5 2.8 collective-permute-start.8
  86.3 1.7 collective-permute-done.5.refs_2_
  88.0 0.6 collective-permute-start.4
  88.6 11.0 %collective-permute-done.9.refs_6_ = bf16[176,1536]{1,0:T(8,128)(2,1)S(1)} collective-permute-done((bf16[176,1536]{1,0:T(8,128)(2,1)}, bf16[176,1536]{1,0:T(8,128)(2,1)S(1)}, u32[]{:S(2)}, u32[]{:S(2)}) %collective-permute-start.9) | collective-permute-done | bytes 540704 | tf_op jit(solution)/shard_map/ppermute | solution.py:193
  99.6 0.5 collective-permute-start.6
  100.1 1.8 broadcast_select_fusion.1
  102.0 1.5 collective-permute-start.21
  103.5 0.7 copy-done.10
  104.3 0.2 copy-done.11
  104.5 0.2 copy-done.13
  104.6 17.9 %shard_map.76 = (bf16[2560,3072]{1,0:T(8,128)(2,1)}, bf16[2560,1536]{1,0:T(8,128)(2,1)}, f32[16,128]{1,0:T(8,128)}) custom-call(bf16[176,1536]{1,0:T(8,128)(2,1)} %copy-done.4, bf16[176,1536]{1,0:T(8,128)(2,1)} %copy-done.10, bf16[176,1536]{1,0:T(8,128)(2,1)} %copy-done.5, ...), custom_call_target="tpu_custom_call", output_to_operand_aliasing={{0}: (9, {}), {1}: (10, {}), {2}: (11, {})} | custom-call | flops 18119393280 | bytes 9437184 | tf_op jit(solution)/shard_map/pallas_call | solution.py:115
  122.6 1.3 slice_reduce_fusion
  123.9 0.6 pad_maximum_fusion.weight_ref
  124.5 13.2 %convolution_convert_fusion.lrq_ref = bf16[1024,2560]{1,0:T(8,128)(2,1)} fusion(bf16[2560,1536]{1,0:T(8,128)(2,1)} %get-tuple-element.28, bf16[1024,1536]{1,0:T(8,128)(2,1)S(1)} %broadcast_select_fusion, bf16[1024,1536]{1,0:T(8,128)(2,1)} %collective-permute-done.15, pred[]{:T(512)S(6)} %eq.22), kind=kOutput, calls=%fused_computation | convolution fusion | flops 8057257984 | bytes 19398656 | tf_op jit(solution)/shard_map/dot_general | solution.py:22
  137.7 68.8 %shard_map.77 = bf16[1024,2560]{1,0:T(8,128)(2,1)} custom-call(f32[8]{0:T(128)} %pad_maximum_fusion.weight_ref, bf16[1536,3072]{1,0:T(8,128)(2,1)} %shard_map.74.kt_ref, bf16[2560,3072]{1,0:T(8,128)(2,1)} %get-tuple-element.27.lrp_ref, bf16[1024,2560]{1,0:T(8,128)(2,1)} %convolution_convert_fusion.lrq_ref), custom_call_target="tpu_custom_call" | custom-call | flops 51539607552 | bytes 40894464 | tf_op jit(solution)/shard_map/pallas_call | solution.py:170
  206.5 12.4 %fusion.9 = f32[1024,1536]{1,0:T(8,128)S(1)} fusion(bf16[1024,2560]{1,0:T(8,128)(2,1)} %shard_map.77, bf16[2560,1536]{1,0:T(8,128)(2,1)} %get-tuple-element.28), kind=kOutput, calls=%fused_computation.37 | convolution fusion | flops 8053063680 | bytes 19398656 | tf_op jit(solution)/shard_map/dot_general | solution.py:22
  218.9 2.6 copy-done
  221.5 0.2 dynamic-slice_convert_fusion
  221.7 1.1 collective-permute-start.16
  222.8 9.6 %convolution_convert_fusion.1.lrq_ref = bf16[512,2560]{1,0:T(8,128)(2,1)} fusion(bf16[2560,1536]{1,0:T(8,128)(2,1)} %get-tuple-element.28, bf16[512,1536]{1,0:T(8,128)(2,1)S(1)} %broadcast_select_fusion.1, bf16[512,1536]{1,0:T(8,128)(2,1)} %collective-permute-done.21, pred[]{:T(512)S(6)} %eq.22), kind=kOutput, calls=%fused_computation.1 | convolution fusion | flops 4028628992 | bytes 13631489 | tf_op jit(solution)/shard_map/dot_general | solution.py:22
  232.5 1.9 convert_add_fusion
  234.3 0.1 dynamic-slice_convert_fusion.2
  234.5 0.6 slice.12.refs_0_
  235.1 21.3 %shard_map.78.refs_0_ = bf16[512,1280]{1,0:T(8,128)(2,1)} custom-call(f32[8]{0:T(128)} %pad_maximum_fusion.weight_ref, bf16[1536,3072]{1,0:T(8,128)(2,1)} %shard_map.74.kt_ref, bf16[2560,3072]{1,0:T(8,128)(2,1)} %get-tuple-element.27.lrp_ref, bf16[512,2560]{1,0:T(8,128)(2,1)} %convolution_convert_fusion.1.lrq_ref, bf16[16,128]{1,0:T(8,128)(2,1)} %slice.12.refs_0_), custom_call_target="tpu_custom_call" | custom-call | flops 12884901888 | bytes 14155776 | tf_op jit(solution)/shard_map/pallas_call | solution.py:170
  256.4 0.2 add_convert_fusion
  256.5 1.4 constant_dynamic-slice_fusion.3
  257.9 21.4 %shard_map.79 = bf16[512,1280]{1,0:T(8,128)(2,1)} custom-call(f32[8]{0:T(128)} %pad_maximum_fusion.weight_ref, bf16[1536,3072]{1,0:T(8,128)(2,1)} %shard_map.74.kt_ref, bf16[2560,3072]{1,0:T(8,128)(2,1)} %get-tuple-element.27.lrp_ref, bf16[512,2560]{1,0:T(8,128)(2,1)} %convolution_convert_fusion.1.lrq_ref, bf16[512,1280]{1,0:T(8,128)(2,1)} %shard_map.78.refs_0_, ...), custom_call_target="tpu_custom_call" | custom-call | flops 12884901888 | bytes 14155776 | tf_op jit(solution)/shard_map/pallas_call | solution.py:170
  279.4 6.9 %fusion.2 = f32[512,1536]{1,0:T(8,128)S(1)} fusion(bf16[2560,1536]{1,0:T(8,128)(2,1)} %get-tuple-element.28, bf16[512,1280]{1,0:T(8,128)(2,1)} %shard_map.79, bf16[512,1280]{1,0:T(8,128)(2,1)S(1)} %copy-done.14), kind=kOutput, calls=%fused_computation.8 | convolution fusion | flops 4031774720 | bytes 13631488 | tf_op jit(solution)/shard_map/dot_general | solution.py:22
  286.3 0.1 dynamic-slice_convert_fusion.1
  286.5 2.3 collective-permute-done.22
  288.8 0.2 convert_add_fusion.1
  289.0 0.8 dynamic-slice_convert_fusion.3
  289.8 1.5 collective-permute-start.23
  291.4 1.9 collective-permute-start.18
  293.3 2.6 collective-permute-start.19
  297.1 25.5 %collective-permute-done.23 = bf16[512,384]{1,0:T(8,128)(2,1)S(1)} collective-permute-done((bf16[512,384]{1,0:T(8,128)(2,1)}, bf16[512,384]{1,0:T(8,128)(2,1)S(1)}, u32[]{:S(2)}, u32[]{:S(2)}) %collective-permute-start.23) | collective-permute-done | bytes 393248 | tf_op jit(solution)/shard_map/ppermute | solution.py:193
  322.7 0.2 constant_dynamic-slice_fusion
  322.9 1.9 collective-permute-start.24
  324.9 5.2 %collective-permute-start.25 = (bf16[512,192]{1,0:T(8,128)(2,1)S(1)}, bf16[512,192]{1,0:T(8,128)(2,1)S(1)}, u32[]{:S(2)}, u32[]{:S(2)}) collective-permute-start(bf16[512,192]{1,0:T(8,128)(2,1)S(1)} %get-tuple-element.39), channel_id=1, source_target_pairs={{0,4},{1,20},{2,12},{3,28},{4,0},{5,16},{6,8},{7,24},{8,5},{9,21},... | collective-permute-start | bytes 589832 | tf_op jit(solution)/shard_map/ppermute | solution.py:193
  330.1 1.1 broadcast_select_fusion.3
  331.2 12.8 %collective-permute-done.24 = bf16[512,192]{1,0:T(8,128)(2,1)S(1)} collective-permute-done((bf16[512,192]{1,0:T(8,128)(2,1)S(1)}, bf16[512,192]{1,0:T(8,128)(2,1)S(1)}, u32[]{:S(2)}, u32[]{:S(2)}) %collective-permute-start.24) | collective-permute-done | bytes 196640 | tf_op jit(solution)/shard_map/ppermute | solution.py:193
  344.0 2.8 collective-permute-done.25
  346.9 0.3 convert_divide_fusion
  347.1 2.2 copy.13
  (50 shorter events, 0.5 us)
Async XLA Ops:
  3.7 37.4 %collective-permute-start.14 = (bf16[1024,1536]{1,0:T(8,128)(2,1)}, bf16[1024,1536]{1,0:T(8,128)(2,1)S(1)}, u32[]{:S(2)}, u32[]{:S(2)}) collective-permute-start(bf16[1024,1536]{1,0:T(8,128)(2,1)} %constant_dynamic-slice_fusion.5), channel_id=1, source_target_pairs={{0,2},{4,6},{9,11},{13,15},{18,16},{22,20},{27,25},{31,29}} | collective-permute-start | bytes 9437192 | tf_op jit(solution)/shard_map/ppermute | solution.py:193
  8.4 24.4 %collective-permute-start = (bf16[176,1536]{1,0:T(8,128)(2,1)}, bf16[176,1536]{1,0:T(8,128)(2,1)}, u32[]{:S(2)}, u32[]{:S(2)}) collective-permute-start(bf16[176,1536]{1,0:T(8,128)(2,1)} %get-tuple-element.17), channel_id=1, source_target_pairs={{0,4},{4,0},{8,12},{12,8},{16,20},{20,16},{24,28},{28,24},{1,5},{5... | collective-permute-start | bytes 1622024 | tf_op jit(solution)/shard_map/ppermute | solution.py:193
  10.5 23.1 %collective-permute-start.1 = (bf16[176,1536]{1,0:T(8,128)(2,1)}, bf16[176,1536]{1,0:T(8,128)(2,1)}, u32[]{:S(2)}, u32[]{:S(2)}) collective-permute-start(bf16[176,1536]{1,0:T(8,128)(2,1)} %get-tuple-element.17), channel_id=1, source_target_pairs={{0,24},{4,28},{8,0},{12,4},{16,8},{20,12},{24,16},{28,20},{1,25},{... | collective-permute-start | bytes 1622024 | tf_op jit(solution)/shard_map/ppermute | solution.py:193
  14.2 23.2 %collective-permute-start.2 = (bf16[176,1536]{1,0:T(8,128)(2,1)}, bf16[176,1536]{1,0:T(8,128)(2,1)}, u32[]{:S(2)}, u32[]{:S(2)}) collective-permute-start(bf16[176,1536]{1,0:T(8,128)(2,1)} %get-tuple-element.17), channel_id=1, source_target_pairs={{0,8},{4,12},{8,16},{12,20},{16,24},{20,28},{24,0},{28,4},{1,9},{5... | collective-permute-start | bytes 1622024 | tf_op jit(solution)/shard_map/ppermute | solution.py:193
  14.3 47.7 %collective-permute-start.7 = (bf16[176,1536]{1,0:T(8,128)(2,1)}, bf16[176,1536]{1,0:T(8,128)(2,1)}, u32[]{:S(2)}, u32[]{:S(2)}) collective-permute-start(bf16[176,1536]{1,0:T(8,128)(2,1)} %get-tuple-element.17), channel_id=1, source_target_pairs={{0,16},{4,20},{8,24},{12,28},{16,0},{20,4},{24,8},{28,12},{1,17},{... | collective-permute-start | bytes 1622024 | tf_op jit(solution)/shard_map/ppermute | solution.py:193
  32.9 67.2 %collective-permute-start.20 = (bf16[512,1536]{1,0:T(8,128)(2,1)}, bf16[512,1536]{1,0:T(8,128)(2,1)S(1)}, u32[]{:S(2)}, u32[]{:S(2)}) collective-permute-start(bf16[512,1536]{1,0:T(8,128)(2,1)} %constant_dynamic-slice_fusion.2), channel_id=1, source_target_pairs={{0,2},{4,6},{9,11},{13,15},{18,16},{22,20},{27,25},{31,29}} | collective-permute-start | bytes 4718600 | tf_op jit(solution)/shard_map/ppermute | solution.py:193
  37.4 24.8 %collective-permute-start.11 = (bf16[176,1536]{1,0:T(8,128)(2,1)}, bf16[176,1536]{1,0:T(8,128)(2,1)S(1)}, u32[]{:S(2)}, u32[]{:S(2)}) collective-permute-start(bf16[176,1536]{1,0:T(8,128)(2,1)} %collective-permute-done.refs_1_), channel_id=1, source_target_pairs={{0,1},{1,0},{2,3},{3,2},{4,5},{5,4},{6,7},{7,6},{8,9},{9,8},{10,11... | collective-permute-start | bytes 1622024 | tf_op jit(solution)/shard_map/ppermute | solution.py:193
  41.1 22.4 %collective-permute-start.12 = (bf16[176,1536]{1,0:T(8,128)(2,1)}, bf16[176,1536]{1,0:T(8,128)(2,1)S(1)}, u32[]{:S(2)}, u32[]{:S(2)}) collective-permute-start(bf16[176,1536]{1,0:T(8,128)(2,1)} %collective-permute-done.1.refs_3_), channel_id=1, source_target_pairs={{0,1},{1,0},{2,3},{3,2},{4,5},{5,4},{6,7},{7,6},{8,9},{9,8},{10,11... | collective-permute-start | bytes 1622024 | tf_op jit(solution)/shard_map/ppermute | solution.py:193
  41.1 22.6 %collective-permute-start.13 = (bf16[176,1536]{1,0:T(8,128)(2,1)}, bf16[176,1536]{1,0:T(8,128)(2,1)S(1)}, u32[]{:S(2)}, u32[]{:S(2)}) collective-permute-start(bf16[176,1536]{1,0:T(8,128)(2,1)} %collective-permute-done.2.refs_5_), channel_id=1, source_target_pairs={{0,1},{1,0},{2,3},{3,2},{4,5},{5,4},{6,7},{7,6},{8,9},{9,8},{10,11... | collective-permute-start | bytes 1622024 | tf_op jit(solution)/shard_map/ppermute | solution.py:193
  62.0 21.5 %collective-permute-start.3 = (bf16[176,1536]{1,0:T(8,128)(2,1)}, bf16[176,1536]{1,0:T(8,128)(2,1)S(1)}, u32[]{:S(2)}, u32[]{:S(2)}) collective-permute-start(bf16[176,1536]{1,0:T(8,128)(2,1)} %collective-permute-done.1.refs_3_), channel_id=1, source_target_pairs={{0,4},{4,0},{8,12},{12,8},{16,20},{20,16},{24,28},{28,24},{1,5},{5... | collective-permute-start | bytes 1622024 | tf_op jit(solution)/shard_map/ppermute | solution.py:193
  62.3 1.5 copy-start.8
  62.3 25.7 %collective-permute-start.5 = (bf16[176,1536]{1,0:T(8,128)(2,1)}, bf16[176,1536]{1,0:T(8,128)(2,1)S(1)}, u32[]{:S(2)}, u32[]{:S(2)}) collective-permute-start(bf16[176,1536]{1,0:T(8,128)(2,1)} %collective-permute-done.2.refs_5_), channel_id=1, source_target_pairs={{0,4},{4,0},{8,12},{12,8},{16,20},{20,16},{24,28},{28,24},{1,5},{5... | collective-permute-start | bytes 1622024 | tf_op jit(solution)/shard_map/ppermute | solution.py:193
  63.5 0.8 copy-start.9
  63.5 36.1 %collective-permute-start.9 = (bf16[176,1536]{1,0:T(8,128)(2,1)}, bf16[176,1536]{1,0:T(8,128)(2,1)S(1)}, u32[]{:S(2)}, u32[]{:S(2)}) collective-permute-start(bf16[176,1536]{1,0:T(8,128)(2,1)} %collective-permute-done.7.refs_4_), channel_id=1, source_target_pairs={{0,4},{4,0},{8,12},{12,8},{16,20},{20,16},{24,28},{28,24},{1,5},{5... | collective-permute-start | bytes 1622024 | tf_op jit(solution)/shard_map/ppermute | solution.py:193
  64.3 1.3 copy-start.12
  64.3 60.2 %collective-permute-start.15 = (bf16[1024,1536]{1,0:T(8,128)(2,1)S(1)}, bf16[1024,1536]{1,0:T(8,128)(2,1)}, u32[]{:S(2)}, u32[]{:S(2)}) collective-permute-start(bf16[1024,1536]{1,0:T(8,128)(2,1)S(1)} %broadcast_select_fusion), channel_id=1, source_target_pairs={{0,1},{2,3},{4,5},{6,7},{9,8},{11,10},{13,12},{15,14},{18,19},{16,... | collective-permute-start | bytes 9437192 | tf_op jit(solution)/shard_map/ppermute | solution.py:193
  83.5 21.1 %copy-start.4 = (bf16[176,1536]{1,0:T(8,128)(2,1)}, bf16[176,1536]{1,0:T(8,128)(2,1)S(1)}, u32[]{:S(2)}) copy-start(bf16[176,1536]{1,0:T(8,128)(2,1)S(1)} %collective-permute-done.3.refs_0_) | copy-start | bytes 1622020
  83.5 18.4 %collective-permute-start.8 = (bf16[176,1536]{1,0:T(8,128)(2,1)}, bf16[176,1536]{1,0:T(8,128)(2,1)S(1)}, u32[]{:S(2)}, u32[]{:S(2)}) collective-permute-start(bf16[176,1536]{1,0:T(8,128)(2,1)} %collective-permute-done.7.refs_4_), channel_id=1, source_target_pairs={{0,1},{1,0},{2,3},{3,2},{4,5},{5,4},{6,7},{7,6},{8,9},{9,8},{10,11... | collective-permute-start | bytes 1622024 | tf_op jit(solution)/shard_map/ppermute | solution.py:193
  88.0 16.6 %copy-start.5 = (bf16[176,1536]{1,0:T(8,128)(2,1)}, bf16[176,1536]{1,0:T(8,128)(2,1)S(1)}, u32[]{:S(2)}) copy-start(bf16[176,1536]{1,0:T(8,128)(2,1)S(1)} %collective-permute-done.5.refs_2_) | copy-start | bytes 1622020
  88.0 15.4 %collective-permute-start.4 = (bf16[176,1536]{1,0:T(8,128)(2,1)S(1)}, bf16[176,1536]{1,0:T(8,128)(2,1)S(1)}, u32[]{:S(2)}, u32[]{:S(2)}) collective-permute-start(bf16[176,1536]{1,0:T(8,128)(2,1)S(1)} %collective-permute-done.3.refs_0_), channel_id=1, source_target_pairs={{0,1},{1,0},{2,3},{3,2},{4,5},{5,4},{6,7},{7,6},{8,9},{9,8},{10,11... | collective-permute-start | bytes 1622024 | tf_op jit(solution)/shard_map/ppermute | solution.py:193
  99.6 5.0 %copy-start.6 = (bf16[176,1536]{1,0:T(8,128)(2,1)}, bf16[176,1536]{1,0:T(8,128)(2,1)S(1)}, u32[]{:S(2)}) copy-start(bf16[176,1536]{1,0:T(8,128)(2,1)S(1)} %collective-permute-done.9.refs_6_) | copy-start | bytes 1622020
  99.6 3.9 %collective-permute-start.6 = (bf16[176,1536]{1,0:T(8,128)(2,1)S(1)}, bf16[176,1536]{1,0:T(8,128)(2,1)S(1)}, u32[]{:S(2)}, u32[]{:S(2)}) collective-permute-start(bf16[176,1536]{1,0:T(8,128)(2,1)S(1)} %collective-permute-done.5.refs_2_), channel_id=1, source_target_pairs={{0,1},{1,0},{2,3},{3,2},{4,5},{5,4},{6,7},{7,6},{8,9},{9,8},{10,11... | collective-permute-start | bytes 1622024 | tf_op jit(solution)/shard_map/ppermute | solution.py:193
  100.1 3.4 collective-permute-start.10
  102.0 1.5 copy-start.7
  102.0 120.8 %collective-permute-start.21 = (bf16[512,1536]{1,0:T(8,128)(2,1)S(1)}, bf16[512,1536]{1,0:T(8,128)(2,1)}, u32[]{:S(2)}, u32[]{:S(2)}) collective-permute-start(bf16[512,1536]{1,0:T(8,128)(2,1)S(1)} %broadcast_select_fusion.1), channel_id=1, source_target_pairs={{0,1},{2,3},{4,5},{6,7},{9,8},{11,10},{13,12},{15,14},{18,19},{16,... | collective-permute-start | bytes 4718600 | tf_op jit(solution)/shard_map/ppermute | solution.py:193
  103.5 0.8 copy-start.10
  103.5 1.0 copy-start.11
  103.5 1.1 copy-start.13
  218.9 2.6 copy-start
  221.7 10.8 %collective-permute-start.16 = (bf16[1024,768]{1,0:T(8,128)(2,1)S(1)}, bf16[1024,768]{1,0:T(8,128)(2,1)}, u32[]{:S(2)}, u32[]{:S(2)}) collective-permute-start(bf16[1024,768]{1,0:T(8,128)(2,1)S(1)} %dynamic-slice_convert_fusion), channel_id=1, source_target_pairs={{0,1},{1,0},{2,3},{3,2},{4,5},{5,4},{6,7},{7,6},{8,9},{9,8},{10,11... | collective-permute-start | bytes 4718600 | tf_op jit(solution)/shard_map/ppermute | solution.py:193
  222.8 9.7 %copy-start.1 = (f32[1024,1536]{1,0:T(8,128)S(1)}, f32[1024,1536]{1,0:T(8,128)}, u32[]{:S(2)}) copy-start(f32[1024,1536]{1,0:T(8,128)} %copy-done) | copy-start | bytes 18874372
  234.4 21.9 %collective-permute-start.17 = (bf16[1024,384]{1,0:T(8,128)(2,1)S(1)}, bf16[1024,384]{1,0:T(8,128)(2,1)S(1)}, u32[]{:S(2)}, u32[]{:S(2)}) collective-permute-start(bf16[1024,384]{1,0:T(8,128)(2,1)S(1)} %dynamic-slice_convert_fusion.2), channel_id=1, source_target_pairs={{0,2},{1,3},{2,0},{3,1},{4,6},{5,7},{6,4},{7,5},{8,10},{9,11},{10,... | collective-permute-start | bytes 2359304 | tf_op jit(solution)/shard_map/ppermute | solution.py:193
  257.9 21.4 %copy-start.14 = (bf16[512,1280]{1,0:T(8,128)(2,1)S(1)}, bf16[512,1280]{1,0:T(8,128)(2,1)}, u32[]{:S(2)}) copy-start(bf16[512,1280]{1,0:T(8,128)(2,1)} %shard_map.78.refs_0_) | copy-start | bytes 3932164
  286.3 5.1 %copy-start.3 = (bf16[1024,192]{1,0:T(8,128)(2,1)S(1)}, bf16[1024,192]{1,0:T(8,128)(2,1)}, u32[]{:S(2)}) copy-start(bf16[1024,192]{1,0:T(8,128)(2,1)} %get-tuple-element.36.refs_1_) | copy-start | bytes 1179652
  286.3 7.0 %copy-start.2 = (bf16[1024,192]{1,0:T(8,128)(2,1)S(1)}, bf16[1024,192]{1,0:T(8,128)(2,1)}, u32[]{:S(2)}) copy-start(bf16[1024,192]{1,0:T(8,128)(2,1)} %get-tuple-element.35.refs_2_) | copy-start | bytes 1179652
  286.4 2.4 collective-permute-start.22
  289.8 32.8 %collective-permute-start.23 = (bf16[512,384]{1,0:T(8,128)(2,1)}, bf16[512,384]{1,0:T(8,128)(2,1)S(1)}, u32[]{:S(2)}, u32[]{:S(2)}) collective-permute-start(bf16[512,384]{1,0:T(8,128)(2,1)} %dynamic-slice_convert_fusion.3), channel_id=1, source_target_pairs={{0,2},{1,3},{2,0},{3,1},{4,6},{5,7},{6,4},{7,5},{8,10},{9,11},{10,... | collective-permute-start | bytes 1179656 | tf_op jit(solution)/shard_map/ppermute | solution.py:193
  291.4 38.7 %collective-permute-start.18 = (bf16[1024,192]{1,0:T(8,128)(2,1)S(1)}, bf16[1024,192]{1,0:T(8,128)(2,1)S(1)}, u32[]{:S(2)}, u32[]{:S(2)}) collective-permute-start(bf16[1024,192]{1,0:T(8,128)(2,1)S(1)} %copy-done.3), channel_id=1, source_target_pairs={{0,0},{1,16},{2,8},{3,24},{4,4},{5,20},{6,12},{7,28},{8,1},{9,17},... | collective-permute-start | bytes 1179656 | tf_op jit(solution)/shard_map/ppermute | solution.py:193
  293.3 36.8 %collective-permute-start.19 = (bf16[1024,192]{1,0:T(8,128)(2,1)S(1)}, bf16[1024,192]{1,0:T(8,128)(2,1)}, u32[]{:S(2)}, u32[]{:S(2)}) collective-permute-start(bf16[1024,192]{1,0:T(8,128)(2,1)S(1)} %copy-done.2), channel_id=1, source_target_pairs={{0,4},{1,20},{2,12},{3,28},{4,0},{5,16},{6,8},{7,24},{8,5},{9,21},... | collective-permute-start | bytes 1179656 | tf_op jit(solution)/shard_map/ppermute | solution.py:193
  322.9 21.1 %collective-permute-start.24 = (bf16[512,192]{1,0:T(8,128)(2,1)S(1)}, bf16[512,192]{1,0:T(8,128)(2,1)S(1)}, u32[]{:S(2)}, u32[]{:S(2)}) collective-permute-start(bf16[512,192]{1,0:T(8,128)(2,1)S(1)} %get-tuple-element.40), channel_id=1, source_target_pairs={{0,0},{1,16},{2,8},{3,24},{4,4},{5,20},{6,12},{7,28},{8,1},{9,17},... | collective-permute-start | bytes 589832 | tf_op jit(solution)/shard_map/ppermute | solution.py:193
  324.9 21.9 %collective-permute-start.25 = (bf16[512,192]{1,0:T(8,128)(2,1)S(1)}, bf16[512,192]{1,0:T(8,128)(2,1)S(1)}, u32[]{:S(2)}, u32[]{:S(2)}) collective-permute-start(bf16[512,192]{1,0:T(8,128)(2,1)S(1)} %get-tuple-element.39), channel_id=1, source_target_pairs={{0,4},{1,20},{2,12},{3,28},{4,0},{5,16},{6,8},{7,24},{8,5},{9,21},... | collective-permute-start | bytes 589832 | tf_op jit(solution)/shard_map/ppermute | solution.py:193

commit v2 on v1

--- a/solution.py
+++ b/solution.py
@@ -108,12 +108,11 @@
     out_ref[...] = dot(stack[...], col_ref[...], NT).astype(BF16)
 
 
-def project(items, rows_each, col, groups, index, before=(), after=()):
+def project(items, rows_each, col, groups, index, before=()):
     size_m, size, total = col.shape[1], col.shape[0], sum(rows_each)
     tile = tile_of(size, 512)
-    hbm, waits = pl.BlockSpec(memory_space=pl.ANY), (*before, *after)
     return pl.pallas_call(
-        functools.partial(project_kernel, tuple(rows_each), len(waits)),
+        functools.partial(project_kernel, tuple(rows_each), len(before)),
         out_shape=[
             jax.ShapeDtypeStruct((groups * total, size), BF16),
             jax.ShapeDtypeStruct((groups * total, size_m), BF16),
@@ -122,7 +121,7 @@
         grid=(size // tile,),
         in_specs=[pl.BlockSpec(x.shape, lambda b: (0, 0), pipeline_mode=pl.Buffered(1)) for x in items]
         + [pl.BlockSpec((tile, size_m), lambda b: (b, 0))]
-        + [hbm] * len(waits),
+        + [pl.BlockSpec(memory_space=pl.ANY)] * len(before),
         out_specs=[
             pl.BlockSpec((total, tile), lambda b: (index, b)),
             pl.BlockSpec((total, size_m), lambda b: (index, 0), pipeline_mode=pl.Buffered(1)),
@@ -132,61 +131,68 @@
         input_output_aliases={len(items) + 1 + n: n for n in range(len(before))},
         compiler_params=pltpu.CompilerParams(vmem_limit_bytes=VMEM_LIMIT),
         cost_estimate=cost(2 * (total + 640) * size_m * size, 2 * size_m * size),
-    )(*items, col, *waits)
-
-
-def pair_kernel(sub, first, waits, weight_ref, kt_ref, lrp_ref, lrq_ref, *refs):
-    out_ref, sides, totals = refs[waits:]
-    occ = sides.shape[2]
-    count = sides.shape[0] // 2
-    for n in range(2 * count):
-        sides[n] = lrq_ref[:, n * occ : (n + 1) * occ]
-    totals[...] = jnp.zeros_like(totals)
-
-    def columns(t, carry):
-        at = pl.ds(pl.multiple_of(t * sub, sub), sub)
-        kern = kt_ref[:, at]
-        for n in range(count):
-            left_t = lrp_ref[2 * n * occ : (2 * n + 1) * occ, at]
-            right_t = lrp_ref[(2 * n + 1) * occ : (2 * n + 2) * occ, at]
-            had_t = kern * dot(sides[2 * n + 1], left_t).astype(BF16)
-            had = kern * dot(sides[2 * n], right_t).astype(BF16)
-            totals[2 * n] += dot(had_t, right_t, NT)
-            totals[2 * n + 1] += dot(had, left_t, NT)
-        return carry
-
-    lax.fori_loop(0, kt_ref.shape[1] // sub, columns, 0)
-    for n in range(2 * count):
-        scale = 2.0 * weight_ref[(first + pl.program_id(0)) * count + n // 2]
-        out_ref[:, n * occ : (n + 1) * occ] = (totals[n] * scale).astype(BF16)
-
-
-def pair_gradients(weights, kernel_t, lrp, lrq, row_at, pairs=None, after=()):
-    size_b, rows, count = kernel_t.shape[1], lrq.shape[0], weights.shape[0] // 2
-    first, last = pairs or (0, count)
+    )(*items, col, *before)
+
+
+def pair_kernel(sub, first, weight_ref, kt_ref, lrp_ref, lrq_ref, out_ref, sides):
+    item, occ = first + pl.program_id(0), sides.shape[2]
+    size_b = kt_ref.shape[1]
+
+    for odd in (0, 1):
+
+        @pl.when(item % 2 == odd)
+        def _():
+            for side in (0, 1):
+                at = (2 * odd + side) * occ
+                sides[side] = lrq_ref[:, at : at + occ]
+
+    total_l = jnp.zeros(sides.shape[1:], F32)
+    total_r = jnp.zeros(sides.shape[1:], F32)
+    for at in range(0, size_b, sub):
+        left_t = lrp_ref[:occ, at : at + sub]
+        right_t = lrp_ref[occ:, at : at + sub]
+        kern = kt_ref[:, at : at + sub]
+        had_t = kern * dot(sides[1], left_t).astype(BF16)
+        had = kern * dot(sides[0], right_t).astype(BF16)
+        total_l += dot(had_t, right_t, NT)
+        total_r += dot(had, left_t, NT)
+    scale = 2.0 * weight_ref[item]
+    sides[0] = (total_l * scale).astype(BF16)
+    sides[1] = (total_r * scale).astype(BF16)
+
+    for odd in (0, 1):
+
+        @pl.when(item % 2 == odd)
+        def _():
+            for side in (0, 1):
+                at = (2 * odd + side) * occ
+                out_ref[:, at : at + occ] = sides[side]
+
+
+def pair_gradients(weights, kernel_t, lrp, lrq, row_at, items=None):
+    size_b, rows, count = kernel_t.shape[1], lrq.shape[0], weights.shape[0]
+    first, last = items or (0, count)
     width = lrp.shape[0] // count
-    occ = width // 4
     at, sub = row_at // rows, tile_of(size_b, 512)
     return pl.pallas_call(
-        functools.partial(pair_kernel, sub, first, len(after)),
+        functools.partial(pair_kernel, sub, first),
         out_shape=jax.ShapeDtypeStruct((rows, (last - first) * width), BF16),
         grid_spec=pltpu.PrefetchScalarGridSpec(
             num_scalar_prefetch=1,
             grid=(last - first,),
             in_specs=[
-                pl.BlockSpec((rows, size_b), lambda p, s: (at, 0), pipeline_mode=pl.Buffered(1)),
-                pl.BlockSpec((width, size_b), lambda p, s: (first + p, 0)),
-                pl.BlockSpec((rows, width), lambda p, s: (0, first + p)),
-            ]
-            + [pl.BlockSpec(memory_space=pl.ANY)] * len(after),
-            out_specs=pl.BlockSpec((rows, width), lambda p, s: (0, p)),
-            scratch_shapes=[pltpu.VMEM((4, rows, occ), BF16), pltpu.VMEM((4, rows, occ), F32)],
+                pl.BlockSpec((rows, size_b), lambda w, s: (at, 0), pipeline_mode=pl.Buffered(1)),
+                pl.BlockSpec((width, size_b), lambda w, s: (first + w, 0)),
+                pl.BlockSpec((rows, 2 * width), lambda w, s: (0, (first + w) // 2)),
+            ],
+            out_specs=pl.BlockSpec((rows, 2 * width), lambda w, s: (0, w // 2)),
+            scratch_shapes=[pltpu.VMEM((2, rows, width // 2), BF16)],
         ),
         compiler_params=pltpu.CompilerParams(vmem_limit_bytes=VMEM_LIMIT),
         cost_estimate=cost(
-            2 * 4 * (last - first) * 2 * 256 * rows * size_b, 2 * (last - first) * (rows + width) * size_b
+            2 * 4 * (last - first) * 256 * rows * size_b, 2 * (last - first) * (rows + width) * size_b
         ),
-    )(weights, kernel_t, lrp, lrq, *after)
+    )(weights, kernel_t, lrp, lrq)
 
 
 def send(x, axes, pairs):
@@ -234,17 +240,20 @@
         give = lax.dynamic_slice_in_dim(part, (1 - at) * size, size, axis).astype(BF16)
         return give, lax.dynamic_slice_in_dim(part, at * size, size, axis)
 
+    tie = lax.optimization_barrier
     chunks = [(0, 2 * size_a // 3), (2 * size_a // 3, size_a // 3)]
     own, half = packed(bra, ket, walker_group, group_occupied, core.reshape(1), walker_weight)
     cols_q = [columns_q(*chunk) for chunk in chunks]
     z1, z3, x0 = along(half, 1), along(half, 3), across(half)
     z2 = along(half, 2)
     kernel_t = turned(kernel)
-    x0, z1, z3, kernel_t = lax.optimization_barrier((x0, z1, z3, kernel_t))
-    x1, x3, x2 = across(z1), across(z3), across(z2)
+    x0, z1, z3, kernel_t = tie((x0, z1, z3, kernel_t))
+    x1, x3 = across(z1), across(z3)
     near_four = [own] + [h for part in (x0, z1, z3) for h in (part, other(part))]
-    far_four = [h for part in (x1, x3, z2, x2) for h in (part, other(part))]
-    first = project(near_four, [width] + [occ] * 6, collocation, 2, 0)
+    lrp, stack, weight_rows = project(near_four, [width] + [occ] * 6, collocation, 2, 0)
+    z2, weight_rows = tie((z2, weight_rows))
+    far_four = [h for part in (x1, x3, z2, across(z2)) for h in (part, other(part))]
+    first = (lrp, stack, weight_rows)
     lrp, stack, weight_rows = project(far_four, [occ] * 8, collocation, 2, 1, first)
     weights = jnp.concatenate([weight_rows[:4, 0], weight_rows[8:12, 0]])
 
@@ -254,8 +263,9 @@
     half_m, quarter, eighth = size_m // 2, size_m // 4, size_m // 8
     swap_y = [(i, i ^ 2) for i in range(npt)]
 
-    def to_place(part):
+    def to_place(part, *later):
         pieces = [lax.dynamic_slice_in_dim(part, (x ^ t) * eighth, eighth, 1) for t in (0, 1)]
+        pieces = tie((*pieces, *later))
         came = []
         for t in (0, 1):
             pairs = []
@@ -273,10 +283,13 @@
     grads = pair_gradients(weights, kernel_t, lrp, rows_q(0), chunks[0][0])
     lrq = rows_q(1)
     give, keep = over_cores(grads)
+    give, lrq = tie((give, lrq))
     got = send(give, "pt", swap_y)
-    early = pair_gradients(weights, kernel_t, lrp, lrq, chunks[1][0], (0, 2), (give[:16, :128],))
-    pieces, came_0 = to_place((keep + got.astype(F32)).astype(BF16))
-    late = pair_gradients(weights, kernel_t, lrp, lrq, chunks[1][0], (2, 4), (early, *pieces))
+    early = pair_gradients(weights, kernel_t, lrp, lrq, chunks[1][0], (0, 4))
+    early, got = tie((early, got))
+    pieces, came_0 = to_place((keep + got.astype(F32)).astype(BF16), lrq)
+    late = pair_gradients(weights, kernel_t, lrp, pieces[2], chunks[1][0], (4, 8))
+    late, *came_0 = tie((late, *came_0))
     give, keep = over_cores(jnp.concatenate([early, late], axis=1))
     _, came_1 = to_place((keep + send(give, "pt", swap_y).astype(F32)).astype(BF16))
 

time: 350 us -> 318 us (0.909); the launches traced: 349 us -> 312 us
  waiting for transfers between devices: 75.5 us -> 40.8 us
  Pallas kernels: 165 us -> 156 us
  starting transfers between devices: 37.7 us -> 46.2 us
  local copies, waits for them, and re-layouts: 16.2 us -> 12.4 us
    ppermute x26, waiting for transfers between devices: 75.5 us -> 40.8 us  [send(): return lax.ppermute(x, axes, pairs)]
    ppermute x26, starting transfers between devices: 37.7 us -> 46.2 us  [send(): return lax.ppermute(x, axes, pairs)]
    pallas_call x5, Pallas kernels: 147 us -> 139 us  [the longest x3 103 us: pair_gradients(): pl.pallas_call(functools.partial(pair_kernel, sub, first), out_shape=jax....]
  transfers between devices with their start and end apart: 26 -> 26, of which waited for: 8 -> 8; matrix products, arithmetic and copies ran while one was open for 13% -> 15% of each run, Pallas kernels for 41% -> 50%
where the time goes in v2:
time: 318 us; the launch traced here: 312 us
  Pallas kernels  156 us (49%)
  starting transfers between devices  46.2 us (15%)
  matrix products  41.6 us (13%)
  waiting for transfers between devices  40.8 us (13%)
  local copies, waits for them, and re-layouts  12.4 us (4%)
  other arithmetic  11.9 us (4%)
  between operations  3.26 us (1%)
    pallas_call x3, Pallas kernels, pair_gradients(): pl.pallas_call(functools.partial(pair_kernel, sub, first), out_shape=jax....  103 us
    ppermute x26, starting transfers between devices, send(): return lax.ppermute(x, axes, pairs)  46.2 us
    dot_general x4, matrix products, dot(): return lax.dot_general(a, b, dims, preferred_element_type=F32)  41.6 us
    ppermute x26, waiting for transfers between devices, send(): return lax.ppermute(x, axes, pairs)  40.8 us
    pallas_call x2, Pallas kernels, project(): pl.pallas_call(functools.partial(project_kernel, tuple(rows_each), len(be...  35.8 us
    pallas_call x1, Pallas kernels, turned(): pl.pallas_call(turn_kernel, out_shape=jax.ShapeDtypeStruct((cols, rows),...  14.8 us
    select_n x2, other arithmetic, columns_q(): near = jnp.where(me_p == z, rows, far)  7.09 us
    dynamic_slice x2, local copies, waits for them, and re-layouts, columns_q(): rows = lax.dynamic_slice_in_dim(collocation, x * size_a + begin, chunk, 0)  6.38 us
  transfers between devices with their start and end apart: 26, of which 8 were waited for; matrix products, arithmetic and copies ran while one was open for 15% of the time, Pallas kernels for 50%

profile of v2, /device:TPU:1, one launch (start us, length us, event | category | flops | bytes accessed | tf_op | source)
XLA Modules:
  0.0 312.3 jit_solution(16550302248298096214)
XLA Ops:
  0.0 3.7 %constant_dynamic-slice_fusion.5 = bf16[1024,1536]{1,0:T(8,128)(2,1)} fusion(bf16[3072,1536]{1,0:T(8,128)(2,1)} %refs_8_.1, s32[]{:T(128)S(6)} %select_n.117), kind=kLoop, calls=%fused_computation.30 | loop fusion | bytes 6291460 | tf_op jit(solution)/shard_map/dynamic_slice | solution.py:233
  3.7 0.9 collective-permute-start.14
  5.9 2.5 shard_map.73
  8.4 2.0 collective-permute-start
  10.5 3.8 %collective-permute-start.1 = (bf16[176,1536]{1,0:T(8,128)(2,1)}, bf16[176,1536]{1,0:T(8,128)(2,1)}, u32[]{:S(2)}, u32[]{:S(2)}) collective-permute-start(bf16[176,1536]{1,0:T(8,128)(2,1)} %get-tuple-element.31), channel_id=1, source_target_pairs={{0,24},{4,28},{8,0},{12,4},{16,8},{20,12},{24,16},{28,20},{1,25},{... | collective-permute-start | bytes 1622024 | tf_op jit(solution)/shard_map/ppermute | solution.py:199
  14.3 1.2 collective-permute-start.7
  15.4 14.8 %shard_map.74.kt_ref = bf16[1536,3072]{1,0:T(8,128)(2,1)} custom-call(bf16[3072,1536]{1,0:T(8,128)(2,1)} %in_ref.1), custom_call_target="tpu_custom_call" | custom-call | bytes 47185920 | tf_op jit(solution)/shard_map/pallas_call | solution.py:36
  30.2 2.7 constant_dynamic-slice_fusion.4
  32.9 1.8 collective-permute-start.17
  34.6 2.8 collective-permute-done.2.refs_5_
  37.4 3.7 %collective-permute-start.10 = (bf16[176,1536]{1,0:T(8,128)(2,1)}, bf16[176,1536]{1,0:T(8,128)(2,1)S(1)}, u32[]{:S(2)}, u32[]{:S(2)}) collective-permute-start(bf16[176,1536]{1,0:T(8,128)(2,1)} %collective-permute-done.2.refs_5_), channel_id=1, source_target_pairs={{0,1},{1,0},{2,3},{3,2},{4,5},{5,4},{6,7},{7,6},{8,9},{9,8},{10,11... | collective-permute-start | bytes 1622024 | tf_op jit(solution)/shard_map/ppermute | solution.py:199
  41.1 1.6 copy-done.2
  42.7 2.6 collective-permute-start.9
  45.4 3.7 %broadcast_select_fusion = bf16[1024,1536]{1,0:T(8,128)(2,1)S(1)} fusion(bf16[1024,1536]{1,0:T(8,128)(2,1)} %copy-done.2, pred[]{:T(512)S(6)} %eq.23, bf16[3072,1536]{1,0:T(8,128)(2,1)} %refs_8_.1, s32[]{:T(128)S(6)} %select_n.117), kind=kLoop, calls=%fused_computation.5 | loop fusion | flops 1572864 | bytes 9437189 | tf_op jit(solution)/shard_map/jit(_where)/select_n | solution.py:235
  49.1 1.3 collective-permute-start.3
  50.4 0.3 collective-permute-start.5
  50.6 1.3 collective-permute-start.15
  51.9 17.9 %shard_map.75 = (bf16[2560,3072]{1,0:T(8,128)(2,1)}, bf16[2560,1536]{1,0:T(8,128)(2,1)}, f32[16,128]{1,0:T(8,128)}) custom-call(bf16[336,1536]{1,0:T(8,128)(2,1)} %get-tuple-element.34.refs_0_, bf16[176,1536]{1,0:T(8,128)(2,1)} %collective-permute-done.refs_1_, bf16[176,1536]{1,0:T(8,128)(2,1)} %copy-done.7, ...), custom_call_target="tpu_custom_call" | custom-call | flops 18119393280 | bytes 9437184 | tf_op jit(solution)/shard_map/pallas_call | solution.py:114
  69.9 1.3 collective-permute-start.12
  71.2 3.0 collective-permute-start.11
  74.2 0.4 collective-permute-done.5.refs_2_
  74.6 0.3 collective-permute-start.4
  74.8 0.2 collective-permute-start.6
  75.1 10.0 %collective-permute-done.12.refs_6_ = bf16[176,1536]{1,0:T(8,128)(2,1)} collective-permute-done((bf16[176,1536]{1,0:T(8,128)(2,1)}, bf16[176,1536]{1,0:T(8,128)(2,1)}, u32[]{:S(2)}, u32[]{:S(2)}) %collective-permute-start.12) | collective-permute-done | bytes 540704 | tf_op jit(solution)/shard_map/ppermute | solution.py:199
  85.1 1.8 collective-permute-start.13
  86.8 3.4 %broadcast_select_fusion.1 = bf16[512,1536]{1,0:T(8,128)(2,1)} fusion(bf16[512,1536]{1,0:T(8,128)(2,1)} %collective-permute-done.17, pred[]{:T(512)S(6)} %eq.23, bf16[3072,1536]{1,0:T(8,128)(2,1)} %refs_8_.1, s32[]{:T(128)S(6)} %select_n.127), kind=kLoop, calls=%fused_computation.17 | loop fusion | flops 786432 | bytes 4718597 | tf_op jit(solution)/shard_map/jit(_where)/select_n | solution.py:235
  90.2 1.5 collective-permute-start.18
  91.8 0.8 copy-done.4
  92.5 0.2 copy-done.6
  92.7 0.2 copy-done.8
  92.9 17.9 %shard_map.76 = (bf16[2560,3072]{1,0:T(8,128)(2,1)}, bf16[2560,1536]{1,0:T(8,128)(2,1)}, f32[16,128]{1,0:T(8,128)}) custom-call(bf16[176,1536]{1,0:T(8,128)(2,1)} %collective-permute-done.3.refs_0_, bf16[176,1536]{1,0:T(8,128)(2,1)} %copy-done.4, ...), custom_call_target="tpu_custom_call", output_to_operand_aliasing={{0}: (9, {}), {1}: (10, {}), {2}: (11, {})} | custom-call | flops 18119393280 | bytes 9437184 | tf_op jit(solution)/shard_map/pallas_call | solution.py:114
  110.8 1.3 slice_reduce_fusion
  112.1 0.6 pad_maximum_fusion.weight_ref
  112.7 13.4 %convolution_convert_fusion.lrq_ref = bf16[1024,2560]{1,0:T(8,128)(2,1)} fusion(bf16[2560,1536]{1,0:T(8,128)(2,1)} %get-tuple-element.44, bf16[1024,1536]{1,0:T(8,128)(2,1)S(1)} %broadcast_select_fusion, bf16[1024,1536]{1,0:T(8,128)(2,1)} %collective-permute-done.15, pred[]{:T(512)S(6)} %eq.22), kind=kOutput, calls=%fused_computation | convolution fusion | flops 8057257984 | bytes 19398656 | tf_op jit(solution)/shard_map/dot_general | solution.py:22
  126.1 64.1 %shard_map.77 = bf16[1024,2560]{1,0:T(8,128)(2,1)} custom-call(f32[8]{0:T(128)} %pad_maximum_fusion.weight_ref, bf16[1536,3072]{1,0:T(8,128)(2,1)} %shard_map.74.kt_ref, bf16[2560,3072]{1,0:T(8,128)(2,1)} %get-tuple-element.43.lrp_ref, bf16[1024,2560]{1,0:T(8,128)(2,1)} %convolution_convert_fusion.lrq_ref), custom_call_target="tpu_custom_call" | custom-call | flops 51539607552 | bytes 66060288 | tf_op jit(solution)/shard_map/pallas_call | solution.py:177
  190.3 11.5 %fusion.9 = f32[1024,1536]{0,1:T(8,128)S(1)} fusion(bf16[1024,2560]{1,0:T(8,128)(2,1)} %shard_map.77, bf16[2560,1536]{1,0:T(8,128)(2,1)S(1)} %bitcast.15), kind=kOutput, calls=%fused_computation.37 | convolution fusion | flops 8053063680 | bytes 19398656 | tf_op jit(solution)/shard_map/dot_general | solution.py:22
  201.8 2.6 copy-done
  204.4 0.2 dynamic-slice_convert_fusion
  204.6 1.9 collective-permute-start.16
  206.5 9.7 %convolution_convert_fusion.1.lrq_ref = bf16[512,2560]{1,0:T(8,128)(2,1)} fusion(bf16[2560,1536]{1,0:T(8,128)(2,1)} %get-tuple-element.44, bf16[512,1536]{1,0:T(8,128)(2,1)} %broadcast_select_fusion.1, bf16[512,1536]{1,0:T(8,128)(2,1)} %collective-permute-done.18, pred[]{:T(512)S(6)} %eq.22), kind=kOutput, calls=%fused_computation.1 | convolution fusion | flops 4028628992 | bytes 13631489 | tf_op jit(solution)/shard_map/dot_general | solution.py:22
  216.2 0.5 convert_add_fusion
  216.7 0.1 dynamic-slice_convert_fusion.2
  216.9 2.7 collective-permute-start.19
  219.5 19.5 %shard_map.78 = bf16[512,1280]{1,0:T(8,128)(2,1)} custom-call(f32[8]{0:T(128)} %pad_maximum_fusion.weight_ref, bf16[1536,3072]{1,0:T(8,128)(2,1)} %shard_map.74.kt_ref, bf16[2560,3072]{1,0:T(8,128)(2,1)} %get-tuple-element.43.lrp_ref, bf16[512,2560]{1,0:T(8,128)(2,1)} %convolution_convert_fusion.1.lrq_ref), custom_call_target="tpu_custom_call" | custom-call | flops 12884901888 | bytes 20447232 | tf_op jit(solution)/shard_map/pallas_call | solution.py:177
  239.0 0.3 add_convert_fusion
  239.3 0.1 constant_dynamic-slice_fusion.2
  239.3 9.3 %collective-permute-start.20 = (bf16[1024,192]{0,1:T(8,128)(2,1)S(1)}, bf16[1024,192]{0,1:T(8,128)(2,1)S(1)}, u32[]{:S(2)}, u32[]{:S(2)}) collective-permute-start(bf16[1024,192]{0,1:T(8,128)(2,1)S(1)} %get-tuple-element.49), channel_id=1, source_target_pairs={{0,0},{1,16},{2,8},{3,24},{4,4},{5,20},{6,12},{7,28},{8,1},{9,17},... | collective-permute-start | bytes 1179656 | tf_op jit(solution)/shard_map/ppermute | solution.py:199
  248.6 0.3 collective-permute-start.21
  249.0 19.5 %shard_map.79 = bf16[512,1280]{1,0:T(8,128)(2,1)} custom-call(f32[8]{0:T(128)} %pad_maximum_fusion.weight_ref, bf16[1536,3072]{1,0:T(8,128)(2,1)} %shard_map.74.kt_ref, bf16[2560,3072]{1,0:T(8,128)(2,1)} %get-tuple-element.43.lrp_ref, bf16[512,2560]{1,0:T(8,128)(2,1)} %convolution_convert_fusion.1.lrq_ref), custom_call_target="tpu_custom_call" | custom-call | flops 12884901888 | bytes 20447232 | tf_op jit(solution)/shard_map/pallas_call | solution.py:177
  268.4 3.7 %collective-permute-done.21 = bf16[1024,192]{0,1:T(8,128)(2,1)S(1)} collective-permute-done((bf16[1024,192]{0,1:T(8,128)(2,1)S(1)}, bf16[1024,192]{0,1:T(8,128)(2,1)S(1)}, u32[]{:S(2)}, u32[]{:S(2)}) %collective-permute-start.21) | collective-permute-done | bytes 393248 | tf_op jit(solution)/shard_map/ppermute | solution.py:199
  272.1 7.0 %fusion.2 = f32[512,1536]{0,1:T(8,128)S(1)} fusion(bf16[2560,1536]{1,0:T(8,128)(2,1)} %get-tuple-element.44, bf16[512,1280]{1,0:T(8,128)(2,1)} %shard_map.79, bf16[512,1280]{1,0:T(8,128)(2,1)S(1)} %copy-done.10), kind=kOutput, calls=%fused_computation.7 | convolution fusion | flops 4031774720 | bytes 13631488 | tf_op jit(solution)/shard_map/dot_general | solution.py:22
  279.1 0.1 dynamic-slice_convert_fusion.1
  279.2 0.1 collective-permute-start.22
  279.3 2.3 collective-permute-done.22
  281.6 0.2 convert_add_fusion.1
  281.8 0.1 dynamic-slice_convert_fusion.3
  281.9 0.1 collective-permute-start.23
  283.2 9.4 %collective-permute-done.23 = bf16[512,384]{0,1:T(8,128)(2,1)S(1)} collective-permute-done((bf16[512,384]{0,1:T(8,128)(2,1)S(1)}, bf16[512,384]{0,1:T(8,128)(2,1)S(1)}, u32[]{:S(2)}, u32[]{:S(2)}) %collective-permute-start.23) | collective-permute-done | bytes 393248 | tf_op jit(solution)/shard_map/ppermute | solution.py:199
  292.5 0.1 add_convert_fusion.1
  292.7 3.8 %collective-permute-start.24 = (bf16[512,192]{0,1:T(8,128)(2,1)S(1)}, bf16[512,192]{0,1:T(8,128)(2,1)S(1)}, u32[]{:S(2)}, u32[]{:S(2)}) collective-permute-start(bf16[512,192]{0,1:T(8,128)(2,1)S(1)} %get-tuple-element.55), channel_id=1, source_target_pairs={{0,0},{1,16},{2,8},{3,24},{4,4},{5,20},{6,12},{7,28},{8,1},{9,17},... | collective-permute-start | bytes 589832 | tf_op jit(solution)/shard_map/ppermute | solution.py:199
  296.5 1.3 collective-permute-start.25
  297.9 10.2 %collective-permute-done.24 = bf16[512,192]{0,1:T(8,128)(2,1)S(1)} collective-permute-done((bf16[512,192]{0,1:T(8,128)(2,1)S(1)}, bf16[512,192]{0,1:T(8,128)(2,1)S(1)}, u32[]{:S(2)}, u32[]{:S(2)}) %collective-permute-start.24) | collective-permute-done | bytes 196640 | tf_op jit(solution)/shard_map/ppermute | solution.py:199
  308.1 2.1 collective-permute-done.25
  310.2 1.7 convert_divide_fusion
  (45 shorter events, 0.2 us)
Async XLA Ops:
  3.7 37.4 %collective-permute-start.14 = (bf16[1024,1536]{1,0:T(8,128)(2,1)}, bf16[1024,1536]{1,0:T(8,128)(2,1)S(1)}, u32[]{:S(2)}, u32[]{:S(2)}) collective-permute-start(bf16[1024,1536]{1,0:T(8,128)(2,1)} %constant_dynamic-slice_fusion.5), channel_id=1, source_target_pairs={{0,2},{4,6},{9,11},{13,15},{18,16},{22,20},{27,25},{31,29}} | collective-permute-start | bytes 9437192 | tf_op jit(solution)/shard_map/ppermute | solution.py:199
  8.4 24.4 %collective-permute-start = (bf16[176,1536]{1,0:T(8,128)(2,1)}, bf16[176,1536]{1,0:T(8,128)(2,1)}, u32[]{:S(2)}, u32[]{:S(2)}) collective-permute-start(bf16[176,1536]{1,0:T(8,128)(2,1)} %get-tuple-element.31), channel_id=1, source_target_pairs={{0,4},{4,0},{8,12},{12,8},{16,20},{20,16},{24,28},{28,24},{1,5},{5... | collective-permute-start | bytes 1622024 | tf_op jit(solution)/shard_map/ppermute | solution.py:199
  10.5 24.2 %collective-permute-start.1 = (bf16[176,1536]{1,0:T(8,128)(2,1)}, bf16[176,1536]{1,0:T(8,128)(2,1)}, u32[]{:S(2)}, u32[]{:S(2)}) collective-permute-start(bf16[176,1536]{1,0:T(8,128)(2,1)} %get-tuple-element.31), channel_id=1, source_target_pairs={{0,24},{4,28},{8,0},{12,4},{16,8},{20,12},{24,16},{28,20},{1,25},{... | collective-permute-start | bytes 1622024 | tf_op jit(solution)/shard_map/ppermute | solution.py:199
  14.2 23.2 %collective-permute-start.2 = (bf16[176,1536]{1,0:T(8,128)(2,1)}, bf16[176,1536]{1,0:T(8,128)(2,1)}, u32[]{:S(2)}, u32[]{:S(2)}) collective-permute-start(bf16[176,1536]{1,0:T(8,128)(2,1)} %get-tuple-element.31), channel_id=1, source_target_pairs={{0,8},{4,12},{8,16},{12,20},{16,24},{20,28},{24,0},{28,4},{1,9},{5... | collective-permute-start | bytes 1622024 | tf_op jit(solution)/shard_map/ppermute | solution.py:199
  14.3 55.6 %collective-permute-start.7 = (bf16[176,1536]{1,0:T(8,128)(2,1)}, bf16[176,1536]{1,0:T(8,128)(2,1)}, u32[]{:S(2)}, u32[]{:S(2)}) collective-permute-start(bf16[176,1536]{1,0:T(8,128)(2,1)} %get-tuple-element.31), channel_id=1, source_target_pairs={{0,16},{4,20},{8,24},{12,28},{16,0},{20,4},{24,8},{28,12},{1,17},{... | collective-permute-start | bytes 1622024 | tf_op jit(solution)/shard_map/ppermute | solution.py:199
  32.9 42.0 %collective-permute-start.17 = (bf16[512,1536]{1,0:T(8,128)(2,1)}, bf16[512,1536]{1,0:T(8,128)(2,1)}, u32[]{:S(2)}, u32[]{:S(2)}) collective-permute-start(bf16[512,1536]{1,0:T(8,128)(2,1)} %constant_dynamic-slice_fusion.4), channel_id=1, source_target_pairs={{0,2},{4,6},{9,11},{13,15},{18,16},{22,20},{27,25},{31,29}} | collective-permute-start | bytes 4718600 | tf_op jit(solution)/shard_map/ppermute | solution.py:199
  37.4 11.6 %collective-permute-start.10 = (bf16[176,1536]{1,0:T(8,128)(2,1)}, bf16[176,1536]{1,0:T(8,128)(2,1)S(1)}, u32[]{:S(2)}, u32[]{:S(2)}) collective-permute-start(bf16[176,1536]{1,0:T(8,128)(2,1)} %collective-permute-done.2.refs_5_), channel_id=1, source_target_pairs={{0,1},{1,0},{2,3},{3,2},{4,5},{5,4},{6,7},{7,6},{8,9},{9,8},{10,11... | collective-permute-start | bytes 1622024 | tf_op jit(solution)/shard_map/ppermute | solution.py:199
  41.1 9.3 %collective-permute-start.8 = (bf16[176,1536]{1,0:T(8,128)(2,1)}, bf16[176,1536]{1,0:T(8,128)(2,1)S(1)}, u32[]{:S(2)}, u32[]{:S(2)}) collective-permute-start(bf16[176,1536]{1,0:T(8,128)(2,1)} %collective-permute-done.refs_1_), channel_id=1, source_target_pairs={{0,1},{1,0},{2,3},{3,2},{4,5},{5,4},{6,7},{7,6},{8,9},{9,8},{10,11... | collective-permute-start | bytes 1622024 | tf_op jit(solution)/shard_map/ppermute | solution.py:199
  41.1 1.6 copy-start.2
  42.7 7.9 %collective-permute-start.9 = (bf16[176,1536]{1,0:T(8,128)(2,1)}, bf16[176,1536]{1,0:T(8,128)(2,1)S(1)}, u32[]{:S(2)}, u32[]{:S(2)}) collective-permute-start(bf16[176,1536]{1,0:T(8,128)(2,1)} %collective-permute-done.1.refs_3_), channel_id=1, source_target_pairs={{0,1},{1,0},{2,3},{3,2},{4,5},{5,4},{6,7},{7,6},{8,9},{9,8},{10,11... | collective-permute-start | bytes 1622024 | tf_op jit(solution)/shard_map/ppermute | solution.py:199
  49.1 2.8 copy-start.5
  49.1 22.1 %collective-permute-start.3 = (bf16[176,1536]{1,0:T(8,128)(2,1)}, bf16[176,1536]{1,0:T(8,128)(2,1)}, u32[]{:S(2)}, u32[]{:S(2)}) collective-permute-start(bf16[176,1536]{1,0:T(8,128)(2,1)} %collective-permute-done.1.refs_3_), channel_id=1, source_target_pairs={{0,4},{4,0},{8,12},{12,8},{16,20},{20,16},{24,28},{28,24},{1,5},{5... | collective-permute-start | bytes 1622024 | tf_op jit(solution)/shard_map/ppermute | solution.py:199
  50.4 1.6 copy-start.7
  50.4 24.2 %collective-permute-start.5 = (bf16[176,1536]{1,0:T(8,128)(2,1)}, bf16[176,1536]{1,0:T(8,128)(2,1)}, u32[]{:S(2)}, u32[]{:S(2)}) collective-permute-start(bf16[176,1536]{1,0:T(8,128)(2,1)} %collective-permute-done.2.refs_5_), channel_id=1, source_target_pairs={{0,4},{4,0},{8,12},{12,8},{16,20},{20,16},{24,28},{28,24},{1,5},{5... | collective-permute-start | bytes 1622024 | tf_op jit(solution)/shard_map/ppermute | solution.py:199
  50.6 1.3 copy-start.9
  50.6 62.1 %collective-permute-start.15 = (bf16[1024,1536]{1,0:T(8,128)(2,1)S(1)}, bf16[1024,1536]{1,0:T(8,128)(2,1)}, u32[]{:S(2)}, u32[]{:S(2)}) collective-permute-start(bf16[1024,1536]{1,0:T(8,128)(2,1)S(1)} %broadcast_select_fusion), channel_id=1, source_target_pairs={{0,1},{2,3},{4,5},{6,7},{9,8},{11,10},{13,12},{15,14},{18,19},{16,... | collective-permute-start | bytes 9437192 | tf_op jit(solution)/shard_map/ppermute | solution.py:199
  69.9 15.2 %collective-permute-start.12 = (bf16[176,1536]{1,0:T(8,128)(2,1)}, bf16[176,1536]{1,0:T(8,128)(2,1)}, u32[]{:S(2)}, u32[]{:S(2)}) collective-permute-start(bf16[176,1536]{1,0:T(8,128)(2,1)} %collective-permute-done.7.refs_4_), channel_id=1, source_target_pairs={{0,4},{4,0},{8,12},{12,8},{16,20},{20,16},{24,28},{28,24},{1,5},{5... | collective-permute-start | bytes 1622024 | tf_op jit(solution)/shard_map/ppermute | solution.py:199
  71.2 19.1 %collective-permute-start.11 = (bf16[176,1536]{1,0:T(8,128)(2,1)}, bf16[176,1536]{1,0:T(8,128)(2,1)S(1)}, u32[]{:S(2)}, u32[]{:S(2)}) collective-permute-start(bf16[176,1536]{1,0:T(8,128)(2,1)} %collective-permute-done.7.refs_4_), channel_id=1, source_target_pairs={{0,1},{1,0},{2,3},{3,2},{4,5},{5,4},{6,7},{7,6},{8,9},{9,8},{10,11... | collective-permute-start | bytes 1622024 | tf_op jit(solution)/shard_map/ppermute | solution.py:199
  74.6 17.2 %collective-permute-start.4 = (bf16[176,1536]{1,0:T(8,128)(2,1)}, bf16[176,1536]{1,0:T(8,128)(2,1)S(1)}, u32[]{:S(2)}, u32[]{:S(2)}) collective-permute-start(bf16[176,1536]{1,0:T(8,128)(2,1)} %collective-permute-done.3.refs_0_), channel_id=1, source_target_pairs={{0,1},{1,0},{2,3},{3,2},{4,5},{5,4},{6,7},{7,6},{8,9},{9,8},{10,11... | collective-permute-start | bytes 1622024 | tf_op jit(solution)/shard_map/ppermute | solution.py:199
  74.8 16.9 %collective-permute-start.6 = (bf16[176,1536]{1,0:T(8,128)(2,1)}, bf16[176,1536]{1,0:T(8,128)(2,1)S(1)}, u32[]{:S(2)}, u32[]{:S(2)}) collective-permute-start(bf16[176,1536]{1,0:T(8,128)(2,1)} %collective-permute-done.5.refs_2_), channel_id=1, source_target_pairs={{0,1},{1,0},{2,3},{3,2},{4,5},{5,4},{6,7},{7,6},{8,9},{9,8},{10,11... | collective-permute-start | bytes 1622024 | tf_op jit(solution)/shard_map/ppermute | solution.py:199
  85.1 6.7 %collective-permute-start.13 = (bf16[176,1536]{1,0:T(8,128)(2,1)}, bf16[176,1536]{1,0:T(8,128)(2,1)S(1)}, u32[]{:S(2)}, u32[]{:S(2)}) collective-permute-start(bf16[176,1536]{1,0:T(8,128)(2,1)} %collective-permute-done.12.refs_6_), channel_id=1, source_target_pairs={{0,1},{1,0},{2,3},{3,2},{4,5},{5,4},{6,7},{7,6},{8,9},{9,8},{10,11... | collective-permute-start | bytes 1622024 | tf_op jit(solution)/shard_map/ppermute | solution.py:199
  90.2 1.5 copy-start.3
  90.2 116.3 %collective-permute-start.18 = (bf16[512,1536]{1,0:T(8,128)(2,1)}, bf16[512,1536]{1,0:T(8,128)(2,1)}, u32[]{:S(2)}, u32[]{:S(2)}) collective-permute-start(bf16[512,1536]{1,0:T(8,128)(2,1)} %broadcast_select_fusion.1), channel_id=1, source_target_pairs={{0,1},{2,3},{4,5},{6,7},{9,8},{11,10},{13,12},{15,14},{18,19},{16,... | collective-permute-start | bytes 4718600 | tf_op jit(solution)/shard_map/ppermute | solution.py:199
  91.7 0.8 copy-start.4
  91.7 1.0 copy-start.6
  91.8 1.2 copy-start.8
  112.7 77.5 %slice-start = ((s8[7864320]{0:T(1024)(128)(4,1)}), s8[4194304]{0:T(1024)(128)(4,1)S(1)}, s32[]{:S(2)}) async-start(s8[7864320]{0:T(1024)(128)(4,1)} %bitcast.14), calls=%async_computation | async-start | bytes 8388608
  126.1 64.1 %slice-start.1 = ((s8[7864320]{0:T(1024)(128)(4,1)}), s8[3670016]{0:T(1024)(128)(4,1)S(1)}, s32[]{:S(2)}) async-start(s8[7864320]{0:T(1024)(128)(4,1)} %bitcast.14), calls=%async_computation.1 | async-start | bytes 7340032
  201.8 2.6 copy-start
  204.6 11.5 %collective-permute-start.16 = (bf16[1024,768]{0,1:T(8,128)(2,1)S(1)}, bf16[1024,768]{0,1:T(8,128)(2,1)S(1)}, u32[]{:S(2)}, u32[]{:S(2)}) collective-permute-start(bf16[1024,768]{0,1:T(8,128)(2,1)S(1)} %dynamic-slice_convert_fusion), channel_id=1, source_target_pairs={{0,1},{1,0},{2,3},{3,2},{4,5},{5,4},{6,7},{7,6},{8,9},{9,8},{10,11... | collective-permute-start | bytes 4718600 | tf_op jit(solution)/shard_map/ppermute | solution.py:199
  206.5 9.7 %copy-start.1 = (f32[1024,1536]{0,1:T(8,128)S(1)}, f32[1024,1536]{0,1:T(8,128)}, u32[]{:S(2)}) copy-start(f32[1024,1536]{0,1:T(8,128)} %copy-done) | copy-start | bytes 18874372
  216.9 22.1 %collective-permute-start.19 = (bf16[1024,384]{0,1:T(8,128)(2,1)S(1)}, bf16[1024,384]{0,1:T(8,128)(2,1)S(1)}, u32[]{:S(2)}, u32[]{:S(2)}) collective-permute-start(bf16[1024,384]{0,1:T(8,128)(2,1)S(1)} %dynamic-slice_convert_fusion.2), channel_id=1, source_target_pairs={{0,2},{1,3},{2,0},{3,1},{4,6},{5,7},{6,4},{7,5},{8,10},{9,11},{10,... | collective-permute-start | bytes 2359304 | tf_op jit(solution)/shard_map/ppermute | solution.py:199
  239.3 32.8 %copy-start.10 = (bf16[512,1280]{1,0:T(8,128)(2,1)S(1)}, bf16[512,1280]{1,0:T(8,128)(2,1)}, u32[]{:S(2)}) copy-start(bf16[512,1280]{1,0:T(8,128)(2,1)} %shard_map.78) | copy-start | bytes 3932164
  239.3 29.1 %collective-permute-start.20 = (bf16[1024,192]{0,1:T(8,128)(2,1)S(1)}, bf16[1024,192]{0,1:T(8,128)(2,1)S(1)}, u32[]{:S(2)}, u32[]{:S(2)}) collective-permute-start(bf16[1024,192]{0,1:T(8,128)(2,1)S(1)} %get-tuple-element.49), channel_id=1, source_target_pairs={{0,0},{1,16},{2,8},{3,24},{4,4},{5,20},{6,12},{7,28},{8,1},{9,17},... | collective-permute-start | bytes 1179656 | tf_op jit(solution)/shard_map/ppermute | solution.py:199
  248.6 23.4 %collective-permute-start.21 = (bf16[1024,192]{0,1:T(8,128)(2,1)S(1)}, bf16[1024,192]{0,1:T(8,128)(2,1)S(1)}, u32[]{:S(2)}, u32[]{:S(2)}) collective-permute-start(bf16[1024,192]{0,1:T(8,128)(2,1)S(1)} %get-tuple-element.50), channel_id=1, source_target_pairs={{0,4},{1,20},{2,12},{3,28},{4,0},{5,16},{6,8},{7,24},{8,5},{9,21},... | collective-permute-start | bytes 1179656 | tf_op jit(solution)/shard_map/ppermute | solution.py:199
  279.2 2.4 collective-permute-start.22
  281.9 10.6 %collective-permute-start.23 = (bf16[512,384]{0,1:T(8,128)(2,1)S(1)}, bf16[512,384]{0,1:T(8,128)(2,1)S(1)}, u32[]{:S(2)}, u32[]{:S(2)}) collective-permute-start(bf16[512,384]{0,1:T(8,128)(2,1)S(1)} %dynamic-slice_convert_fusion.3), channel_id=1, source_target_pairs={{0,2},{1,3},{2,0},{3,1},{4,6},{5,7},{6,4},{7,5},{8,10},{9,11},{10,... | collective-permute-start | bytes 1179656 | tf_op jit(solution)/shard_map/ppermute | solution.py:199
  292.7 15.4 %collective-permute-start.24 = (bf16[512,192]{0,1:T(8,128)(2,1)S(1)}, bf16[512,192]{0,1:T(8,128)(2,1)S(1)}, u32[]{:S(2)}, u32[]{:S(2)}) collective-permute-start(bf16[512,192]{0,1:T(8,128)(2,1)S(1)} %get-tuple-element.55), channel_id=1, source_target_pairs={{0,0},{1,16},{2,8},{3,24},{4,4},{5,20},{6,12},{7,28},{8,1},{9,17},... | collective-permute-start | bytes 589832 | tf_op jit(solution)/shard_map/ppermute | solution.py:199
  296.5 13.7 %collective-permute-start.25 = (bf16[512,192]{0,1:T(8,128)(2,1)S(1)}, bf16[512,192]{0,1:T(8,128)(2,1)S(1)}, u32[]{:S(2)}, u32[]{:S(2)}) collective-permute-start(bf16[512,192]{0,1:T(8,128)(2,1)S(1)} %get-tuple-element.56), channel_id=1, source_target_pairs={{0,4},{1,20},{2,12},{3,28},{4,0},{5,16},{6,8},{7,24},{8,5},{9,21},... | collective-permute-start | bytes 589832 | tf_op jit(solution)/shard_map/ppermute | solution.py:199

commit v3 on v2

--- a/solution.py
+++ b/solution.py
@@ -134,45 +134,29 @@
     )(*items, col, *before)
 
 
-def pair_kernel(sub, first, weight_ref, kt_ref, lrp_ref, lrq_ref, out_ref, sides):
-    item, occ = first + pl.program_id(0), sides.shape[2]
-    size_b = kt_ref.shape[1]
-
-    for odd in (0, 1):
-
-        @pl.when(item % 2 == odd)
-        def _():
-            for side in (0, 1):
-                at = (2 * odd + side) * occ
-                sides[side] = lrq_ref[:, at : at + occ]
-
-    total_l = jnp.zeros(sides.shape[1:], F32)
-    total_r = jnp.zeros(sides.shape[1:], F32)
+def pair_kernel(sub, first, weight_ref, kt_ref, lrp_ref, lrq_ref, out_ref):
+    rows, size_b = kt_ref.shape
+    occ = lrp_ref.shape[0] // 4
+    sides = [lrq_ref[:, n * occ : (n + 1) * occ] for n in range(4)]
+    totals = [jnp.zeros((rows, occ), F32) for _ in range(4)]
     for at in range(0, size_b, sub):
-        left_t = lrp_ref[:occ, at : at + sub]
-        right_t = lrp_ref[occ:, at : at + sub]
-        kern = kt_ref[:, at : at + sub]
-        had_t = kern * dot(sides[1], left_t).astype(BF16)
-        had = kern * dot(sides[0], right_t).astype(BF16)
-        total_l += dot(had_t, right_t, NT)
-        total_r += dot(had, left_t, NT)
-    scale = 2.0 * weight_ref[item]
-    sides[0] = (total_l * scale).astype(BF16)
-    sides[1] = (total_r * scale).astype(BF16)
-
-    for odd in (0, 1):
-
-        @pl.when(item % 2 == odd)
-        def _():
-            for side in (0, 1):
-                at = (2 * odd + side) * occ
-                out_ref[:, at : at + occ] = sides[side]
-
-
-def pair_gradients(weights, kernel_t, lrp, lrq, row_at, items=None):
-    size_b, rows, count = kernel_t.shape[1], lrq.shape[0], weights.shape[0]
-    first, last = items or (0, count)
-    width = lrp.shape[0] // count
+        kern = kt_ref[:, at : at + sub].astype(F32)
+        for n in (0, 2):
+            left_t = lrp_ref[n * occ : (n + 1) * occ, at : at + sub]
+            right_t = lrp_ref[(n + 1) * occ : (n + 2) * occ, at : at + sub]
+            had_t = (kern * dot(sides[n + 1], left_t)).astype(BF16)
+            had = (kern * dot(sides[n], right_t)).astype(BF16)
+            totals[n] += dot(had_t, right_t, NT)
+            totals[n + 1] += dot(had, left_t, NT)
+    for n in range(4):
+        scale = 2.0 * weight_ref[2 * (first + pl.program_id(0)) + n // 2]
+        out_ref[:, n * occ : (n + 1) * occ] = (totals[n] * scale).astype(BF16)
+
+
+def pair_gradients(weights, kernel_t, lrp, lrq, row_at, rows, items=None):
+    size_b, count = kernel_t.shape[1], weights.shape[0]
+    first, last = [n // 2 for n in items or (0, count)]
+    width = 2 * lrp.shape[0] // count
     at, sub = row_at // rows, tile_of(size_b, 512)
     return pl.pallas_call(
         functools.partial(pair_kernel, sub, first),
@@ -181,16 +165,15 @@
             num_scalar_prefetch=1,
             grid=(last - first,),
             in_specs=[
-                pl.BlockSpec((rows, size_b), lambda w, s: (at, 0), pipeline_mode=pl.Buffered(1)),
-                pl.BlockSpec((width, size_b), lambda w, s: (first + w, 0)),
-                pl.BlockSpec((rows, 2 * width), lambda w, s: (0, (first + w) // 2)),
+                pl.BlockSpec((rows, size_b), lambda p, s: (at, 0), pipeline_mode=pl.Buffered(1)),
+                pl.BlockSpec((width, size_b), lambda p, s: (first + p, 0)),
+                pl.BlockSpec((rows, width), lambda p, s: (at, first + p)),
             ],
-            out_specs=pl.BlockSpec((rows, 2 * width), lambda w, s: (0, w // 2)),
-            scratch_shapes=[pltpu.VMEM((2, rows, width // 2), BF16)],
+            out_specs=pl.BlockSpec((rows, width), lambda p, s: (0, p)),
         ),
         compiler_params=pltpu.CompilerParams(vmem_limit_bytes=VMEM_LIMIT),
         cost_estimate=cost(
-            2 * 4 * (last - first) * 256 * rows * size_b, 2 * (last - first) * (rows + width) * size_b
+            2 * 8 * (last - first) * 256 * rows * size_b, 2 * (last - first) * (rows + width) * size_b
         ),
     )(weights, kernel_t, lrp, lrq)
 
@@ -245,20 +228,20 @@
     own, half = packed(bra, ket, walker_group, group_occupied, core.reshape(1), walker_weight)
     cols_q = [columns_q(*chunk) for chunk in chunks]
     z1, z3, x0 = along(half, 1), along(half, 3), across(half)
-    z2 = along(half, 2)
     kernel_t = turned(kernel)
     x0, z1, z3, kernel_t = tie((x0, z1, z3, kernel_t))
-    x1, x3 = across(z1), across(z3)
+    z2, x1, x3 = along(z1, 1), across(z1), across(z3)
+    z2, z1, z3 = tie((z2, z1, z3))
+    x2 = across(z2)
     near_four = [own] + [h for part in (x0, z1, z3) for h in (part, other(part))]
     lrp, stack, weight_rows = project(near_four, [width] + [occ] * 6, collocation, 2, 0)
-    z2, weight_rows = tie((z2, weight_rows))
-    far_four = [h for part in (x1, x3, z2, across(z2)) for h in (part, other(part))]
     first = (lrp, stack, weight_rows)
+    x2, *first = tie((x2, *first))
+    far_four = [h for part in (x1, x3, z2, x2) for h in (part, other(part))]
     lrp, stack, weight_rows = project(far_four, [occ] * 8, collocation, 2, 1, first)
     weights = jnp.concatenate([weight_rows[:4, 0], weight_rows[8:12, 0]])
 
-    def rows_q(c):
-        return dot(cols_q[c], stack, NT).astype(BF16)
+    lrq = dot(jnp.concatenate(cols_q, axis=0), stack, NT).astype(BF16)
 
     half_m, quarter, eighth = size_m // 2, size_m // 4, size_m // 8
     swap_y = [(i, i ^ 2) for i in range(npt)]
@@ -277,20 +260,22 @@
         return pieces, came
 
     def over_cores(grads):
-        give, keep = split(dot(grads, stack), core, half_m)
+        give, keep = split(grads, core, half_m)
         return split(keep + other(give).astype(F32), y, quarter)
 
-    grads = pair_gradients(weights, kernel_t, lrp, rows_q(0), chunks[0][0])
-    lrq = rows_q(1)
-    give, keep = over_cores(grads)
+    (at_0, rows_0), (at_1, rows_1) = chunks
+    middle = stack.shape[0] // 2
+    grads = pair_gradients(weights, kernel_t, lrp, lrq, at_0, rows_0)
+    give, keep = over_cores(dot(grads, stack))
     give, lrq = tie((give, lrq))
     got = send(give, "pt", swap_y)
-    early = pair_gradients(weights, kernel_t, lrp, lrq, chunks[1][0], (0, 4))
-    early, got = tie((early, got))
+    early = pair_gradients(weights, kernel_t, lrp, lrq, at_1, rows_1, (0, 4))
+    part = dot(early, stack[:middle])
+    part, got = tie((part, got))
     pieces, came_0 = to_place((keep + got.astype(F32)).astype(BF16), lrq)
-    late = pair_gradients(weights, kernel_t, lrp, pieces[2], chunks[1][0], (4, 8))
+    late = pair_gradients(weights, kernel_t, lrp, pieces[2], at_1, rows_1, (4, 8))
     late, *came_0 = tie((late, *came_0))
-    give, keep = over_cores(jnp.concatenate([early, late], axis=1))
+    give, keep = over_cores(part + dot(late, stack[middle:]))
     _, came_1 = to_place((keep + send(give, "pt", swap_y).astype(F32)).astype(BF16))
 
     ordered = [jnp.where(x == side, came[0], came[1]) for side in (0, 1) for came in (came_0, came_1)]
@@ -307,7 +292,7 @@
     col_q = lax.dynamic_slice_in_dim(all_rows, me_w * size_a, size_a, 0)
     lrp = dot(orbitals, collocation, NT).astype(BF16)
     lrq = dot(col_q, orbitals, NT).astype(BF16)
-    grads = pair_gradients(weights / jnp.sum(weights), turned(kernel), lrp, lrq, 0)
+    grads = pair_gradients(weights / jnp.sum(weights), turned(kernel), lrp, lrq, 0, size_a)
     part = lax.psum(dot(grads, orbitals), "pt")
     part = jnp.where((me_w * size_a) // size_b == me_p, part, 0.0)
     wide = lax.dynamic_update_slice_in_dim(jnp.zeros((size_b, size_m), F32), part, (me_w * size_a) % size_b, 0)

time: 318 us -> 313 us (0.984)
  starting transfers between devices: 46.2 us -> 39.9 us
  waiting for transfers between devices: 40.8 us -> 44.9 us
  Pallas kernels: 156 us -> 152 us
    ppermute x26, starting transfers between devices: 46.2 us -> 39.9 us  [send(): return lax.ppermute(x, axes, pairs)]
    ppermute x26, waiting for transfers between devices: 40.8 us -> 44.9 us  [send(): return lax.ppermute(x, axes, pairs)]
    pallas_call x3, Pallas kernels: 103 us -> 99.2 us  [pair_gradients(): pl.pallas_call(functools.partial(pair_kernel, sub, first), out_shape=jax....]
  transfers between devices with their start and end apart: 26 -> 26, of which waited for: 8 -> 10; matrix products, arithmetic and copies ran while one was open for 15% -> 6% of each run, Pallas kernels for 50% -> 29%
where the time goes in v3:
time: 313 us; the launch traced here: 308 us
  Pallas kernels  152 us (49%)
  waiting for transfers between devices  44.9 us (14%)
  starting transfers between devices  39.9 us (13%)
  matrix products  39.3 us (13%)
  other arithmetic  15 us (5%)
  local copies, waits for them, and re-layouts  13 us (4%)
  between operations  3.39 us (1%)
    pallas_call x3, Pallas kernels, pair_gradients(): pl.pallas_call(functools.partial(pair_kernel, sub, first), out_shape=jax....  99.2 us
    ppermute x26, waiting for transfers between devices, send(): return lax.ppermute(x, axes, pairs)  44.9 us
    ppermute x26, starting transfers between devices, send(): return lax.ppermute(x, axes, pairs)  39.9 us
    dot_general x4, matrix products, dot(): return lax.dot_general(a, b, dims, preferred_element_type=F32)  39.3 us
    pallas_call x2, Pallas kernels, project(): pl.pallas_call(functools.partial(project_kernel, tuple(rows_each), len(be...  35.8 us
    pallas_call x1, Pallas kernels, turned(): pl.pallas_call(turn_kernel, out_shape=jax.ShapeDtypeStruct((cols, rows),...  14.7 us
    dynamic_slice x2, local copies, waits for them, and re-layouts, columns_q(): rows = lax.dynamic_slice_in_dim(collocation, x * size_a + begin, chunk, 0)  6.37 us
  transfers between devices with their start and end apart: 26, of which 10 were waited for; matrix products, arithmetic and copies ran while one was open for 6% of the time, Pallas kernels for 29%

profile of v3, /device:TPU:1, one launch (start us, length us, event | category | flops | bytes accessed | tf_op | source)
XLA Modules:
  0.0 307.6 jit_solution(9860640163066847657)
XLA Ops:
  0.0 3.7 %constant_dynamic-slice_fusion.5 = bf16[1024,1536]{1,0:T(8,128)(2,1)} fusion(bf16[3072,1536]{1,0:T(8,128)(2,1)} %refs_8_.1, s32[]{:T(128)S(6)} %select_n.117), kind=kLoop, calls=%fused_computation.31 | loop fusion | bytes 6291460 | tf_op jit(solution)/shard_map/dynamic_slice | solution.py:216
  3.7 0.9 collective-permute-start.14
  5.9 2.6 shard_map.73
  8.5 2.0 collective-permute-start
  10.5 3.8 %collective-permute-start.1 = (bf16[176,1536]{1,0:T(8,128)(2,1)}, bf16[176,1536]{1,0:T(8,128)(2,1)}, u32[]{:S(2)}, u32[]{:S(2)}) collective-permute-start(bf16[176,1536]{1,0:T(8,128)(2,1)} %get-tuple-element.36), channel_id=1, source_target_pairs={{0,24},{4,28},{8,0},{12,4},{16,8},{20,12},{24,16},{28,20},{1,25},{... | collective-permute-start | bytes 1622024 | tf_op jit(solution)/shard_map/ppermute | solution.py:182
  14.3 14.7 %shard_map.74.kt_ref = bf16[1536,3072]{1,0:T(8,128)(2,1)} custom-call(bf16[3072,1536]{1,0:T(8,128)(2,1)} %in_ref.1), custom_call_target="tpu_custom_call" | custom-call | bytes 47185920 | tf_op jit(solution)/shard_map/pallas_call | solution.py:36
  29.0 8.5 %collective-permute-done.2.refs_5_ = bf16[176,1536]{1,0:T(8,128)(2,1)} collective-permute-done((bf16[176,1536]{1,0:T(8,128)(2,1)}, bf16[176,1536]{1,0:T(8,128)(2,1)}, u32[]{:S(2)}, u32[]{:S(2)}) %collective-permute-start.2) | collective-permute-done | bytes 540704 | tf_op jit(solution)/shard_map/ppermute | solution.py:182
  37.5 3.1 %collective-permute-start.7 = (bf16[176,1536]{1,0:T(8,128)(2,1)}, bf16[176,1536]{1,0:T(8,128)(2,1)}, u32[]{:S(2)}, u32[]{:S(2)}) collective-permute-start(bf16[176,1536]{1,0:T(8,128)(2,1)} %collective-permute-done.1.refs_3_), channel_id=1, source_target_pairs={{0,24},{4,28},{8,0},{12,4},{16,8},{20,12},{24,16},{28,20},{1,25},{... | collective-permute-start | bytes 1622024 | tf_op jit(solution)/shard_map/ppermute | solution.py:182
  40.5 2.7 constant_dynamic-slice_fusion.4
  43.2 1.8 collective-permute-start.16
  45.0 0.3 collective-permute-start.3
  45.2 4.7 %collective-permute-start.10 = (bf16[176,1536]{1,0:T(8,128)(2,1)}, bf16[176,1536]{1,0:T(8,128)(2,1)S(1)}, u32[]{:S(2)}, u32[]{:S(2)}) collective-permute-start(bf16[176,1536]{1,0:T(8,128)(2,1)} %collective-permute-done.refs_1_), channel_id=1, source_target_pairs={{0,1},{1,0},{2,3},{3,2},{4,5},{5,4},{6,7},{7,6},{8,9},{9,8},{10,11... | collective-permute-start | bytes 1622024 | tf_op jit(solution)/shard_map/ppermute | solution.py:182
  49.9 1.2 collective-permute-done.7.refs_4_
  51.2 2.2 collective-permute-start.11
  53.4 2.7 broadcast_select_fusion
  56.1 0.3 collective-permute-start.5
  56.4 1.2 collective-permute-start.9
  57.6 1.3 collective-permute-start.15
  58.9 17.9 %shard_map.75 = (bf16[2560,3072]{1,0:T(8,128)(2,1)}, bf16[2560,1536]{1,0:T(8,128)(2,1)}, f32[16,128]{1,0:T(8,128)}) custom-call(bf16[336,1536]{1,0:T(8,128)(2,1)} %get-tuple-element.40.refs_0_, bf16[176,1536]{1,0:T(8,128)(2,1)} %collective-permute-done.refs_1_, bf16[176,1536]{1,0:T(8,128)(2,1)} %copy-done.1, ...), custom_call_target="tpu_custom_call" | custom-call | flops 18119393280 | bytes 9437184 | tf_op jit(solution)/shard_map/pallas_call | solution.py:114
  76.9 1.4 collective-permute-start.8
  78.2 0.1 collective-permute-start.4
  78.3 3.9 %collective-permute-done.9.refs_6_ = bf16[176,1536]{1,0:T(8,128)(2,1)} collective-permute-done((bf16[176,1536]{1,0:T(8,128)(2,1)}, bf16[176,1536]{1,0:T(8,128)(2,1)}, u32[]{:S(2)}, u32[]{:S(2)}) %collective-permute-start.9) | collective-permute-done | bytes 540704 | tf_op jit(solution)/shard_map/ppermute | solution.py:182
  82.2 0.9 collective-permute-start.6
  83.2 2.3 broadcast_select_fusion.2
  85.5 1.8 collective-permute-start.17
  87.3 17.9 %shard_map.76 = (bf16[2560,3072]{1,0:T(8,128)(2,1)}, bf16[2560,1536]{1,0:T(8,128)(2,1)}, f32[16,128]{1,0:T(8,128)}) custom-call(bf16[176,1536]{1,0:T(8,128)(2,1)} %collective-permute-done.3.refs_0_, bf16[176,1536]{1,0:T(8,128)(2,1)} %collective-permute-done.4.refs_1_, ...), custom_call_target="tpu_custom_call", output_to_operand_aliasing={{0}: (9, {}), {1}: (10, {}), {2}: (11, {})} | custom-call | flops 18119393280 | bytes 9437184 | tf_op jit(solution)/shard_map/pallas_call | solution.py:114
  105.2 1.4 slice_reduce_fusion
  106.5 0.6 pad_maximum_fusion.weight_ref
  107.2 1.6 broadcast_select_fusion.3
  108.8 0.3 broadcast_select_fusion.1
  109.1 17.4 %convolution_convert_fusion.lrq_ref = bf16[1536,2560]{1,0:T(8,128)(2,1)} fusion(bf16[2560,1536]{1,0:T(8,128)(2,1)} %get-tuple-element.54, bf16[512,1536]{1,0:T(8,128)(2,1)S(1)} %broadcast_select_fusion.3, bf16[1024,1536]{1,0:T(8,128)(2,1)S(1)} %broadcast_select_fusion.1), kind=kOutput, calls=%fused_computation | convolution fusion | flops 12092964864 | bytes 20447232 | tf_op jit(solution)/shard_map/dot_general | solution.py:22
  126.6 61.9 %shard_map.77 = bf16[1024,2560]{1,0:T(8,128)(2,1)} custom-call(f32[8]{0:T(128)} %pad_maximum_fusion.weight_ref, bf16[1536,3072]{1,0:T(8,128)(2,1)} %shard_map.74.kt_ref, bf16[2560,3072]{1,0:T(8,128)(2,1)} %get-tuple-element.53.lrp_ref, bf16[1536,2560]{1,0:T(8,128)(2,1)} %convolution_convert_fusion.lrq_ref), custom_call_target="tpu_custom_call" | custom-call | flops 51539607552 | bytes 40894464 | tf_op jit(solution)/shard_map/pallas_call | solution.py:161
  188.5 11.3 %fusion.11 = f32[1024,1536]{0,1:T(8,128)S(1)} fusion(bf16[1024,2560]{1,0:T(8,128)(2,1)} %shard_map.77, bf16[2560,1536]{1,0:T(8,128)(2,1)S(1)} %bitcast.15), kind=kOutput, calls=%fused_computation.38 | convolution fusion | flops 8053063680 | bytes 19398656 | tf_op jit(solution)/shard_map/dot_general | solution.py:22
  199.8 2.7 copy-done
  202.5 0.2 dynamic-slice_convert_fusion
  202.8 0.9 collective-permute-start.18
  203.7 3.0 collective-permute-done.18
  206.7 2.7 convert_add_fusion
  209.4 0.1 dynamic-slice_convert_fusion.2
  209.5 2.5 collective-permute-start.19
  212.0 18.8 %shard_map.78 = bf16[512,1280]{1,0:T(8,128)(2,1)} custom-call(f32[8]{0:T(128)} %pad_maximum_fusion.weight_ref, bf16[1536,3072]{1,0:T(8,128)(2,1)} %shard_map.74.kt_ref, bf16[2560,3072]{1,0:T(8,128)(2,1)} %get-tuple-element.53.lrp_ref, bf16[1536,2560]{1,0:T(8,128)(2,1)} %convolution_convert_fusion.lrq_ref), custom_call_target="tpu_custom_call" | custom-call | flops 12884901888 | bytes 14155776 | tf_op jit(solution)/shard_map/pallas_call | solution.py:161
  230.8 4.7 %fusion.5 = f32[512,1536]{1,0:T(8,128)S(1)} fusion(bf16[512,1280]{1,0:T(8,128)(2,1)} %shard_map.78, bf16[2560,1536]{1,0:T(8,128)(2,1)} %get-tuple-element.54), kind=kOutput, calls=%fused_computation.6 | convolution fusion | flops 2013265920 | bytes 8388608 | tf_op jit(solution)/shard_map/dot_general | solution.py:22
  235.5 0.3 add_convert_fusion
  235.7 1.0 constant_dynamic-slice_fusion.2
  236.7 3.3 %collective-permute-start.20 = (bf16[1024,192]{0,1:T(8,128)(2,1)}, bf16[1024,192]{0,1:T(8,128)(2,1)S(1)}, u32[]{:S(2)}, u32[]{:S(2)}) collective-permute-start(bf16[1024,192]{0,1:T(8,128)(2,1)} %get-tuple-element.59), channel_id=1, source_target_pairs={{0,0},{1,16},{2,8},{3,24},{4,4},{5,20},{6,12},{7,28},{8,1},{9,17},... | collective-permute-start | bytes 1179656 | tf_op jit(solution)/shard_map/ppermute | solution.py:182
  240.0 1.3 collective-permute-start.21
  241.3 18.5 %shard_map.79 = bf16[512,1280]{1,0:T(8,128)(2,1)} custom-call(f32[8]{0:T(128)} %pad_maximum_fusion.weight_ref, bf16[1536,3072]{1,0:T(8,128)(2,1)} %shard_map.74.kt_ref, bf16[2560,3072]{1,0:T(8,128)(2,1)} %get-tuple-element.53.lrp_ref, bf16[1536,2560]{1,0:T(8,128)(2,1)} %convolution_convert_fusion.lrq_ref), custom_call_target="tpu_custom_call" | custom-call | flops 12884901888 | bytes 14155776 | tf_op jit(solution)/shard_map/pallas_call | solution.py:161
  259.8 2.3 copy.15
  262.2 1.1 collective-permute-done.20
  263.3 4.3 %collective-permute-done.21 = bf16[1024,192]{0,1:T(8,128)(2,1)} collective-permute-done((bf16[1024,192]{0,1:T(8,128)(2,1)}, bf16[1024,192]{0,1:T(8,128)(2,1)}, u32[]{:S(2)}, u32[]{:S(2)}) %collective-permute-start.21) | collective-permute-done | bytes 393248 | tf_op jit(solution)/shard_map/ppermute | solution.py:182
  267.6 5.8 %fusion.7 = f32[512,1536]{0,1:T(8,128)S(1)} fusion(f32[512,1536]{0,1:T(8,128)} %copy.15, bf16[512,1280]{1,0:T(8,128)(2,1)} %shard_map.79, bf16[2560,1536]{1,0:T(8,128)(2,1)} %get-tuple-element.54), kind=kOutput, calls=%fused_computation.8 | convolution fusion | flops 2014052352 | bytes 11534336 | tf_op jit(solution)/shard_map/dot_general | solution.py:22
  273.4 0.1 dynamic-slice_convert_fusion.1
  273.5 0.1 collective-permute-start.22
  273.6 2.3 collective-permute-done.22
  275.9 0.2 convert_add_fusion.1
  276.2 0.1 collective-permute-start.23
  277.6 9.2 %collective-permute-done.23 = bf16[512,384]{0,1:T(8,128)(2,1)S(1)} collective-permute-done((bf16[512,384]{0,1:T(8,128)(2,1)S(1)}, bf16[512,384]{0,1:T(8,128)(2,1)S(1)}, u32[]{:S(2)}, u32[]{:S(2)}) %collective-permute-start.23) | collective-permute-done | bytes 393248 | tf_op jit(solution)/shard_map/ppermute | solution.py:182
  286.9 0.1 add_convert_fusion.1
  287.0 2.0 collective-permute-start.24
  289.1 4.1 %collective-permute-start.25 = (bf16[512,192]{0,1:T(8,128)(2,1)S(1)}, bf16[512,192]{0,1:T(8,128)(2,1)S(1)}, u32[]{:S(2)}, u32[]{:S(2)}) collective-permute-start(bf16[512,192]{0,1:T(8,128)(2,1)S(1)} %get-tuple-element.66), channel_id=1, source_target_pairs={{0,4},{1,20},{2,12},{3,28},{4,0},{5,16},{6,8},{7,24},{8,5},{9,21},... | collective-permute-start | bytes 589832 | tf_op jit(solution)/shard_map/ppermute | solution.py:182
  293.1 1.1 broadcast_select_fusion.5
  294.2 8.3 %collective-permute-done.24 = bf16[512,192]{0,1:T(8,128)(2,1)S(1)} collective-permute-done((bf16[512,192]{0,1:T(8,128)(2,1)S(1)}, bf16[512,192]{0,1:T(8,128)(2,1)S(1)}, u32[]{:S(2)}, u32[]{:S(2)}) %collective-permute-start.24) | collective-permute-done | bytes 196640 | tf_op jit(solution)/shard_map/ppermute | solution.py:182
  302.4 3.0 collective-permute-done.25
  305.5 1.7 convert_divide_fusion
  (32 shorter events, 0.2 us)
Async XLA Ops:
  3.7 49.6 %collective-permute-start.14 = (bf16[1024,1536]{1,0:T(8,128)(2,1)}, bf16[1024,1536]{1,0:T(8,128)(2,1)S(1)}, u32[]{:S(2)}, u32[]{:S(2)}) collective-permute-start(bf16[1024,1536]{1,0:T(8,128)(2,1)} %constant_dynamic-slice_fusion.5), channel_id=1, source_target_pairs={{0,2},{4,6},{9,11},{13,15},{18,16},{22,20},{27,25},{31,29}} | collective-permute-start | bytes 9437192 | tf_op jit(solution)/shard_map/ppermute | solution.py:182
  8.5 20.5 %collective-permute-start = (bf16[176,1536]{1,0:T(8,128)(2,1)}, bf16[176,1536]{1,0:T(8,128)(2,1)}, u32[]{:S(2)}, u32[]{:S(2)}) collective-permute-start(bf16[176,1536]{1,0:T(8,128)(2,1)} %get-tuple-element.36), channel_id=1, source_target_pairs={{0,4},{4,0},{8,12},{12,8},{16,20},{20,16},{24,28},{28,24},{1,5},{5... | collective-permute-start | bytes 1622024 | tf_op jit(solution)/shard_map/ppermute | solution.py:182
  10.5 18.5 %collective-permute-start.1 = (bf16[176,1536]{1,0:T(8,128)(2,1)}, bf16[176,1536]{1,0:T(8,128)(2,1)}, u32[]{:S(2)}, u32[]{:S(2)}) collective-permute-start(bf16[176,1536]{1,0:T(8,128)(2,1)} %get-tuple-element.36), channel_id=1, source_target_pairs={{0,24},{4,28},{8,0},{12,4},{16,8},{20,12},{24,16},{28,20},{1,25},{... | collective-permute-start | bytes 1622024 | tf_op jit(solution)/shard_map/ppermute | solution.py:182
  14.2 23.2 %collective-permute-start.2 = (bf16[176,1536]{1,0:T(8,128)(2,1)}, bf16[176,1536]{1,0:T(8,128)(2,1)}, u32[]{:S(2)}, u32[]{:S(2)}) collective-permute-start(bf16[176,1536]{1,0:T(8,128)(2,1)} %get-tuple-element.36), channel_id=1, source_target_pairs={{0,8},{4,12},{8,16},{12,20},{16,24},{20,28},{24,0},{28,4},{1,9},{5... | collective-permute-start | bytes 1622024 | tf_op jit(solution)/shard_map/ppermute | solution.py:182
  37.5 13.7 %collective-permute-start.7 = (bf16[176,1536]{1,0:T(8,128)(2,1)}, bf16[176,1536]{1,0:T(8,128)(2,1)}, u32[]{:S(2)}, u32[]{:S(2)}) collective-permute-start(bf16[176,1536]{1,0:T(8,128)(2,1)} %collective-permute-done.1.refs_3_), channel_id=1, source_target_pairs={{0,24},{4,28},{8,0},{12,4},{16,8},{20,12},{24,16},{28,20},{1,25},{... | collective-permute-start | bytes 1622024 | tf_op jit(solution)/shard_map/ppermute | solution.py:182
  43.2 40.0 %collective-permute-start.16 = (bf16[512,1536]{1,0:T(8,128)(2,1)}, bf16[512,1536]{1,0:T(8,128)(2,1)}, u32[]{:S(2)}, u32[]{:S(2)}) collective-permute-start(bf16[512,1536]{1,0:T(8,128)(2,1)} %constant_dynamic-slice_fusion.4), channel_id=1, source_target_pairs={{0,2},{4,6},{9,11},{13,15},{18,16},{22,20},{27,25},{31,29}} | collective-permute-start | bytes 4718600 | tf_op jit(solution)/shard_map/ppermute | solution.py:182
  45.0 31.9 %collective-permute-start.3 = (bf16[176,1536]{1,0:T(8,128)(2,1)}, bf16[176,1536]{1,0:T(8,128)(2,1)}, u32[]{:S(2)}, u32[]{:S(2)}) collective-permute-start(bf16[176,1536]{1,0:T(8,128)(2,1)} %collective-permute-done.1.refs_3_), channel_id=1, source_target_pairs={{0,4},{4,0},{8,12},{12,8},{16,20},{20,16},{24,28},{28,24},{1,5},{5... | collective-permute-start | bytes 1622024 | tf_op jit(solution)/shard_map/ppermute | solution.py:182
  45.2 10.8 %collective-permute-start.10 = (bf16[176,1536]{1,0:T(8,128)(2,1)}, bf16[176,1536]{1,0:T(8,128)(2,1)S(1)}, u32[]{:S(2)}, u32[]{:S(2)}) collective-permute-start(bf16[176,1536]{1,0:T(8,128)(2,1)} %collective-permute-done.refs_1_), channel_id=1, source_target_pairs={{0,1},{1,0},{2,3},{3,2},{4,5},{5,4},{6,7},{7,6},{8,9},{9,8},{10,11... | collective-permute-start | bytes 1622024 | tf_op jit(solution)/shard_map/ppermute | solution.py:182
  51.2 5.3 %collective-permute-start.11 = (bf16[176,1536]{1,0:T(8,128)(2,1)}, bf16[176,1536]{1,0:T(8,128)(2,1)S(1)}, u32[]{:S(2)}, u32[]{:S(2)}) collective-permute-start(bf16[176,1536]{1,0:T(8,128)(2,1)} %collective-permute-done.1.refs_3_), channel_id=1, source_target_pairs={{0,1},{1,0},{2,3},{3,2},{4,5},{5,4},{6,7},{7,6},{8,9},{9,8},{10,11... | collective-permute-start | bytes 1622024 | tf_op jit(solution)/shard_map/ppermute | solution.py:182
  53.3 4.3 %collective-permute-start.12 = (bf16[176,1536]{1,0:T(8,128)(2,1)}, bf16[176,1536]{1,0:T(8,128)(2,1)}, u32[]{:S(2)}, u32[]{:S(2)}) collective-permute-start(bf16[176,1536]{1,0:T(8,128)(2,1)} %collective-permute-done.2.refs_5_), channel_id=1, source_target_pairs={{0,1},{1,0},{2,3},{3,2},{4,5},{5,4},{6,7},{7,6},{8,9},{9,8},{10,11... | collective-permute-start | bytes 1622024 | tf_op jit(solution)/shard_map/ppermute | solution.py:182
  56.1 2.8 copy-start.1
  56.1 22.1 %collective-permute-start.5 = (bf16[176,1536]{1,0:T(8,128)(2,1)}, bf16[176,1536]{1,0:T(8,128)(2,1)}, u32[]{:S(2)}, u32[]{:S(2)}) collective-permute-start(bf16[176,1536]{1,0:T(8,128)(2,1)} %collective-permute-done.2.refs_5_), channel_id=1, source_target_pairs={{0,4},{4,0},{8,12},{12,8},{16,20},{20,16},{24,28},{28,24},{1,5},{5... | collective-permute-start | bytes 1622024 | tf_op jit(solution)/shard_map/ppermute | solution.py:182
  56.4 2.5 copy-start.2
  56.4 25.8 %collective-permute-start.9 = (bf16[176,1536]{1,0:T(8,128)(2,1)}, bf16[176,1536]{1,0:T(8,128)(2,1)}, u32[]{:S(2)}, u32[]{:S(2)}) collective-permute-start(bf16[176,1536]{1,0:T(8,128)(2,1)} %collective-permute-done.7.refs_4_), channel_id=1, source_target_pairs={{0,4},{4,0},{8,12},{12,8},{16,20},{20,16},{24,28},{28,24},{1,5},{5... | collective-permute-start | bytes 1622024 | tf_op jit(solution)/shard_map/ppermute | solution.py:182
  57.6 51.1 %collective-permute-start.15 = (bf16[1024,1536]{1,0:T(8,128)(2,1)S(1)}, bf16[1024,1536]{1,0:T(8,128)(2,1)S(1)}, u32[]{:S(2)}, u32[]{:S(2)}) collective-permute-start(bf16[1024,1536]{1,0:T(8,128)(2,1)S(1)} %broadcast_select_fusion), channel_id=1, source_target_pairs={{0,1},{2,3},{4,5},{6,7},{9,8},{11,10},{13,12},{15,14},{18,19},{16,... | collective-permute-start | bytes 9437192 | tf_op jit(solution)/shard_map/ppermute | solution.py:182
  76.9 8.6 %collective-permute-start.8 = (bf16[176,1536]{1,0:T(8,128)(2,1)}, bf16[176,1536]{1,0:T(8,128)(2,1)}, u32[]{:S(2)}, u32[]{:S(2)}) collective-permute-start(bf16[176,1536]{1,0:T(8,128)(2,1)} %collective-permute-done.7.refs_4_), channel_id=1, source_target_pairs={{0,1},{1,0},{2,3},{3,2},{4,5},{5,4},{6,7},{7,6},{8,9},{9,8},{10,11... | collective-permute-start | bytes 1622024 | tf_op jit(solution)/shard_map/ppermute | solution.py:182
  78.2 9.0 %collective-permute-start.4 = (bf16[176,1536]{1,0:T(8,128)(2,1)}, bf16[176,1536]{1,0:T(8,128)(2,1)}, u32[]{:S(2)}, u32[]{:S(2)}) collective-permute-start(bf16[176,1536]{1,0:T(8,128)(2,1)} %collective-permute-done.3.refs_0_), channel_id=1, source_target_pairs={{0,1},{1,0},{2,3},{3,2},{4,5},{5,4},{6,7},{7,6},{8,9},{9,8},{10,11... | collective-permute-start | bytes 1622024 | tf_op jit(solution)/shard_map/ppermute | solution.py:182
  82.2 5.0 %collective-permute-start.6 = (bf16[176,1536]{1,0:T(8,128)(2,1)}, bf16[176,1536]{1,0:T(8,128)(2,1)}, u32[]{:S(2)}, u32[]{:S(2)}) collective-permute-start(bf16[176,1536]{1,0:T(8,128)(2,1)} %collective-permute-done.5.refs_2_), channel_id=1, source_target_pairs={{0,1},{1,0},{2,3},{3,2},{4,5},{5,4},{6,7},{7,6},{8,9},{9,8},{10,11... | collective-permute-start | bytes 1622024 | tf_op jit(solution)/shard_map/ppermute | solution.py:182
  83.2 4.1 %collective-permute-start.13 = (bf16[176,1536]{1,0:T(8,128)(2,1)}, bf16[176,1536]{1,0:T(8,128)(2,1)}, u32[]{:S(2)}, u32[]{:S(2)}) collective-permute-start(bf16[176,1536]{1,0:T(8,128)(2,1)} %collective-permute-done.9.refs_6_), channel_id=1, source_target_pairs={{0,1},{1,0},{2,3},{3,2},{4,5},{5,4},{6,7},{7,6},{8,9},{9,8},{10,11... | collective-permute-start | bytes 1622024 | tf_op jit(solution)/shard_map/ppermute | solution.py:182
  85.5 21.7 %collective-permute-start.17 = (bf16[512,1536]{1,0:T(8,128)(2,1)S(1)}, bf16[512,1536]{1,0:T(8,128)(2,1)}, u32[]{:S(2)}, u32[]{:S(2)}) collective-permute-start(bf16[512,1536]{1,0:T(8,128)(2,1)S(1)} %broadcast_select_fusion.2), channel_id=1, source_target_pairs={{0,1},{2,3},{4,5},{6,7},{9,8},{11,10},{13,12},{15,14},{18,19},{16,... | collective-permute-start | bytes 4718600 | tf_op jit(solution)/shard_map/ppermute | solution.py:182
  109.1 79.3 %slice-start = ((s8[7864320]{0:T(1024)(128)(4,1)}), s8[4194304]{0:T(1024)(128)(4,1)S(1)}, s32[]{:S(2)}) async-start(s8[7864320]{0:T(1024)(128)(4,1)} %bitcast.14), calls=%async_computation | async-start | bytes 8388608
  126.6 61.9 %slice-start.1 = ((s8[7864320]{0:T(1024)(128)(4,1)}), s8[3670016]{0:T(1024)(128)(4,1)S(1)}, s32[]{:S(2)}) async-start(s8[7864320]{0:T(1024)(128)(4,1)} %bitcast.14), calls=%async_computation.1 | async-start | bytes 7340032
  199.8 2.7 copy-start
  202.8 4.0 %collective-permute-start.18 = (bf16[1024,768]{0,1:T(8,128)(2,1)S(1)}, bf16[1024,768]{0,1:T(8,128)(2,1)S(1)}, u32[]{:S(2)}, u32[]{:S(2)}) collective-permute-start(bf16[1024,768]{0,1:T(8,128)(2,1)S(1)} %dynamic-slice_convert_fusion), channel_id=1, source_target_pairs={{0,1},{1,0},{2,3},{3,2},{4,5},{5,4},{6,7},{7,6},{8,9},{9,8},{10,11... | collective-permute-start | bytes 4718600 | tf_op jit(solution)/shard_map/ppermute | solution.py:182
  209.5 26.0 %collective-permute-start.19 = (bf16[1024,384]{0,1:T(8,128)(2,1)S(1)}, bf16[1024,384]{0,1:T(8,128)(2,1)S(1)}, u32[]{:S(2)}, u32[]{:S(2)}) collective-permute-start(bf16[1024,384]{0,1:T(8,128)(2,1)S(1)} %dynamic-slice_convert_fusion.2), channel_id=1, source_target_pairs={{0,2},{1,3},{2,0},{3,1},{4,6},{5,7},{6,4},{7,5},{8,10},{9,11},{10,... | collective-permute-start | bytes 2359304 | tf_op jit(solution)/shard_map/ppermute | solution.py:182
  236.7 26.6 %collective-permute-start.20 = (bf16[1024,192]{0,1:T(8,128)(2,1)}, bf16[1024,192]{0,1:T(8,128)(2,1)S(1)}, u32[]{:S(2)}, u32[]{:S(2)}) collective-permute-start(bf16[1024,192]{0,1:T(8,128)(2,1)} %get-tuple-element.59), channel_id=1, source_target_pairs={{0,0},{1,16},{2,8},{3,24},{4,4},{5,20},{6,12},{7,28},{8,1},{9,17},... | collective-permute-start | bytes 1179656 | tf_op jit(solution)/shard_map/ppermute | solution.py:182
  240.0 27.6 %collective-permute-start.21 = (bf16[1024,192]{0,1:T(8,128)(2,1)}, bf16[1024,192]{0,1:T(8,128)(2,1)}, u32[]{:S(2)}, u32[]{:S(2)}) collective-permute-start(bf16[1024,192]{0,1:T(8,128)(2,1)} %get-tuple-element.60), channel_id=1, source_target_pairs={{0,4},{1,20},{2,12},{3,28},{4,0},{5,16},{6,8},{7,24},{8,5},{9,21},... | collective-permute-start | bytes 1179656 | tf_op jit(solution)/shard_map/ppermute | solution.py:182
  273.5 2.4 collective-permute-start.22
  276.2 10.6 %collective-permute-start.23 = (bf16[512,384]{0,1:T(8,128)(2,1)S(1)}, bf16[512,384]{0,1:T(8,128)(2,1)S(1)}, u32[]{:S(2)}, u32[]{:S(2)}) collective-permute-start(bf16[512,384]{0,1:T(8,128)(2,1)S(1)} %dynamic-slice_convert_fusion.3), channel_id=1, source_target_pairs={{0,2},{1,3},{2,0},{3,1},{4,6},{5,7},{6,4},{7,5},{8,10},{9,11},{10,... | collective-permute-start | bytes 1179656 | tf_op jit(solution)/shard_map/ppermute | solution.py:182
  287.0 15.4 %collective-permute-start.24 = (bf16[512,192]{0,1:T(8,128)(2,1)S(1)}, bf16[512,192]{0,1:T(8,128)(2,1)S(1)}, u32[]{:S(2)}, u32[]{:S(2)}) collective-permute-start(bf16[512,192]{0,1:T(8,128)(2,1)S(1)} %get-tuple-element.65), channel_id=1, source_target_pairs={{0,0},{1,16},{2,8},{3,24},{4,4},{5,20},{6,12},{7,28},{8,1},{9,17},... | collective-permute-start | bytes 589832 | tf_op jit(solution)/shard_map/ppermute | solution.py:182
  289.1 16.4 %collective-permute-start.25 = (bf16[512,192]{0,1:T(8,128)(2,1)S(1)}, bf16[512,192]{0,1:T(8,128)(2,1)S(1)}, u32[]{:S(2)}, u32[]{:S(2)}) collective-permute-start(bf16[512,192]{0,1:T(8,128)(2,1)S(1)} %get-tuple-element.66), channel_id=1, source_target_pairs={{0,4},{1,20},{2,12},{3,28},{4,0},{5,16},{6,8},{7,24},{8,5},{9,21},... | collective-permute-start | bytes 589832 | tf_op jit(solution)/shard_map/ppermute | solution.py:182

commit v4 on v3

--- a/solution.py
+++ b/solution.py
@@ -4,6 +4,7 @@
 import jax.numpy as jnp
 from jax import lax
 from jax.experimental import pallas as pl
+from jax.experimental.layout import Layout, with_layout_constraint
 from jax.experimental.pallas import tpu as pltpu
 from jax.sharding import PartitionSpec as P
 
@@ -178,6 +179,46 @@
     )(weights, kernel_t, lrp, lrq)
 
 
+def product_kernel(side_ref, grads_ref, orbitals_ref, give_ref, keep_ref):
+    part = dot(grads_ref[...], orbitals_ref[...])
+    step, half = pl.program_id(0), pl.num_programs(0) // 2
+
+    @pl.when(step < half)
+    def _():
+        give_ref[...] = part.astype(BF16)
+
+    @pl.when(step >= half)
+    def _():
+        keep_ref[...] = part
+
+
+def product_halves(grads, orbitals, side):
+    (rows, depth), size_m = grads.shape, orbitals.shape[1]
+    tile = tile_of(size_m // 2, 384)
+    half = size_m // 2 // tile
+    return pl.pallas_call(
+        product_kernel,
+        out_shape=[
+            jax.ShapeDtypeStruct((rows, size_m // 2), BF16),
+            jax.ShapeDtypeStruct((rows, size_m // 2), F32),
+        ],
+        grid_spec=pltpu.PrefetchScalarGridSpec(
+            num_scalar_prefetch=1,
+            grid=(2 * half,),
+            in_specs=[
+                pl.BlockSpec((rows, depth), lambda n, s: (0, 0), pipeline_mode=pl.Buffered(1)),
+                pl.BlockSpec((depth, tile), lambda n, s: (0, (n + half * (1 - s[0])) % (2 * half))),
+            ],
+            out_specs=[
+                pl.BlockSpec((rows, tile), lambda n, s: (0, jnp.minimum(n, half - 1))),
+                pl.BlockSpec((rows, tile), lambda n, s: (0, jnp.maximum(n - half, 0))),
+            ],
+        ),
+        compiler_params=pltpu.CompilerParams(vmem_limit_bytes=VMEM_LIMIT),
+        cost_estimate=cost(2 * rows * depth * size_m, 2 * (rows + size_m) * depth),
+    )(side, grads, orbitals)
+
+
 def send(x, axes, pairs):
     return lax.ppermute(x, axes, pairs)
 
@@ -212,21 +253,16 @@
     def other(part):
         return send(part, "pt", [(i, i ^ 1) for i in range(npt)])
 
-    def columns_q(begin, chunk):
-        rows = lax.dynamic_slice_in_dim(collocation, x * size_a + begin, chunk, 0)
-        far = send(rows, BOTH, [(put(j, j // 2), put(j, j // 2 ^ 2)) for j in range(nw)])
-        near = jnp.where(me_p == z, rows, far)
-        pairs = [(put(j, j // 2 ^ s), put(j, j // 2 ^ s ^ 1)) for j in range(nw) for s in (0, 2)]
-        return jnp.where(core == z % 2, near, send(near, BOTH, pairs))
-
     def split(part, at, size, axis=1):
         give = lax.dynamic_slice_in_dim(part, (1 - at) * size, size, axis).astype(BF16)
         return give, lax.dynamic_slice_in_dim(part, at * size, size, axis)
 
     tie = lax.optimization_barrier
-    chunks = [(0, 2 * size_a // 3), (2 * size_a // 3, size_a // 3)]
+    sixth = size_a // 6
+    chunks = [(0, 3 * sixth), (4 * sixth, 2 * sixth), (3 * sixth, sixth)]
+    rows = lax.dynamic_slice_in_dim(collocation, x * size_a, size_a, 0)
+    far = send(rows, BOTH, [(put(j, j // 2), put(j, j // 2 ^ 2)) for j in range(nw)])
     own, half = packed(bra, ket, walker_group, group_occupied, core.reshape(1), walker_weight)
-    cols_q = [columns_q(*chunk) for chunk in chunks]
     z1, z3, x0 = along(half, 1), along(half, 3), across(half)
     kernel_t = turned(kernel)
     x0, z1, z3, kernel_t = tie((x0, z1, z3, kernel_t))
@@ -235,19 +271,25 @@
     x2 = across(z2)
     near_four = [own] + [h for part in (x0, z1, z3) for h in (part, other(part))]
     lrp, stack, weight_rows = project(near_four, [width] + [occ] * 6, collocation, 2, 0)
+    x1, x3, x2, weight_rows = tie((x1, x3, x2, weight_rows))
+    far, weight_rows = tie((far, weight_rows))
     first = (lrp, stack, weight_rows)
-    x2, *first = tie((x2, *first))
     far_four = [h for part in (x1, x3, z2, x2) for h in (part, other(part))]
     lrp, stack, weight_rows = project(far_four, [occ] * 8, collocation, 2, 1, first)
     weights = jnp.concatenate([weight_rows[:4, 0], weight_rows[8:12, 0]])
 
-    lrq = dot(jnp.concatenate(cols_q, axis=0), stack, NT).astype(BF16)
+    near = jnp.where(me_p == z, rows, far)
+    pairs = [(put(j, j // 2 ^ s), put(j, j // 2 ^ s ^ 1)) for j in range(nw) for s in (0, 2)]
+    col_q = jnp.where(core == z % 2, near, send(near, BOTH, pairs))
+    lrq = dot(col_q, stack, NT).astype(BF16)
 
     half_m, quarter, eighth = size_m // 2, size_m // 4, size_m // 8
     swap_y = [(i, i ^ 2) for i in range(npt)]
 
     def to_place(part, *later):
-        pieces = [lax.dynamic_slice_in_dim(part, (x ^ t) * eighth, eighth, 1) for t in (0, 1)]
+        row_major = Layout(major_to_minor=(0, 1))
+        part = with_layout_constraint(with_layout_constraint(part, row_major).T, row_major)
+        pieces = [lax.dynamic_slice_in_dim(part, (x ^ t) * eighth, eighth, 0) for t in (0, 1)]
         pieces = tie((*pieces, *later))
         came = []
         for t in (0, 1):
@@ -259,27 +301,30 @@
             came.append(send(pieces[t], BOTH, pairs))
         return pieces, came
 
-    def over_cores(grads):
-        give, keep = split(grads, core, half_m)
+    side = core.reshape(1)
+
+    def over_cores(give, keep):
         return split(keep + other(give).astype(F32), y, quarter)
 
-    (at_0, rows_0), (at_1, rows_1) = chunks
-    middle = stack.shape[0] // 2
-    grads = pair_gradients(weights, kernel_t, lrp, lrq, at_0, rows_0)
-    give, keep = over_cores(dot(grads, stack))
-    give, lrq = tie((give, lrq))
-    got = send(give, "pt", swap_y)
-    early = pair_gradients(weights, kernel_t, lrp, lrq, at_1, rows_1, (0, 4))
-    part = dot(early, stack[:middle])
-    part, got = tie((part, got))
-    pieces, came_0 = to_place((keep + got.astype(F32)).astype(BF16), lrq)
-    late = pair_gradients(weights, kernel_t, lrp, pieces[2], at_1, rows_1, (4, 8))
-    late, *came_0 = tie((late, *came_0))
-    give, keep = over_cores(part + dot(late, stack[middle:]))
-    _, came_1 = to_place((keep + send(give, "pt", swap_y).astype(F32)).astype(BF16))
-
-    ordered = [jnp.where(x == side, came[0], came[1]) for side in (0, 1) for came in (came_0, came_1)]
-    return jnp.concatenate(ordered, axis=0).astype(F32) / jnp.sum(weights)
+    grads = pair_gradients(weights, kernel_t, lrp, lrq, *chunks[0])
+    give_0, keep_0 = over_cores(*product_halves(grads, stack, side))
+    give_0, scale = tie((give_0, weights))
+    got_0 = send(give_0, "pt", swap_y)
+    grads = pair_gradients(scale, kernel_t, lrp, lrq, *chunks[1])
+    give, keep = product_halves(grads, stack, side)
+    keep, got_0 = tie((keep, got_0))
+    pieces, came_0 = to_place((keep_0 + got_0.astype(F32)).astype(BF16), weights)
+    give_1, keep_1 = over_cores(give, keep)
+    give_1, scale = tie((give_1, pieces[2]))
+    got_1 = send(give_1, "pt", swap_y)
+    grads = pair_gradients(scale, kernel_t, lrp, lrq, *chunks[2])
+    _, got_1, *came_0 = tie((grads[:16, :128], got_1, *came_0))
+    pieces, came_1 = to_place((keep_1 + got_1.astype(F32)).astype(BF16), side)
+    give_2, keep_2 = over_cores(*product_halves(grads, stack, pieces[2]))
+    _, came_2 = to_place((keep_2 + send(give_2, "pt", swap_y).astype(F32)).astype(BF16))
+
+    ordered = [jnp.where(x == side, came[0], came[1]) for side in (0, 1) for came in (came_0, came_2, came_1)]
+    return (jnp.concatenate(ordered, axis=1).astype(F32) / jnp.sum(weights)).T
 
 
 def on_device_any(nw, own, collocation, kernel, walker_weight):

time: 313 us -> 335 us (1.070)
  Pallas kernels: 152 us -> 182 us
  matrix products: 39.3 us -> 18.4 us
  waiting for transfers between devices: 44.9 us -> 59.5 us
  local copies, waits for them, and re-layouts: 13 us -> 6.79 us
  starting transfers between devices: 39.9 us -> 44 us
    pallas_call x0 -> x3, Pallas kernels: none -> 30.1 us  [product_halves(): pl.pallas_call(product_kernel, out_shape=[jax.ShapeDtypeStruct((rows, siz...]
    dot_general x4 -> x1, matrix products: 39.3 us -> 18.4 us  [dot(): return lax.dot_general(a, b, dims, preferred_element_type=F32)]
    ppermute x26 -> x28, waiting for transfers between devices: 44.9 us -> 59.5 us  [send(): return lax.ppermute(x, axes, pairs)]
    ppermute x26 -> x28, starting transfers between devices: 39.9 us -> 44 us  [send(): return lax.ppermute(x, axes, pairs)]
    select_n x6 -> x1, other arithmetic: 7.97 us -> 7.36 us  [on_device_8x4(): near = jnp.where(me_p == z, rows, far)]
  transfers between devices with their start and end apart: 26 -> 28, of which waited for: 10 -> 11; matrix products, arithmetic and copies ran while one was open for 6% -> 1% of each run, Pallas kernels for 29% -> 35%
where the time goes in v4:
time: 335 us; the launch traced here: 330 us
  Pallas kernels  182 us (54%)
  waiting for transfers between devices  59.5 us (18%)
  starting transfers between devices  44 us (13%)
  matrix products  18.4 us (5%)
  other arithmetic  15.9 us (5%)
  local copies, waits for them, and re-layouts  6.79 us (2%)
    pallas_call x3, Pallas kernels, pair_gradients(): pl.pallas_call(functools.partial(pair_kernel, sub, first), out_shape=jax....  98.9 us
    ppermute x28, waiting for transfers between devices, send(): return lax.ppermute(x, axes, pairs)  59.5 us
    ppermute x28, starting transfers between devices, send(): return lax.ppermute(x, axes, pairs)  44 us
    pallas_call x2, Pallas kernels, project(): pl.pallas_call(functools.partial(project_kernel, tuple(rows_each), len(be...  35.9 us
    pallas_call x3, Pallas kernels, product_halves(): pl.pallas_call(product_kernel, out_shape=[jax.ShapeDtypeStruct((rows, siz...  30.1 us
    dot_general x1, matrix products, dot(): return lax.dot_general(a, b, dims, preferred_element_type=F32)  18.4 us
    pallas_call x1, Pallas kernels, turned(): pl.pallas_call(turn_kernel, out_shape=jax.ShapeDtypeStruct((cols, rows),...  14.7 us
    select_n x1, other arithmetic, on_device_8x4(): near = jnp.where(me_p == z, rows, far)  7.36 us
  transfers between devices with their start and end apart: 28, of which 11 were waited for; matrix products, arithmetic and copies ran while one was open for 1% of the time, Pallas kernels for 35%

profile of v4, /device:TPU:1, one launch (start us, length us, event | category | flops | bytes accessed | tf_op | source)
XLA Modules:
  0.0 329.6 jit_solution(2894243549618424340)
XLA Ops:
  0.0 4.8 %constant_dynamic-slice_fusion.6 = bf16[1536,1536]{1,0:T(8,128)(2,1)} fusion(bf16[3072,1536]{1,0:T(8,128)(2,1)} %refs_8_.1, s32[]{:T(128)S(6)} %select_n.104), kind=kLoop, calls=%fused_computation.26 | loop fusion | bytes 9437188 | tf_op jit(solution)/shard_map/dynamic_slice | solution.py:263
  4.8 2.9 collective-permute-start.14
  8.9 2.6 shard_map.73
  11.5 4.6 %collective-permute-start.2 = (bf16[176,1536]{1,0:T(8,128)(2,1)}, bf16[176,1536]{1,0:T(8,128)(2,1)S(1)}, u32[]{:S(2)}, u32[]{:S(2)}) collective-permute-start(bf16[176,1536]{1,0:T(8,128)(2,1)} %get-tuple-element.49), channel_id=1, source_target_pairs={{0,8},{4,12},{8,16},{12,20},{16,24},{20,28},{24,0},{28,4},{1,9},{5... | collective-permute-start | bytes 1622024 | tf_op jit(solution)/shard_map/ppermute | solution.py:223
  16.1 1.2 collective-permute-start
  17.3 14.7 %shard_map.74.kt_ref = bf16[1536,3072]{1,0:T(8,128)(2,1)} custom-call(bf16[3072,1536]{1,0:T(8,128)(2,1)} %in_ref.1), custom_call_target="tpu_custom_call" | custom-call | bytes 47185920 | tf_op jit(solution)/shard_map/pallas_call | solution.py:37
  32.0 7.9 %collective-permute-done.1.refs_3_ = bf16[176,1536]{1,0:T(8,128)(2,1)S(1)} collective-permute-done((bf16[176,1536]{1,0:T(8,128)(2,1)}, bf16[176,1536]{1,0:T(8,128)(2,1)S(1)}, u32[]{:S(2)}, u32[]{:S(2)}) %collective-permute-start.1) | collective-permute-done | bytes 540704 | tf_op jit(solution)/shard_map/ppermute | solution.py:223
  39.9 3.8 %collective-permute-start.5 = (bf16[176,1536]{1,0:T(8,128)(2,1)S(1)}, bf16[176,1536]{1,0:T(8,128)(2,1)S(1)}, u32[]{:S(2)}, u32[]{:S(2)}) collective-permute-start(bf16[176,1536]{1,0:T(8,128)(2,1)S(1)} %collective-permute-done.1.refs_3_), channel_id=1, source_target_pairs={{0,24},{4,28},{8,0},{12,4},{16,8},{20,12},{24,16},{28,20},{1,25},{... | collective-permute-start | bytes 1622024 | tf_op jit(solution)/shard_map/ppermute | solution.py:223
  43.7 0.7 collective-permute-start.7
  44.4 10.6 %collective-permute-done.5.refs_4_ = bf16[176,1536]{1,0:T(8,128)(2,1)S(1)} collective-permute-done((bf16[176,1536]{1,0:T(8,128)(2,1)S(1)}, bf16[176,1536]{1,0:T(8,128)(2,1)S(1)}, u32[]{:S(2)}, u32[]{:S(2)}) %collective-permute-start.5) | collective-permute-done | bytes 540704 | tf_op jit(solution)/shard_map/ppermute | solution.py:223
  55.0 1.2 collective-permute-start.8
  56.2 1.2 collective-permute-start.4
  57.4 0.3 collective-permute-start.3
  57.7 0.5 copy-done.9
  58.2 0.9 collective-permute-start.6
  59.1 17.9 %shard_map.75 = (bf16[2560,3072]{1,0:T(8,128)(2,1)}, bf16[2560,1536]{1,0:T(8,128)(2,1)}, f32[16,128]{1,0:T(8,128)}) custom-call(bf16[336,1536]{1,0:T(8,128)(2,1)} %get-tuple-element.53.refs_0_, bf16[176,1536]{1,0:T(8,128)(2,1)} %copy-done.7, bf16[176,1536]{1,0:T(8,128)(2,1)} %copy-done.9, bf16[176,1536]{1,0:T(8,128)(2,1)} %copy-done.6, ...), custom_call_target="tpu_custom_call" | custom-call | flops 18119393280 | bytes 9437184 | tf_op jit(solution)/shard_map/pallas_call | solution.py:115
  77.1 4.0 %collective-permute-done.3.refs_0_ = bf16[176,1536]{1,0:T(8,128)(2,1)S(1)} collective-permute-done((bf16[176,1536]{1,0:T(8,128)(2,1)S(1)}, bf16[176,1536]{1,0:T(8,128)(2,1)S(1)}, u32[]{:S(2)}, u32[]{:S(2)}) %collective-permute-start.3) | collective-permute-done | bytes 540704 | tf_op jit(solution)/shard_map/ppermute | solution.py:223
  81.1 11.6 %collective-permute-done.6.refs_6_ = bf16[176,1536]{1,0:T(8,128)(2,1)S(1)} collective-permute-done((bf16[176,1536]{1,0:T(8,128)(2,1)S(1)}, bf16[176,1536]{1,0:T(8,128)(2,1)S(1)}, u32[]{:S(2)}, u32[]{:S(2)}) %collective-permute-start.6) | collective-permute-done | bytes 540704 | tf_op jit(solution)/shard_map/ppermute | solution.py:223
  92.7 7.4 %broadcast_select_fusion = bf16[1536,1536]{1,0:T(8,128)(2,1)} fusion(bf16[1536,1536]{1,0:T(8,128)(2,1)} %collective-permute-done.14, pred[]{:T(512)S(6)} %eq.22, bf16[3072,1536]{1,0:T(8,128)(2,1)} %refs_8_.1, s32[]{:T(128)S(6)} %select_n.104), kind=kLoop, calls=%fused_computation.2 | loop fusion | flops 2359296 | bytes 14155781 | tf_op jit(solution)/shard_map/jit(_where)/select_n | solution.py:281
  100.1 1.8 collective-permute-start.15
  101.9 3.4 %collective-permute-start.12 = (bf16[176,1536]{1,0:T(8,128)(2,1)S(1)}, bf16[176,1536]{1,0:T(8,128)(2,1)S(1)}, u32[]{:S(2)}, u32[]{:S(2)}) collective-permute-start(bf16[176,1536]{1,0:T(8,128)(2,1)S(1)} %collective-permute-done.5.refs_4_), channel_id=1, source_target_pairs={{0,1},{1,0},{2,3},{3,2},{4,5},{5,4},{6,7},{7,6},{8,9},{9,8},{10,11... | collective-permute-start | bytes 1622024 | tf_op jit(solution)/shard_map/ppermute | solution.py:223
  105.3 0.1 collective-permute-start.10
  105.4 0.4 collective-permute-start.11
  105.8 0.1 collective-permute-start.13
  105.9 5.5 %collective-permute-done.12.refs_5_ = bf16[176,1536]{1,0:T(8,128)(2,1)S(1)} collective-permute-done((bf16[176,1536]{1,0:T(8,128)(2,1)S(1)}, bf16[176,1536]{1,0:T(8,128)(2,1)S(1)}, u32[]{:S(2)}, u32[]{:S(2)}) %collective-permute-start.12) | collective-permute-done | bytes 540704 | tf_op jit(solution)/shard_map/ppermute | solution.py:223
  111.4 1.5 collective-permute-done.10.refs_1_
  113.0 0.1 collective-permute-done.13.refs_7_
  113.1 0.7 copy-done.10
  113.8 17.9 %shard_map.76 = (bf16[2560,3072]{1,0:T(8,128)(2,1)}, bf16[2560,1536]{1,0:T(8,128)(2,1)}, f32[16,128]{1,0:T(8,128)}) custom-call(bf16[176,1536]{1,0:T(8,128)(2,1)} %copy-done.3, bf16[176,1536]{1,0:T(8,128)(2,1)} %copy-done.10, bf16[176,1536]{1,0:T(8,128)(2,1)} %copy-done.2, ...), custom_call_target="tpu_custom_call", output_to_operand_aliasing={{0}: (9, {}), {1}: (10, {}), {2}: (11, {})} | custom-call | flops 18119393280 | bytes 9437184 | tf_op jit(solution)/shard_map/pallas_call | solution.py:115
  131.7 1.3 slice_reduce_fusion
  133.0 0.6 pad_maximum_fusion.weight_ref
  133.6 18.4 %convolution_convert_fusion.lrq_ref = bf16[1536,2560]{1,0:T(8,128)(2,1)} fusion(bf16[2560,1536]{1,0:T(8,128)(2,1)} %get-tuple-element.69.orbitals_ref, bf16[1536,1536]{1,0:T(8,128)(2,1)} %broadcast_select_fusion, bf16[1536,1536]{1,0:T(8,128)(2,1)} %collective-permute-done.15, pred[]{:T(512)S(6)} %eq.21), kind=kOutput, calls=%fused_computation | convolution fusion | flops 12085886976 | bytes 25165824 | tf_op jit(solution)/shard_map/dot_general | solution.py:23
  152.0 47.4 %shard_map.77.grads_ref = bf16[768,2560]{1,0:T(8,128)(2,1)} custom-call(f32[8]{0:T(128)} %pad_maximum_fusion.weight_ref, bf16[1536,3072]{1,0:T(8,128)(2,1)} %shard_map.74.kt_ref, bf16[2560,3072]{1,0:T(8,128)(2,1)} %get-tuple-element.67.lrp_ref, bf16[1536,2560]{1,0:T(8,128)(2,1)} %convolution_convert_fusion.lrq_ref), custom_call_target="tpu_custom_call" | custom-call | flops 38654705664 | bytes 34603008 | tf_op jit(solution)/shard_map/pallas_call | solution.py:162
  199.4 13.1 %shard_map.78 = (bf16[768,768]{1,0:T(8,128)(2,1)}, f32[768,768]{1,0:T(8,128)}) custom-call(s32[1]{0:T(128)} %bitcast.side_ref, bf16[768,2560]{1,0:T(8,128)(2,1)} %shard_map.77.grads_ref, bf16[2560,1536]{1,0:T(8,128)(2,1)} %get-tuple-element.69.orbitals_ref), custom_call_target="tpu_custom_call" | custom-call | flops 6039797760 | bytes 11796480 | tf_op jit(solution)/shard_map/pallas_call | solution.py:199
  212.5 0.1 collective-permute-start.16
  212.7 2.9 collective-permute-done.16
  215.6 1.9 convert_add_fusion
  217.5 0.1 dynamic-slice_convert_fusion
  217.6 0.8 collective-permute-start.17
  218.3 32.5 %shard_map.79.grads_ref = bf16[512,2560]{1,0:T(8,128)(2,1)} custom-call(f32[8]{0:T(128)} %pad_maximum_fusion.weight_ref, bf16[1536,3072]{1,0:T(8,128)(2,1)} %shard_map.74.kt_ref, bf16[2560,3072]{1,0:T(8,128)(2,1)} %get-tuple-element.67.lrp_ref, bf16[1536,2560]{1,0:T(8,128)(2,1)} %convolution_convert_fusion.lrq_ref), custom_call_target="tpu_custom_call" | custom-call | flops 25769803776 | bytes 28311552 | tf_op jit(solution)/shard_map/pallas_call | solution.py:162
  250.9 9.8 %shard_map.80 = (bf16[512,768]{1,0:T(8,128)(2,1)}, f32[512,768]{1,0:T(8,128)}) custom-call(s32[1]{0:T(128)} %bitcast.side_ref, bf16[512,2560]{1,0:T(8,128)(2,1)} %shard_map.79.grads_ref, bf16[2560,1536]{1,0:T(8,128)(2,1)} %get-tuple-element.69.orbitals_ref), custom_call_target="tpu_custom_call" | custom-call | flops 4026531840 | bytes 10485760 | tf_op jit(solution)/shard_map/pallas_call | solution.py:199
  260.7 0.4 collective-permute-start.18
  261.1 0.1 add_convert_fusion
  261.3 0.3 copy.14
  261.6 2.8 collective-permute-start.20
  264.4 3.3 %collective-permute-start.21 = (bf16[192,768]{1,0:T(8,128)(2,1)S(1)}, bf16[192,768]{1,0:T(8,128)(2,1)S(1)}, u32[]{:S(2)}, u32[]{:S(2)}) collective-permute-start(bf16[192,768]{1,0:T(8,128)(2,1)S(1)} %get-tuple-element.81), channel_id=1, source_target_pairs={{0,4},{1,20},{2,12},{3,28},{4,0},{5,16},{6,8},{7,24},{8,5},{9,21},... | collective-permute-start | bytes 884744 | tf_op jit(solution)/shard_map/ppermute | solution.py:223
  267.7 1.3 convert_add_fusion.1
  269.1 3.0 collective-permute-start.19
  272.1 18.9 %shard_map.81.grads_ref = bf16[256,2560]{1,0:T(8,128)(2,1)} custom-call(f32[8]{0:T(128)} %pad_maximum_fusion.weight_ref, bf16[1536,3072]{1,0:T(8,128)(2,1)} %shard_map.74.kt_ref, bf16[2560,3072]{1,0:T(8,128)(2,1)} %get-tuple-element.67.lrp_ref, bf16[1536,2560]{1,0:T(8,128)(2,1)} %convolution_convert_fusion.lrq_ref), custom_call_target="tpu_custom_call" | custom-call | flops 12884901888 | bytes 22020096 | tf_op jit(solution)/shard_map/pallas_call | solution.py:162
  291.0 0.1 add_convert_fusion.1
  291.1 0.2 copy.15
  291.3 7.2 %shard_map.82 = (bf16[256,768]{1,0:T(8,128)(2,1)}, f32[256,768]{1,0:T(8,128)}) custom-call(s32[1]{0:T(128)} %bitcast.side_ref, bf16[256,2560]{1,0:T(8,128)(2,1)} %shard_map.81.grads_ref, bf16[2560,1536]{1,0:T(8,128)(2,1)} %get-tuple-element.69.orbitals_ref), custom_call_target="tpu_custom_call" | custom-call | flops 2013265920 | bytes 9175040 | tf_op jit(solution)/shard_map/pallas_call | solution.py:199
  298.5 1.9 collective-permute-done.22
  300.4 1.2 convert_add_fusion.2
  301.7 0.1 collective-permute-start.23
  303.0 3.2 collective-permute-start.26
  306.1 2.9 collective-permute-start.27
  309.1 0.1 copy.16
  309.3 2.3 collective-permute-start.24
  311.6 2.4 collective-permute-start.25
  314.0 0.1 select_dynamic-update-slice_fusion.1
  314.1 11.7 %collective-permute-done.24 = bf16[192,256]{1,0:T(8,128)(2,1)S(1)} collective-permute-done((bf16[192,256]{1,0:T(8,128)(2,1)S(1)}, bf16[192,256]{1,0:T(8,128)(2,1)S(1)}, u32[]{:S(2)}, u32[]{:S(2)}) %collective-permute-start.24) | collective-permute-done | bytes 98336 | tf_op jit(solution)/shard_map/ppermute | solution.py:223
  325.7 1.6 collective-permute-done.25
  327.6 1.7 divide_bitcast_fusion
  (51 shorter events, 0.6 us)
Async XLA Ops:
  4.8 88.0 %collective-permute-start.14 = (bf16[1536,1536]{1,0:T(8,128)(2,1)}, bf16[1536,1536]{1,0:T(8,128)(2,1)}, u32[]{:S(2)}, u32[]{:S(2)}) collective-permute-start(bf16[1536,1536]{1,0:T(8,128)(2,1)} %constant_dynamic-slice_fusion.6), channel_id=1, source_target_pairs={{0,2},{4,6},{9,11},{13,15},{18,16},{22,20},{27,25},{31,29}} | collective-permute-start | bytes 14155784 | tf_op jit(solution)/shard_map/ppermute | solution.py:223
  11.5 20.5 %collective-permute-start.2 = (bf16[176,1536]{1,0:T(8,128)(2,1)}, bf16[176,1536]{1,0:T(8,128)(2,1)S(1)}, u32[]{:S(2)}, u32[]{:S(2)}) collective-permute-start(bf16[176,1536]{1,0:T(8,128)(2,1)} %get-tuple-element.49), channel_id=1, source_target_pairs={{0,8},{4,12},{8,16},{12,20},{16,24},{20,28},{24,0},{28,4},{1,9},{5... | collective-permute-start | bytes 1622024 | tf_op jit(solution)/shard_map/ppermute | solution.py:223
  16.1 23.8 %collective-permute-start.1 = (bf16[176,1536]{1,0:T(8,128)(2,1)}, bf16[176,1536]{1,0:T(8,128)(2,1)S(1)}, u32[]{:S(2)}, u32[]{:S(2)}) collective-permute-start(bf16[176,1536]{1,0:T(8,128)(2,1)} %get-tuple-element.49), channel_id=1, source_target_pairs={{0,24},{4,28},{8,0},{12,4},{16,8},{20,12},{24,16},{28,20},{1,25},{... | collective-permute-start | bytes 1622024 | tf_op jit(solution)/shard_map/ppermute | solution.py:223
  16.1 23.8 %collective-permute-start = (bf16[176,1536]{1,0:T(8,128)(2,1)}, bf16[176,1536]{1,0:T(8,128)(2,1)S(1)}, u32[]{:S(2)}, u32[]{:S(2)}) collective-permute-start(bf16[176,1536]{1,0:T(8,128)(2,1)} %get-tuple-element.49), channel_id=1, source_target_pairs={{0,4},{4,0},{8,12},{12,8},{16,20},{20,16},{24,28},{28,24},{1,5},{5... | collective-permute-start | bytes 1622024 | tf_op jit(solution)/shard_map/ppermute | solution.py:223
  32.0 27.1 %copy-start.5 = (bf16[176,1536]{1,0:T(8,128)(2,1)}, bf16[176,1536]{1,0:T(8,128)(2,1)S(1)}, u32[]{:S(2)}) copy-start(bf16[176,1536]{1,0:T(8,128)(2,1)S(1)} %collective-permute-done.2.refs_5_) | copy-start | bytes 1622020
  39.9 19.2 %copy-start.6 = (bf16[176,1536]{1,0:T(8,128)(2,1)}, bf16[176,1536]{1,0:T(8,128)(2,1)S(1)}, u32[]{:S(2)}) copy-start(bf16[176,1536]{1,0:T(8,128)(2,1)S(1)} %collective-permute-done.1.refs_3_) | copy-start | bytes 1622020
  39.9 17.5 %copy-start.7 = (bf16[176,1536]{1,0:T(8,128)(2,1)}, bf16[176,1536]{1,0:T(8,128)(2,1)S(1)}, u32[]{:S(2)}) copy-start(bf16[176,1536]{1,0:T(8,128)(2,1)S(1)} %collective-permute-done.refs_1_) | copy-start | bytes 1622020
  39.9 15.0 %collective-permute-start.5 = (bf16[176,1536]{1,0:T(8,128)(2,1)S(1)}, bf16[176,1536]{1,0:T(8,128)(2,1)S(1)}, u32[]{:S(2)}, u32[]{:S(2)}) collective-permute-start(bf16[176,1536]{1,0:T(8,128)(2,1)S(1)} %collective-permute-done.1.refs_3_), channel_id=1, source_target_pairs={{0,24},{4,28},{8,0},{12,4},{16,8},{20,12},{24,16},{28,20},{1,25},{... | collective-permute-start | bytes 1622024 | tf_op jit(solution)/shard_map/ppermute | solution.py:223
  43.7 13.7 %collective-permute-start.7 = (bf16[176,1536]{1,0:T(8,128)(2,1)S(1)}, bf16[176,1536]{1,0:T(8,128)(2,1)S(1)}, u32[]{:S(2)}, u32[]{:S(2)}) collective-permute-start(bf16[176,1536]{1,0:T(8,128)(2,1)S(1)} %collective-permute-done.refs_1_), channel_id=1, source_target_pairs={{0,1},{1,0},{2,3},{3,2},{4,5},{5,4},{6,7},{7,6},{8,9},{9,8},{10,11... | collective-permute-start | bytes 1622024 | tf_op jit(solution)/shard_map/ppermute | solution.py:223
  55.0 46.9 %copy-start.1 = (bf16[176,1536]{1,0:T(8,128)(2,1)}, bf16[176,1536]{1,0:T(8,128)(2,1)S(1)}, u32[]{:S(2)}) copy-start(bf16[176,1536]{1,0:T(8,128)(2,1)S(1)} %collective-permute-done.5.refs_4_) | copy-start | bytes 1622020
  55.0 3.3 collective-permute-start.8
  56.2 2.9 collective-permute-start.9
  56.2 20.9 %collective-permute-start.4 = (bf16[176,1536]{1,0:T(8,128)(2,1)S(1)}, bf16[176,1536]{1,0:T(8,128)(2,1)S(1)}, u32[]{:S(2)}, u32[]{:S(2)}) collective-permute-start(bf16[176,1536]{1,0:T(8,128)(2,1)S(1)} %collective-permute-done.2.refs_5_), channel_id=1, source_target_pairs={{0,4},{4,0},{8,12},{12,8},{16,20},{20,16},{24,28},{28,24},{1,5},{5... | collective-permute-start | bytes 1622024 | tf_op jit(solution)/shard_map/ppermute | solution.py:223
  57.4 0.8 copy-start.9
  57.4 23.7 %collective-permute-start.3 = (bf16[176,1536]{1,0:T(8,128)(2,1)S(1)}, bf16[176,1536]{1,0:T(8,128)(2,1)S(1)}, u32[]{:S(2)}, u32[]{:S(2)}) collective-permute-start(bf16[176,1536]{1,0:T(8,128)(2,1)S(1)} %collective-permute-done.1.refs_3_), channel_id=1, source_target_pairs={{0,4},{4,0},{8,12},{12,8},{16,20},{20,16},{24,28},{28,24},{1,5},{5... | collective-permute-start | bytes 1622024 | tf_op jit(solution)/shard_map/ppermute | solution.py:223
  58.2 34.5 %collective-permute-start.6 = (bf16[176,1536]{1,0:T(8,128)(2,1)S(1)}, bf16[176,1536]{1,0:T(8,128)(2,1)S(1)}, u32[]{:S(2)}, u32[]{:S(2)}) collective-permute-start(bf16[176,1536]{1,0:T(8,128)(2,1)S(1)} %collective-permute-done.5.refs_4_), channel_id=1, source_target_pairs={{0,4},{4,0},{8,12},{12,8},{16,20},{20,16},{24,28},{28,24},{1,5},{5... | collective-permute-start | bytes 1622024 | tf_op jit(solution)/shard_map/ppermute | solution.py:223
  77.1 28.3 %copy-start.2 = (bf16[176,1536]{1,0:T(8,128)(2,1)}, bf16[176,1536]{1,0:T(8,128)(2,1)S(1)}, u32[]{:S(2)}) copy-start(bf16[176,1536]{1,0:T(8,128)(2,1)S(1)} %collective-permute-done.4.refs_2_) | copy-start | bytes 1622020
  81.1 24.2 %copy-start.3 = (bf16[176,1536]{1,0:T(8,128)(2,1)}, bf16[176,1536]{1,0:T(8,128)(2,1)S(1)}, u32[]{:S(2)}) copy-start(bf16[176,1536]{1,0:T(8,128)(2,1)S(1)} %collective-permute-done.3.refs_0_) | copy-start | bytes 1622020
  92.7 13.1 %copy-start.4 = (bf16[176,1536]{1,0:T(8,128)(2,1)}, bf16[176,1536]{1,0:T(8,128)(2,1)S(1)}, u32[]{:S(2)}) copy-start(bf16[176,1536]{1,0:T(8,128)(2,1)S(1)} %collective-permute-done.6.refs_6_) | copy-start | bytes 1622020
  100.1 33.5 %collective-permute-start.15 = (bf16[1536,1536]{1,0:T(8,128)(2,1)}, bf16[1536,1536]{1,0:T(8,128)(2,1)}, u32[]{:S(2)}, u32[]{:S(2)}) collective-permute-start(bf16[1536,1536]{1,0:T(8,128)(2,1)} %broadcast_select_fusion), channel_id=1, source_target_pairs={{0,1},{2,3},{4,5},{6,7},{9,8},{11,10},{13,12},{15,14},{18,19},{16,... | collective-permute-start | bytes 14155784 | tf_op jit(solution)/shard_map/ppermute | solution.py:223
  101.9 9.5 %collective-permute-start.12 = (bf16[176,1536]{1,0:T(8,128)(2,1)S(1)}, bf16[176,1536]{1,0:T(8,128)(2,1)S(1)}, u32[]{:S(2)}, u32[]{:S(2)}) collective-permute-start(bf16[176,1536]{1,0:T(8,128)(2,1)S(1)} %collective-permute-done.5.refs_4_), channel_id=1, source_target_pairs={{0,1},{1,0},{2,3},{3,2},{4,5},{5,4},{6,7},{7,6},{8,9},{9,8},{10,11... | collective-permute-start | bytes 1622024 | tf_op jit(solution)/shard_map/ppermute | solution.py:223
  105.3 7.7 %collective-permute-start.10 = (bf16[176,1536]{1,0:T(8,128)(2,1)S(1)}, bf16[176,1536]{1,0:T(8,128)(2,1)S(1)}, u32[]{:S(2)}, u32[]{:S(2)}) collective-permute-start(bf16[176,1536]{1,0:T(8,128)(2,1)S(1)} %collective-permute-done.3.refs_0_), channel_id=1, source_target_pairs={{0,1},{1,0},{2,3},{3,2},{4,5},{5,4},{6,7},{7,6},{8,9},{9,8},{10,11... | collective-permute-start | bytes 1622024 | tf_op jit(solution)/shard_map/ppermute | solution.py:223
  105.4 7.6 %collective-permute-start.11 = (bf16[176,1536]{1,0:T(8,128)(2,1)S(1)}, bf16[176,1536]{1,0:T(8,128)(2,1)}, u32[]{:S(2)}, u32[]{:S(2)}) collective-permute-start(bf16[176,1536]{1,0:T(8,128)(2,1)S(1)} %collective-permute-done.4.refs_2_), channel_id=1, source_target_pairs={{0,1},{1,0},{2,3},{3,2},{4,5},{5,4},{6,7},{7,6},{8,9},{9,8},{10,11... | collective-permute-start | bytes 1622024 | tf_op jit(solution)/shard_map/ppermute | solution.py:223
  105.8 7.3 %collective-permute-start.13 = (bf16[176,1536]{1,0:T(8,128)(2,1)S(1)}, bf16[176,1536]{1,0:T(8,128)(2,1)}, u32[]{:S(2)}, u32[]{:S(2)}) collective-permute-start(bf16[176,1536]{1,0:T(8,128)(2,1)S(1)} %collective-permute-done.6.refs_6_), channel_id=1, source_target_pairs={{0,1},{1,0},{2,3},{3,2},{4,5},{5,4},{6,7},{7,6},{8,9},{9,8},{10,11... | collective-permute-start | bytes 1622024 | tf_op jit(solution)/shard_map/ppermute | solution.py:223
  111.4 1.7 copy-start.8
  113.0 0.8 copy-start.10
  212.5 3.1 collective-permute-start.16
  217.6 43.6 %collective-permute-start.17 = (bf16[768,384]{1,0:T(8,128)(2,1)S(1)}, bf16[768,384]{1,0:T(8,128)(2,1)S(1)}, u32[]{:S(2)}, u32[]{:S(2)}) collective-permute-start(bf16[768,384]{1,0:T(8,128)(2,1)S(1)} %dynamic-slice_convert_fusion), channel_id=1, source_target_pairs={{0,2},{1,3},{2,0},{3,1},{4,6},{5,7},{6,4},{7,5},{8,10},{9,11},{10,... | collective-permute-start | bytes 1769480 | tf_op jit(solution)/shard_map/ppermute | solution.py:223
  260.7 7.0 %collective-permute-start.18 = (bf16[512,768]{1,0:T(8,128)(2,1)}, bf16[512,768]{1,0:T(8,128)(2,1)}, u32[]{:S(2)}, u32[]{:S(2)}) collective-permute-start(bf16[512,768]{1,0:T(8,128)(2,1)} %get-tuple-element.76), channel_id=1, source_target_pairs={{0,1},{1,0},{2,3},{3,2},{4,5},{5,4},{6,7},{7,6},{8,9},{9,8},{10,11... | collective-permute-start | bytes 2359304 | tf_op jit(solution)/shard_map/ppermute | solution.py:223
  261.3 6.5 %copy-start = (f32[512,768]{1,0:T(8,128)S(1)}, f32[512,768]{1,0:T(8,128)}, u32[]{:S(2)}) copy-start(f32[512,768]{1,0:T(8,128)} %get-tuple-element.75) | copy-start | bytes 4718596
  261.6 29.4 %collective-permute-start.20 = (bf16[192,768]{1,0:T(8,128)(2,1)S(1)}, bf16[192,768]{1,0:T(8,128)(2,1)S(1)}, u32[]{:S(2)}, u32[]{:S(2)}) collective-permute-start(bf16[192,768]{1,0:T(8,128)(2,1)S(1)} %get-tuple-element.80), channel_id=1, source_target_pairs={{0,0},{1,16},{2,8},{3,24},{4,4},{5,20},{6,12},{7,28},{8,1},{9,17},... | collective-permute-start | bytes 884744 | tf_op jit(solution)/shard_map/ppermute | solution.py:223
  264.4 26.6 %collective-permute-start.21 = (bf16[192,768]{1,0:T(8,128)(2,1)S(1)}, bf16[192,768]{1,0:T(8,128)(2,1)S(1)}, u32[]{:S(2)}, u32[]{:S(2)}) collective-permute-start(bf16[192,768]{1,0:T(8,128)(2,1)S(1)} %get-tuple-element.81), channel_id=1, source_target_pairs={{0,4},{1,20},{2,12},{3,28},{4,0},{5,16},{6,8},{7,24},{8,5},{9,21},... | collective-permute-start | bytes 884744 | tf_op jit(solution)/shard_map/ppermute | solution.py:223
  269.1 21.9 %collective-permute-start.19 = (bf16[512,384]{1,0:T(8,128)(2,1)S(1)}, bf16[512,384]{1,0:T(8,128)(2,1)S(1)}, u32[]{:S(2)}, u32[]{:S(2)}) collective-permute-start(bf16[512,384]{1,0:T(8,128)(2,1)S(1)} %dynamic-slice_convert_fusion.1), channel_id=1, source_target_pairs={{0,2},{1,3},{2,0},{3,1},{4,6},{5,7},{6,4},{7,5},{8,10},{9,11},{10,... | collective-permute-start | bytes 1179656 | tf_op jit(solution)/shard_map/ppermute | solution.py:223
  298.5 1.9 collective-permute-start.22
  301.7 7.4 %collective-permute-start.23 = (bf16[256,384]{1,0:T(8,128)(2,1)S(1)}, bf16[256,384]{1,0:T(8,128)(2,1)S(1)}, u32[]{:S(2)}, u32[]{:S(2)}) collective-permute-start(bf16[256,384]{1,0:T(8,128)(2,1)S(1)} %dynamic-slice_convert_fusion.2), channel_id=1, source_target_pairs={{0,2},{1,3},{2,0},{3,1},{4,6},{5,7},{6,4},{7,5},{8,10},{9,11},{10,... | collective-permute-start | bytes 589832 | tf_op jit(solution)/shard_map/ppermute | solution.py:223
  303.0 24.4 %collective-permute-start.26 = (bf16[192,512]{1,0:T(8,128)(2,1)S(1)}, bf16[192,512]{1,0:T(8,128)(2,1)S(1)}, u32[]{:S(2)}, u32[]{:S(2)}) collective-permute-start(bf16[192,512]{1,0:T(8,128)(2,1)S(1)} %get-tuple-element.91), channel_id=1, source_target_pairs={{0,0},{1,16},{2,8},{3,24},{4,4},{5,20},{6,12},{7,28},{8,1},{9,17},... | collective-permute-start | bytes 589832 | tf_op jit(solution)/shard_map/ppermute | solution.py:223
  306.1 21.3 %collective-permute-start.27 = (bf16[192,512]{1,0:T(8,128)(2,1)S(1)}, bf16[192,512]{1,0:T(8,128)(2,1)S(1)}, u32[]{:S(2)}, u32[]{:S(2)}) collective-permute-start(bf16[192,512]{1,0:T(8,128)(2,1)S(1)} %get-tuple-element.92), channel_id=1, source_target_pairs={{0,4},{1,20},{2,12},{3,28},{4,0},{5,16},{6,8},{7,24},{8,5},{9,21},... | collective-permute-start | bytes 589832 | tf_op jit(solution)/shard_map/ppermute | solution.py:223
  309.3 16.5 %collective-permute-start.24 = (bf16[192,256]{1,0:T(8,128)(2,1)S(1)}, bf16[192,256]{1,0:T(8,128)(2,1)S(1)}, u32[]{:S(2)}, u32[]{:S(2)}) collective-permute-start(bf16[192,256]{1,0:T(8,128)(2,1)S(1)} %get-tuple-element.89), channel_id=1, source_target_pairs={{0,0},{1,16},{2,8},{3,24},{4,4},{5,20},{6,12},{7,28},{8,1},{9,17},... | collective-permute-start | bytes 294920 | tf_op jit(solution)/shard_map/ppermute | solution.py:223
  311.6 15.7 %collective-permute-start.25 = (bf16[192,256]{1,0:T(8,128)(2,1)S(1)}, bf16[192,256]{1,0:T(8,128)(2,1)S(1)}, u32[]{:S(2)}, u32[]{:S(2)}) collective-permute-start(bf16[192,256]{1,0:T(8,128)(2,1)S(1)} %get-tuple-element.90), channel_id=1, source_target_pairs={{0,4},{1,20},{2,12},{3,28},{4,0},{5,16},{6,8},{7,24},{8,5},{9,21},... | collective-permute-start | bytes 294920 | tf_op jit(solution)/shard_map/ppermute | solution.py:223

commit v5 on v3

--- a/solution.py
+++ b/solution.py
@@ -224,19 +224,21 @@
         return give, lax.dynamic_slice_in_dim(part, at * size, size, axis)
 
     tie = lax.optimization_barrier
-    chunks = [(0, 2 * size_a // 3), (2 * size_a // 3, size_a // 3)]
+    third = size_a // 3
+    sent = [(0, 2 * third), (2 * third, third)]
+    chunks = [(0, third + third // 2), (2 * third, third), (third + third // 2, third // 2)]
     own, half = packed(bra, ket, walker_group, group_occupied, core.reshape(1), walker_weight)
-    cols_q = [columns_q(*chunk) for chunk in chunks]
+    cols_q = [columns_q(*chunk) for chunk in sent]
     z1, z3, x0 = along(half, 1), along(half, 3), across(half)
     kernel_t = turned(kernel)
     x0, z1, z3, kernel_t = tie((x0, z1, z3, kernel_t))
     z2, x1, x3 = along(z1, 1), across(z1), across(z3)
-    z2, z1, z3 = tie((z2, z1, z3))
-    x2 = across(z2)
+    x1, z1, z3 = tie((x1, z1, z3))
+    x2 = along(x1, 1)
     near_four = [own] + [h for part in (x0, z1, z3) for h in (part, other(part))]
     lrp, stack, weight_rows = project(near_four, [width] + [occ] * 6, collocation, 2, 0)
+    x2, x3, weight_rows = tie((x2, x3, weight_rows))
     first = (lrp, stack, weight_rows)
-    x2, *first = tie((x2, *first))
     far_four = [h for part in (x1, x3, z2, x2) for h in (part, other(part))]
     lrp, stack, weight_rows = project(far_four, [occ] * 8, collocation, 2, 1, first)
     weights = jnp.concatenate([weight_rows[:4, 0], weight_rows[8:12, 0]])
@@ -263,22 +265,25 @@
         give, keep = split(grads, core, half_m)
         return split(keep + other(give).astype(F32), y, quarter)
 
-    (at_0, rows_0), (at_1, rows_1) = chunks
-    middle = stack.shape[0] // 2
-    grads = pair_gradients(weights, kernel_t, lrp, lrq, at_0, rows_0)
-    give, keep = over_cores(dot(grads, stack))
-    give, lrq = tie((give, lrq))
-    got = send(give, "pt", swap_y)
-    early = pair_gradients(weights, kernel_t, lrp, lrq, at_1, rows_1, (0, 4))
-    part = dot(early, stack[:middle])
-    part, got = tie((part, got))
-    pieces, came_0 = to_place((keep + got.astype(F32)).astype(BF16), lrq)
-    late = pair_gradients(weights, kernel_t, lrp, pieces[2], at_1, rows_1, (4, 8))
-    late, *came_0 = tie((late, *came_0))
-    give, keep = over_cores(part + dot(late, stack[middle:]))
-    _, came_1 = to_place((keep + send(give, "pt", swap_y).astype(F32)).astype(BF16))
-
-    ordered = [jnp.where(x == side, came[0], came[1]) for side in (0, 1) for came in (came_0, came_1)]
+    grads = pair_gradients(weights, kernel_t, lrp, lrq, *chunks[0])
+    give_0, keep_0 = over_cores(dot(grads, stack))
+    give_0, scale = tie((give_0, weights))
+    got_0 = send(give_0, "pt", swap_y)
+    grads = pair_gradients(scale, kernel_t, lrp, lrq, *chunks[1])
+    grads, got_0 = tie((grads, got_0))
+    part = dot(grads, stack)
+    pieces, came_0 = to_place((keep_0 + got_0.astype(F32)).astype(BF16), weights)
+    give_1, keep_1 = over_cores(part)
+    give_1, scale = tie((give_1, pieces[2]))
+    got_1 = send(give_1, "pt", swap_y)
+    grads = pair_gradients(scale, kernel_t, lrp, lrq, *chunks[2])
+    grads, got_1, *came_0 = tie((grads, got_1, *came_0))
+    pieces, came_1 = to_place((keep_1 + got_1.astype(F32)).astype(BF16), grads)
+    give_2, keep_2 = over_cores(dot(pieces[2], stack))
+    give_2, *came_1 = tie((give_2, *came_1))
+    _, came_2 = to_place((keep_2 + send(give_2, "pt", swap_y).astype(F32)).astype(BF16))
+
+    ordered = [jnp.where(x == side, came[0], came[1]) for side in (0, 1) for came in (came_0, came_2, came_1)]
     return jnp.concatenate(ordered, axis=0).astype(F32) / jnp.sum(weights)
 
 

time: 313 us -> 318 us (1.016)
  the two profiles are of different devices: /device:TPU:1 before, /device:TPU:5 now
where the time goes in v5:
time: 318 us; the launch traced here: 312 us
  Pallas kernels  153 us (48%)
  starting transfers between devices  47.8 us (15%)
  matrix products  40.8 us (13%)
  waiting for transfers between devices  40.2 us (13%)
  other arithmetic  15.7 us (5%)
  local copies, waits for them, and re-layouts  11.6 us (4%)
    pallas_call x3, Pallas kernels, pair_gradients(): pl.pallas_call(functools.partial(pair_kernel, sub, first), out_shape=jax....  99.5 us
    ppermute x30, starting transfers between devices, send(): return lax.ppermute(x, axes, pairs)  47.8 us
    dot_general x4, matrix products, dot(): return lax.dot_general(a, b, dims, preferred_element_type=F32)  40.8 us
    ppermute x30, waiting for transfers between devices, send(): return lax.ppermute(x, axes, pairs)  40.2 us
    pallas_call x2, Pallas kernels, project(): pl.pallas_call(functools.partial(project_kernel, tuple(rows_each), len(be...  35.8 us
    pallas_call x1, Pallas kernels, turned(): pl.pallas_call(turn_kernel, out_shape=jax.ShapeDtypeStruct((cols, rows),...  14.7 us
    dynamic_slice x2, local copies, waits for them, and re-layouts, columns_q(): rows = lax.dynamic_slice_in_dim(collocation, x * size_a + begin, chunk, 0)  6.37 us
  transfers between devices with their start and end apart: 30, of which 10 were waited for; matrix products, arithmetic and copies ran while one was open for 5% of the time, Pallas kernels for 33%

profile of v5, /device:TPU:5, one launch (start us, length us, event | category | flops | bytes accessed | tf_op | source)
XLA Modules:
  0.0 311.9 jit_solution(13543154913827228548)
XLA Ops:
  0.0 3.7 %constant_dynamic-slice_fusion.7 = bf16[1024,1536]{1,0:T(8,128)(2,1)} fusion(bf16[3072,1536]{1,0:T(8,128)(2,1)} %refs_8_.1, s32[]{:T(128)S(6)} %select_n.137), kind=kLoop, calls=%fused_computation.34 | loop fusion | bytes 6291460 | tf_op jit(solution)/shard_map/dynamic_slice | solution.py:216
  3.7 0.9 collective-permute-start.14
  5.9 2.6 shard_map.73
  8.5 1.2 collective-permute-start
  9.7 4.8 %collective-permute-start.1 = (bf16[176,1536]{1,0:T(8,128)(2,1)}, bf16[176,1536]{1,0:T(8,128)(2,1)}, u32[]{:S(2)}, u32[]{:S(2)}) collective-permute-start(bf16[176,1536]{1,0:T(8,128)(2,1)} %get-tuple-element.44), channel_id=1, source_target_pairs={{0,24},{4,28},{8,0},{12,4},{16,8},{20,12},{24,16},{28,20},{1,25},{... | collective-permute-start | bytes 1622024 | tf_op jit(solution)/shard_map/ppermute | solution.py:182
  14.5 14.7 %shard_map.74.kt_ref = bf16[1536,3072]{1,0:T(8,128)(2,1)} custom-call(bf16[3072,1536]{1,0:T(8,128)(2,1)} %in_ref.1), custom_call_target="tpu_custom_call" | custom-call | bytes 47185920 | tf_op jit(solution)/shard_map/pallas_call | solution.py:36
  29.2 9.3 %collective-permute-done.2.refs_5_ = bf16[176,1536]{1,0:T(8,128)(2,1)} collective-permute-done((bf16[176,1536]{1,0:T(8,128)(2,1)}, bf16[176,1536]{1,0:T(8,128)(2,1)}, u32[]{:S(2)}, u32[]{:S(2)}) %collective-permute-start.2) | collective-permute-done | bytes 540704 | tf_op jit(solution)/shard_map/ppermute | solution.py:182
  38.5 0.3 collective-permute-start.3
  38.7 2.7 constant_dynamic-slice_fusion.6
  41.4 1.8 collective-permute-start.16
  43.2 1.0 collective-permute-start.7
  44.2 1.2 collective-permute-start.6
  45.4 6.0 %collective-permute-done.3.refs_0_ = bf16[176,1536]{1,0:T(8,128)(2,1)} collective-permute-done((bf16[176,1536]{1,0:T(8,128)(2,1)}, bf16[176,1536]{1,0:T(8,128)(2,1)}, u32[]{:S(2)}, u32[]{:S(2)}) %collective-permute-start.3) | collective-permute-done | bytes 540704 | tf_op jit(solution)/shard_map/ppermute | solution.py:182
  51.4 3.7 %collective-permute-start.8 = (bf16[176,1536]{1,0:T(8,128)(2,1)}, bf16[176,1536]{1,0:T(8,128)(2,1)S(1)}, u32[]{:S(2)}, u32[]{:S(2)}) collective-permute-start(bf16[176,1536]{1,0:T(8,128)(2,1)} %collective-permute-done.1.refs_3_), channel_id=1, source_target_pairs={{0,1},{1,0},{2,3},{3,2},{4,5},{5,4},{6,7},{7,6},{8,9},{9,8},{10,11... | collective-permute-start | bytes 1622024 | tf_op jit(solution)/shard_map/ppermute | solution.py:182
  55.2 2.7 broadcast_select_fusion
  57.9 1.5 collective-permute-start.11
  59.4 0.1 collective-permute-start.5
  59.5 0.7 copy-done.5
  60.2 1.3 collective-permute-start.15
  61.5 17.9 %shard_map.75 = (bf16[2560,3072]{1,0:T(8,128)(2,1)}, bf16[2560,1536]{1,0:T(8,128)(2,1)}, f32[16,128]{1,0:T(8,128)}) custom-call(bf16[336,1536]{1,0:T(8,128)(2,1)} %get-tuple-element.48.refs_0_, bf16[176,1536]{1,0:T(8,128)(2,1)} %collective-permute-done.refs_1_, bf16[176,1536]{1,0:T(8,128)(2,1)} %copy-done.4, ...), custom_call_target="tpu_custom_call" | custom-call | flops 18119393280 | bytes 9437184 | tf_op jit(solution)/shard_map/pallas_call | solution.py:114
  79.4 1.4 collective-permute-start.4
  80.8 0.1 collective-permute-start.12
  80.9 2.3 collective-permute-done.5.refs_6_
  83.2 1.4 collective-permute-start.10
  84.6 2.3 broadcast_select_fusion.2
  86.8 1.5 collective-permute-start.17
  88.4 17.9 %shard_map.76 = (bf16[2560,3072]{1,0:T(8,128)(2,1)}, bf16[2560,1536]{1,0:T(8,128)(2,1)}, f32[16,128]{1,0:T(8,128)}) custom-call(bf16[176,1536]{1,0:T(8,128)(2,1)} %collective-permute-done.3.refs_0_, bf16[176,1536]{1,0:T(8,128)(2,1)} %collective-permute-done.4.refs_1_, ...), custom_call_target="tpu_custom_call", output_to_operand_aliasing={{0}: (9, {}), {1}: (10, {}), {2}: (11, {})} | custom-call | flops 18119393280 | bytes 9437184 | tf_op jit(solution)/shard_map/pallas_call | solution.py:114
  106.3 1.3 slice_reduce_fusion
  107.6 0.6 pad_maximum_fusion.weight_ref
  108.2 1.6 broadcast_select_fusion.3
  109.8 0.3 broadcast_select_fusion.1
  110.1 17.5 %convolution_convert_fusion.lrq_ref = bf16[1536,2560]{1,0:T(8,128)(2,1)} fusion(bf16[2560,1536]{1,0:T(8,128)(2,1)} %get-tuple-element.61, bf16[512,1536]{1,0:T(8,128)(2,1)S(1)} %broadcast_select_fusion.3, bf16[1024,1536]{1,0:T(8,128)(2,1)S(1)} %broadcast_select_fusion.1), kind=kOutput, calls=%fused_computation | convolution fusion | flops 12092964864 | bytes 20447232 | tf_op jit(solution)/shard_map/dot_general | solution.py:22
  127.6 48.2 %shard_map.77 = bf16[768,2560]{1,0:T(8,128)(2,1)} custom-call(f32[8]{0:T(128)} %pad_maximum_fusion.weight_ref, bf16[1536,3072]{1,0:T(8,128)(2,1)} %shard_map.74.kt_ref, bf16[2560,3072]{1,0:T(8,128)(2,1)} %get-tuple-element.60.lrp_ref, bf16[1536,2560]{1,0:T(8,128)(2,1)} %convolution_convert_fusion.lrq_ref), custom_call_target="tpu_custom_call" | custom-call | flops 38654705664 | bytes 34603008 | tf_op jit(solution)/shard_map/pallas_call | solution.py:161
  175.8 9.3 %fusion.4 = f32[768,1536]{0,1:T(8,128)S(1)} fusion(bf16[768,2560]{1,0:T(8,128)(2,1)} %shard_map.77, bf16[2560,1536]{1,0:T(8,128)(2,1)S(1)} %bitcast.17), kind=kOutput, calls=%fused_computation.41 | convolution fusion | flops 6039797760 | bytes 16515072 | tf_op jit(solution)/shard_map/dot_general | solution.py:22
  185.1 2.1 copy-done
  187.2 0.1 dynamic-slice_convert_fusion
  187.3 0.9 collective-permute-start.18
  188.2 2.5 collective-permute-done.18
  190.6 1.9 convert_add_fusion
  192.7 32.5 %shard_map.78 = bf16[512,2560]{1,0:T(8,128)(2,1)} custom-call(f32[8]{0:T(128)} %pad_maximum_fusion.weight_ref, bf16[1536,3072]{1,0:T(8,128)(2,1)} %shard_map.74.kt_ref, bf16[2560,3072]{1,0:T(8,128)(2,1)} %get-tuple-element.60.lrp_ref, bf16[1536,2560]{1,0:T(8,128)(2,1)} %convolution_convert_fusion.lrq_ref), custom_call_target="tpu_custom_call" | custom-call | flops 25769803776 | bytes 28311552 | tf_op jit(solution)/shard_map/pallas_call | solution.py:161
  225.2 7.7 %fusion.5 = f32[512,1536]{0,1:T(8,128)S(1)} fusion(bf16[512,2560]{1,0:T(8,128)(2,1)} %shard_map.78, bf16[2560,1536]{1,0:T(8,128)(2,1)} %get-tuple-element.61), kind=kOutput, calls=%fused_computation.42 | convolution fusion | flops 4026531840 | bytes 13631488 | tf_op jit(solution)/shard_map/dot_general | solution.py:22
  232.9 1.7 copy-done.1
  234.6 0.1 dynamic-slice_convert_fusion.1
  234.7 0.4 collective-permute-start.20
  235.1 1.3 add_convert_fusion
  236.5 6.7 %collective-permute-start.22 = (bf16[768,192]{0,1:T(8,128)(2,1)S(1)}, bf16[768,192]{0,1:T(8,128)(2,1)S(1)}, u32[]{:S(2)}, u32[]{:S(2)}) collective-permute-start(bf16[768,192]{0,1:T(8,128)(2,1)S(1)} %get-tuple-element.69), channel_id=1, source_target_pairs={{0,0},{1,16},{2,8},{3,24},{4,4},{5,20},{6,12},{7,28},{8,1},{9,17},... | collective-permute-start | bytes 884744 | tf_op jit(solution)/shard_map/ppermute | solution.py:182
  243.3 1.4 convert_add_fusion.1
  244.8 18.8 %shard_map.79 = bf16[256,2560]{1,0:T(8,128)(2,1)} custom-call(f32[8]{0:T(128)} %pad_maximum_fusion.weight_ref, bf16[1536,3072]{1,0:T(8,128)(2,1)} %shard_map.74.kt_ref, bf16[2560,3072]{1,0:T(8,128)(2,1)} %get-tuple-element.60.lrp_ref, bf16[1536,2560]{1,0:T(8,128)(2,1)} %convolution_convert_fusion.lrq_ref), custom_call_target="tpu_custom_call" | custom-call | flops 12884901888 | bytes 22020096 | tf_op jit(solution)/shard_map/pallas_call | solution.py:161
  263.7 0.9 collective-permute-done.21
  264.6 0.1 add_convert_fusion.1
  264.8 0.2 copy-done.6
  265.0 6.4 %fusion.6 = f32[256,1536]{0,1:T(8,128)S(1)} fusion(bf16[256,2560]{1,0:T(8,128)(2,1)S(1)} %copy-done.6, bf16[2560,1536]{1,0:T(8,128)(2,1)} %get-tuple-element.61), kind=kOutput, calls=%fused_computation.43 | convolution fusion | flops 2013265920 | bytes 10747904 | tf_op jit(solution)/shard_map/dot_general | solution.py:22
  271.4 0.2 collective-permute-start.24
  271.7 6.1 %collective-permute-start.25 = (bf16[512,192]{0,1:T(8,128)(2,1)S(1)}, bf16[512,192]{0,1:T(8,128)(2,1)S(1)}, u32[]{:S(2)}, u32[]{:S(2)}) collective-permute-start(bf16[512,192]{0,1:T(8,128)(2,1)S(1)} %get-tuple-element.76), channel_id=1, source_target_pairs={{0,0},{1,16},{2,8},{3,24},{4,4},{5,20},{6,12},{7,28},{8,1},{9,17},... | collective-permute-start | bytes 589832 | tf_op jit(solution)/shard_map/ppermute | solution.py:182
  277.8 1.0 collective-permute-start.26
  278.8 0.1 convert_add_fusion.2
  278.9 4.7 %collective-permute-done.25 = bf16[512,192]{0,1:T(8,128)(2,1)S(1)} collective-permute-done((bf16[512,192]{0,1:T(8,128)(2,1)S(1)}, bf16[512,192]{0,1:T(8,128)(2,1)S(1)}, u32[]{:S(2)}, u32[]{:S(2)}) %collective-permute-start.25) | collective-permute-done | bytes 196640 | tf_op jit(solution)/shard_map/ppermute | solution.py:182
  283.7 4.6 %collective-permute-done.26 = bf16[512,192]{0,1:T(8,128)(2,1)S(1)} collective-permute-done((bf16[512,192]{0,1:T(8,128)(2,1)S(1)}, bf16[512,192]{0,1:T(8,128)(2,1)S(1)}, u32[]{:S(2)}, u32[]{:S(2)}) %collective-permute-start.26) | collective-permute-done | bytes 196640 | tf_op jit(solution)/shard_map/ppermute | solution.py:182
  288.3 3.1 collective-permute-start.27
  292.6 2.4 collective-permute-done.27
  295.0 7.0 %collective-permute-start.28 = (bf16[256,192]{0,1:T(8,128)(2,1)S(1)}, bf16[256,192]{0,1:T(8,128)(2,1)S(1)}, u32[]{:S(2)}, u32[]{:S(2)}) collective-permute-start(bf16[256,192]{0,1:T(8,128)(2,1)S(1)} %get-tuple-element.79), channel_id=1, source_target_pairs={{0,0},{1,16},{2,8},{3,24},{4,4},{5,20},{6,12},{7,28},{8,1},{9,17},... | collective-permute-start | bytes 294920 | tf_op jit(solution)/shard_map/ppermute | solution.py:182
  302.2 2.4 collective-permute-done.28
  304.6 5.1 %collective-permute-done.29 = bf16[256,192]{0,1:T(8,128)(2,1)S(1)} collective-permute-done((bf16[256,192]{0,1:T(8,128)(2,1)S(1)}, bf16[256,192]{0,1:T(8,128)(2,1)S(1)}, u32[]{:S(2)}, u32[]{:S(2)}) %collective-permute-start.29) | collective-permute-done | bytes 98336 | tf_op jit(solution)/shard_map/ppermute | solution.py:182
  310.0 1.7 convert_divide_fusion
  (56 shorter events, 1.0 us)
Async XLA Ops:
  3.7 51.4 %collective-permute-start.14 = (bf16[1024,1536]{1,0:T(8,128)(2,1)}, bf16[1024,1536]{1,0:T(8,128)(2,1)S(1)}, u32[]{:S(2)}, u32[]{:S(2)}) collective-permute-start(bf16[1024,1536]{1,0:T(8,128)(2,1)} %constant_dynamic-slice_fusion.7), channel_id=1, source_target_pairs={{0,2},{4,6},{9,11},{13,15},{18,16},{22,20},{27,25},{31,29}} | collective-permute-start | bytes 9437192 | tf_op jit(solution)/shard_map/ppermute | solution.py:182
  8.5 20.7 %collective-permute-start = (bf16[176,1536]{1,0:T(8,128)(2,1)}, bf16[176,1536]{1,0:T(8,128)(2,1)}, u32[]{:S(2)}, u32[]{:S(2)}) collective-permute-start(bf16[176,1536]{1,0:T(8,128)(2,1)} %get-tuple-element.44), channel_id=1, source_target_pairs={{0,4},{4,0},{8,12},{12,8},{16,20},{20,16},{24,28},{28,24},{1,5},{5... | collective-permute-start | bytes 1622024 | tf_op jit(solution)/shard_map/ppermute | solution.py:182
  9.7 19.5 %collective-permute-start.1 = (bf16[176,1536]{1,0:T(8,128)(2,1)}, bf16[176,1536]{1,0:T(8,128)(2,1)}, u32[]{:S(2)}, u32[]{:S(2)}) collective-permute-start(bf16[176,1536]{1,0:T(8,128)(2,1)} %get-tuple-element.44), channel_id=1, source_target_pairs={{0,24},{4,28},{8,0},{12,4},{16,8},{20,12},{24,16},{28,20},{1,25},{... | collective-permute-start | bytes 1622024 | tf_op jit(solution)/shard_map/ppermute | solution.py:182
  14.5 24.0 %collective-permute-start.2 = (bf16[176,1536]{1,0:T(8,128)(2,1)}, bf16[176,1536]{1,0:T(8,128)(2,1)}, u32[]{:S(2)}, u32[]{:S(2)}) collective-permute-start(bf16[176,1536]{1,0:T(8,128)(2,1)} %get-tuple-element.44), channel_id=1, source_target_pairs={{0,8},{4,12},{8,16},{12,20},{16,24},{20,28},{24,0},{28,4},{1,9},{5... | collective-permute-start | bytes 1622024 | tf_op jit(solution)/shard_map/ppermute | solution.py:182
  38.5 12.9 %collective-permute-start.3 = (bf16[176,1536]{1,0:T(8,128)(2,1)}, bf16[176,1536]{1,0:T(8,128)(2,1)}, u32[]{:S(2)}, u32[]{:S(2)}) collective-permute-start(bf16[176,1536]{1,0:T(8,128)(2,1)} %collective-permute-done.1.refs_3_), channel_id=1, source_target_pairs={{0,4},{4,0},{8,12},{12,8},{16,20},{20,16},{24,28},{28,24},{1,5},{5... | collective-permute-start | bytes 1622024 | tf_op jit(solution)/shard_map/ppermute | solution.py:182
  41.4 43.2 %collective-permute-start.16 = (bf16[512,1536]{1,0:T(8,128)(2,1)}, bf16[512,1536]{1,0:T(8,128)(2,1)}, u32[]{:S(2)}, u32[]{:S(2)}) collective-permute-start(bf16[512,1536]{1,0:T(8,128)(2,1)} %constant_dynamic-slice_fusion.6), channel_id=1, source_target_pairs={{0,2},{4,6},{9,11},{13,15},{18,16},{22,20},{27,25},{31,29}} | collective-permute-start | bytes 4718600 | tf_op jit(solution)/shard_map/ppermute | solution.py:182
  43.2 14.7 %collective-permute-start.7 = (bf16[176,1536]{1,0:T(8,128)(2,1)}, bf16[176,1536]{1,0:T(8,128)(2,1)S(1)}, u32[]{:S(2)}, u32[]{:S(2)}) collective-permute-start(bf16[176,1536]{1,0:T(8,128)(2,1)} %collective-permute-done.refs_1_), channel_id=1, source_target_pairs={{0,1},{1,0},{2,3},{3,2},{4,5},{5,4},{6,7},{7,6},{8,9},{9,8},{10,11... | collective-permute-start | bytes 1622024 | tf_op jit(solution)/shard_map/ppermute | solution.py:182
  44.2 35.2 %collective-permute-start.6 = (bf16[176,1536]{1,0:T(8,128)(2,1)}, bf16[176,1536]{1,0:T(8,128)(2,1)}, u32[]{:S(2)}, u32[]{:S(2)}) collective-permute-start(bf16[176,1536]{1,0:T(8,128)(2,1)} %collective-permute-done.2.refs_5_), channel_id=1, source_target_pairs={{0,4},{4,0},{8,12},{12,8},{16,20},{20,16},{24,28},{28,24},{1,5},{5... | collective-permute-start | bytes 1622024 | tf_op jit(solution)/shard_map/ppermute | solution.py:182
  51.4 8.0 %collective-permute-start.8 = (bf16[176,1536]{1,0:T(8,128)(2,1)}, bf16[176,1536]{1,0:T(8,128)(2,1)S(1)}, u32[]{:S(2)}, u32[]{:S(2)}) collective-permute-start(bf16[176,1536]{1,0:T(8,128)(2,1)} %collective-permute-done.1.refs_3_), channel_id=1, source_target_pairs={{0,1},{1,0},{2,3},{3,2},{4,5},{5,4},{6,7},{7,6},{8,9},{9,8},{10,11... | collective-permute-start | bytes 1622024 | tf_op jit(solution)/shard_map/ppermute | solution.py:182
  55.1 5.1 %collective-permute-start.9 = (bf16[176,1536]{1,0:T(8,128)(2,1)}, bf16[176,1536]{1,0:T(8,128)(2,1)}, u32[]{:S(2)}, u32[]{:S(2)}) collective-permute-start(bf16[176,1536]{1,0:T(8,128)(2,1)} %collective-permute-done.2.refs_5_), channel_id=1, source_target_pairs={{0,1},{1,0},{2,3},{3,2},{4,5},{5,4},{6,7},{7,6},{8,9},{9,8},{10,11... | collective-permute-start | bytes 1622024 | tf_op jit(solution)/shard_map/ppermute | solution.py:182
  57.9 1.6 copy-start.4
  57.9 22.9 %collective-permute-start.11 = (bf16[176,1536]{1,0:T(8,128)(2,1)}, bf16[176,1536]{1,0:T(8,128)(2,1)}, u32[]{:S(2)}, u32[]{:S(2)}) collective-permute-start(bf16[176,1536]{1,0:T(8,128)(2,1)} %collective-permute-done.1.refs_3_), channel_id=1, source_target_pairs={{0,24},{4,28},{8,0},{12,4},{16,8},{20,12},{24,16},{28,20},{1,25},{... | collective-permute-start | bytes 1622024 | tf_op jit(solution)/shard_map/ppermute | solution.py:182
  59.4 0.8 copy-start.5
  59.4 23.8 %collective-permute-start.5 = (bf16[176,1536]{1,0:T(8,128)(2,1)}, bf16[176,1536]{1,0:T(8,128)(2,1)}, u32[]{:S(2)}, u32[]{:S(2)}) collective-permute-start(bf16[176,1536]{1,0:T(8,128)(2,1)} %collective-permute-done.3.refs_0_), channel_id=1, source_target_pairs={{0,24},{4,28},{8,0},{12,4},{16,8},{20,12},{24,16},{28,20},{1,25},{... | collective-permute-start | bytes 1622024 | tf_op jit(solution)/shard_map/ppermute | solution.py:182
  60.2 49.6 %collective-permute-start.15 = (bf16[1024,1536]{1,0:T(8,128)(2,1)S(1)}, bf16[1024,1536]{1,0:T(8,128)(2,1)S(1)}, u32[]{:S(2)}, u32[]{:S(2)}) collective-permute-start(bf16[1024,1536]{1,0:T(8,128)(2,1)S(1)} %broadcast_select_fusion), channel_id=1, source_target_pairs={{0,1},{2,3},{4,5},{6,7},{9,8},{11,10},{13,12},{15,14},{18,19},{16,... | collective-permute-start | bytes 9437192 | tf_op jit(solution)/shard_map/ppermute | solution.py:182
  79.4 7.4 %collective-permute-start.4 = (bf16[176,1536]{1,0:T(8,128)(2,1)}, bf16[176,1536]{1,0:T(8,128)(2,1)}, u32[]{:S(2)}, u32[]{:S(2)}) collective-permute-start(bf16[176,1536]{1,0:T(8,128)(2,1)} %collective-permute-done.3.refs_0_), channel_id=1, source_target_pairs={{0,1},{1,0},{2,3},{3,2},{4,5},{5,4},{6,7},{7,6},{8,9},{9,8},{10,11... | collective-permute-start | bytes 1622024 | tf_op jit(solution)/shard_map/ppermute | solution.py:182
  80.8 7.5 %collective-permute-start.12 = (bf16[176,1536]{1,0:T(8,128)(2,1)}, bf16[176,1536]{1,0:T(8,128)(2,1)}, u32[]{:S(2)}, u32[]{:S(2)}) collective-permute-start(bf16[176,1536]{1,0:T(8,128)(2,1)} %collective-permute-done.11.refs_4_), channel_id=1, source_target_pairs={{0,1},{1,0},{2,3},{3,2},{4,5},{5,4},{6,7},{7,6},{8,9},{9,8},{10,11... | collective-permute-start | bytes 1622024 | tf_op jit(solution)/shard_map/ppermute | solution.py:182
  83.2 5.2 %collective-permute-start.10 = (bf16[176,1536]{1,0:T(8,128)(2,1)}, bf16[176,1536]{1,0:T(8,128)(2,1)}, u32[]{:S(2)}, u32[]{:S(2)}) collective-permute-start(bf16[176,1536]{1,0:T(8,128)(2,1)} %collective-permute-done.6.refs_2_), channel_id=1, source_target_pairs={{0,1},{1,0},{2,3},{3,2},{4,5},{5,4},{6,7},{7,6},{8,9},{9,8},{10,11... | collective-permute-start | bytes 1622024 | tf_op jit(solution)/shard_map/ppermute | solution.py:182
  84.6 3.8 %collective-permute-start.13 = (bf16[176,1536]{1,0:T(8,128)(2,1)}, bf16[176,1536]{1,0:T(8,128)(2,1)}, u32[]{:S(2)}, u32[]{:S(2)}) collective-permute-start(bf16[176,1536]{1,0:T(8,128)(2,1)} %collective-permute-done.5.refs_6_), channel_id=1, source_target_pairs={{0,1},{1,0},{2,3},{3,2},{4,5},{5,4},{6,7},{7,6},{8,9},{9,8},{10,11... | collective-permute-start | bytes 1622024 | tf_op jit(solution)/shard_map/ppermute | solution.py:182
  86.8 21.4 %collective-permute-start.17 = (bf16[512,1536]{1,0:T(8,128)(2,1)S(1)}, bf16[512,1536]{1,0:T(8,128)(2,1)}, u32[]{:S(2)}, u32[]{:S(2)}) collective-permute-start(bf16[512,1536]{1,0:T(8,128)(2,1)S(1)} %broadcast_select_fusion.2), channel_id=1, source_target_pairs={{0,1},{2,3},{4,5},{6,7},{9,8},{11,10},{13,12},{15,14},{18,19},{16,... | collective-permute-start | bytes 4718600 | tf_op jit(solution)/shard_map/ppermute | solution.py:182
  110.1 65.7 %slice-start = ((s8[7864320]{0:T(1024)(128)(4,1)}), s8[4194304]{0:T(1024)(128)(4,1)S(1)}, s32[]{:S(2)}) async-start(s8[7864320]{0:T(1024)(128)(4,1)} %bitcast.16), calls=%async_computation | async-start | bytes 8388608
  127.6 48.2 %slice-start.1 = ((s8[7864320]{0:T(1024)(128)(4,1)}), s8[3670016]{0:T(1024)(128)(4,1)S(1)}, s32[]{:S(2)}) async-start(s8[7864320]{0:T(1024)(128)(4,1)} %bitcast.16), calls=%async_computation.1 | async-start | bytes 7340032
  185.1 2.1 copy-start
  187.3 3.4 %collective-permute-start.18 = (bf16[768,768]{0,1:T(8,128)(2,1)S(1)}, bf16[768,768]{0,1:T(8,128)(2,1)S(1)}, u32[]{:S(2)}, u32[]{:S(2)}) collective-permute-start(bf16[768,768]{0,1:T(8,128)(2,1)S(1)} %dynamic-slice_convert_fusion), channel_id=1, source_target_pairs={{0,1},{1,0},{2,3},{3,2},{4,5},{5,4},{6,7},{7,6},{8,9},{9,8},{10,11... | collective-permute-start | bytes 3538952 | tf_op jit(solution)/shard_map/ppermute | solution.py:182
  192.6 32.6 %collective-permute-start.19 = (bf16[768,384]{0,1:T(8,128)(2,1)S(1)}, bf16[768,384]{0,1:T(8,128)(2,1)S(1)}, u32[]{:S(2)}, u32[]{:S(2)}) collective-permute-start(bf16[768,384]{0,1:T(8,128)(2,1)S(1)} %dynamic-slice_convert_fusion.2), channel_id=1, source_target_pairs={{0,2},{1,3},{2,0},{3,1},{4,6},{5,7},{6,4},{7,5},{8,10},{9,11},{10,... | collective-permute-start | bytes 1769480 | tf_op jit(solution)/shard_map/ppermute | solution.py:182
  225.2 7.7 %copy-start.3 = (bf16[768,384]{0,1:T(8,128)(2,1)}, bf16[768,384]{0,1:T(8,128)(2,1)S(1)}, u32[]{:S(2)}) copy-start(bf16[768,384]{0,1:T(8,128)(2,1)S(1)} %collective-permute-done.19) | copy-start | bytes 1769476
  232.9 1.7 copy-start.1
  234.7 8.6 %collective-permute-start.20 = (bf16[512,768]{0,1:T(8,128)(2,1)S(1)}, bf16[512,768]{0,1:T(8,128)(2,1)}, u32[]{:S(2)}, u32[]{:S(2)}) collective-permute-start(bf16[512,768]{0,1:T(8,128)(2,1)S(1)} %dynamic-slice_convert_fusion.1), channel_id=1, source_target_pairs={{0,1},{1,0},{2,3},{3,2},{4,5},{5,4},{6,7},{7,6},{8,9},{9,8},{10,11... | collective-permute-start | bytes 2359304 | tf_op jit(solution)/shard_map/ppermute | solution.py:182
  235.1 8.2 %copy-start.2 = (f32[512,1536]{0,1:T(8,128)S(1)}, f32[512,1536]{0,1:T(8,128)}, u32[]{:S(2)}) copy-start(f32[512,1536]{0,1:T(8,128)} %copy-done.1) | copy-start | bytes 9437188
  236.5 27.2 %collective-permute-start.22 = (bf16[768,192]{0,1:T(8,128)(2,1)S(1)}, bf16[768,192]{0,1:T(8,128)(2,1)S(1)}, u32[]{:S(2)}, u32[]{:S(2)}) collective-permute-start(bf16[768,192]{0,1:T(8,128)(2,1)S(1)} %get-tuple-element.69), channel_id=1, source_target_pairs={{0,0},{1,16},{2,8},{3,24},{4,4},{5,20},{6,12},{7,28},{8,1},{9,17},... | collective-permute-start | bytes 884744 | tf_op jit(solution)/shard_map/ppermute | solution.py:182
  243.2 20.5 %collective-permute-start.23 = (bf16[768,192]{0,1:T(8,128)(2,1)S(1)}, bf16[768,192]{0,1:T(8,128)(2,1)S(1)}, u32[]{:S(2)}, u32[]{:S(2)}) collective-permute-start(bf16[768,192]{0,1:T(8,128)(2,1)S(1)} %get-tuple-element.70), channel_id=1, source_target_pairs={{0,4},{1,20},{2,12},{3,28},{4,0},{5,16},{6,8},{7,24},{8,5},{9,21},... | collective-permute-start | bytes 884744 | tf_op jit(solution)/shard_map/ppermute | solution.py:182
  244.8 19.8 %collective-permute-start.21 = (bf16[512,384]{0,1:T(8,128)(2,1)S(1)}, bf16[512,384]{0,1:T(8,128)(2,1)S(1)}, u32[]{:S(2)}, u32[]{:S(2)}) collective-permute-start(bf16[512,384]{0,1:T(8,128)(2,1)S(1)} %dynamic-slice_convert_fusion.4), channel_id=1, source_target_pairs={{0,2},{1,3},{2,0},{3,1},{4,6},{5,7},{6,4},{7,5},{8,10},{9,11},{10,... | collective-permute-start | bytes 1179656 | tf_op jit(solution)/shard_map/ppermute | solution.py:182
  263.7 1.3 copy-start.6
  271.4 7.4 %collective-permute-start.24 = (bf16[256,768]{0,1:T(8,128)(2,1)S(1)}, bf16[256,768]{0,1:T(8,128)(2,1)S(1)}, u32[]{:S(2)}, u32[]{:S(2)}) collective-permute-start(bf16[256,768]{0,1:T(8,128)(2,1)S(1)} %dynamic-slice_convert_fusion.3), channel_id=1, source_target_pairs={{0,1},{1,0},{2,3},{3,2},{4,5},{5,4},{6,7},{7,6},{8,9},{9,8},{10,11... | collective-permute-start | bytes 1179656 | tf_op jit(solution)/shard_map/ppermute | solution.py:182
  271.7 12.0 %collective-permute-start.25 = (bf16[512,192]{0,1:T(8,128)(2,1)S(1)}, bf16[512,192]{0,1:T(8,128)(2,1)S(1)}, u32[]{:S(2)}, u32[]{:S(2)}) collective-permute-start(bf16[512,192]{0,1:T(8,128)(2,1)S(1)} %get-tuple-element.76), channel_id=1, source_target_pairs={{0,0},{1,16},{2,8},{3,24},{4,4},{5,20},{6,12},{7,28},{8,1},{9,17},... | collective-permute-start | bytes 589832 | tf_op jit(solution)/shard_map/ppermute | solution.py:182
  277.8 10.5 %collective-permute-start.26 = (bf16[512,192]{0,1:T(8,128)(2,1)S(1)}, bf16[512,192]{0,1:T(8,128)(2,1)S(1)}, u32[]{:S(2)}, u32[]{:S(2)}) collective-permute-start(bf16[512,192]{0,1:T(8,128)(2,1)S(1)} %get-tuple-element.77), channel_id=1, source_target_pairs={{0,4},{1,20},{2,12},{3,28},{4,0},{5,16},{6,8},{7,24},{8,5},{9,21},... | collective-permute-start | bytes 589832 | tf_op jit(solution)/shard_map/ppermute | solution.py:182
  288.3 6.6 %collective-permute-start.27 = (bf16[256,384]{0,1:T(8,128)(2,1)S(1)}, bf16[256,384]{0,1:T(8,128)(2,1)S(1)}, u32[]{:S(2)}, u32[]{:S(2)}) collective-permute-start(bf16[256,384]{0,1:T(8,128)(2,1)S(1)} %dynamic-slice_convert_fusion.5), channel_id=1, source_target_pairs={{0,2},{1,3},{2,0},{3,1},{4,6},{5,7},{6,4},{7,5},{8,10},{9,11},{10,... | collective-permute-start | bytes 589832 | tf_op jit(solution)/shard_map/ppermute | solution.py:182
  295.0 9.6 %collective-permute-start.28 = (bf16[256,192]{0,1:T(8,128)(2,1)S(1)}, bf16[256,192]{0,1:T(8,128)(2,1)S(1)}, u32[]{:S(2)}, u32[]{:S(2)}) collective-permute-start(bf16[256,192]{0,1:T(8,128)(2,1)S(1)} %get-tuple-element.79), channel_id=1, source_target_pairs={{0,0},{1,16},{2,8},{3,24},{4,4},{5,20},{6,12},{7,28},{8,1},{9,17},... | collective-permute-start | bytes 294920 | tf_op jit(solution)/shard_map/ppermute | solution.py:182
  302.0 7.7 %collective-permute-start.29 = (bf16[256,192]{0,1:T(8,128)(2,1)S(1)}, bf16[256,192]{0,1:T(8,128)(2,1)S(1)}, u32[]{:S(2)}, u32[]{:S(2)}) collective-permute-start(bf16[256,192]{0,1:T(8,128)(2,1)S(1)} %get-tuple-element.80), channel_id=1, source_target_pairs={{0,4},{1,20},{2,12},{3,28},{4,0},{5,16},{6,8},{7,24},{8,5},{9,21},... | collective-permute-start | bytes 294920 | tf_op jit(solution)/shard_map/ppermute | solution.py:182
